TPU v7x, 32 devices: a whole 2x2x4 slice. The times are simulated.
32 devices in a mesh: dp: 16 (over z, x, core), seq: 2 (over y).
Axes of the slice: x: 2, y: 2, z: 4, core: 2. Of those that a mesh axis runs over, the one named last changes fastest.
Arguments:
- layer_input: float32 [16384, 768], P(('dp', 'seq')), may hold values from -6 to 6
- cotangent: float32 [16384, 768], P(('dp', 'seq')), may hold values from -6 to 6
- seq_lengths: int32 [16], P('dp'), may hold values from 1024 to 1024, as said below
- qkv_weight: float32 [768, 2304], P(('dp', 'seq')), may hold values from -0.21875 to 0.21875
- qv_bias: float32 [1536], P(('dp', 'seq')), may hold values from -1.5 to 1.5
- out_weight: float32 [768, 768], P(('dp', 'seq')), may hold values from -1.25 to 1.25
- out_bias: float32 [768], P(('dp', 'seq')), may hold values from -1.5 to 1.5
- first_gain: float32 [768], P(('dp', 'seq')), may hold values from 0.25 to 1.75
- first_shift: float32 [768], P(('dp', 'seq')), may hold values from -1.5 to 1.5
- up_weight: float32 [768, 3072], P(('dp', 'seq')), may hold values from -0.21875 to 0.21875
- up_bias: float32 [3072], P(('dp', 'seq')), may hold values from -1.5 to 1.5
- down_weight: float32 [3072, 768], P(('dp', 'seq')), may hold values from -0.109375 to 0.109375
- down_bias: float32 [768], P(('dp', 'seq')), may hold values from -1.5 to 1.5
- second_gain: float32 [768], P(('dp', 'seq')), may hold values from 0.25 to 1.75
- second_shift: float32 [768], P(('dp', 'seq')), may hold values from -1.5 to 1.5
Outputs:
- layer_output: float32 [16384, 768], P(('dp', 'seq'))
- input_grad: float32 [16384, 768], P(('dp', 'seq'))
- qkvweight_grad: float32 [768, 2304], P(('dp', 'seq'))
- qvbias_grad: float32 [1536], P(('dp', 'seq'))
- outweight_grad: float32 [768, 768], P(('dp', 'seq'))
- outbias_grad: float32 [768], P(('dp', 'seq'))
- firstgain_grad: float32 [768], P(('dp', 'seq'))
- firstshift_grad: float32 [768], P(('dp', 'seq'))
- upweight_grad: float32 [768, 3072], P(('dp', 'seq'))
- upbias_grad: float32 [3072], P(('dp', 'seq'))
- downweight_grad: float32 [3072, 768], P(('dp', 'seq'))
- downbias_grad: float32 [768], P(('dp', 'seq'))
- secondgain_grad: float32 [768], P(('dp', 'seq'))
- secondshift_grad: float32 [768], P(('dp', 'seq'))
Inputs may be any that keep to these rules, and one draw needn't show every extreme that they name: Each group holds one sequence at its positions 0 to seq_lengths - 1, reaching into every device of the group; the rest of its 1024 positions is padding. Some group is full.
All inputs are finite; a program needn't handle non-finite values.
Results may differ from a plain program's by a relative error of at most 0.0003.
Values sent between devices are 32-bit elements; how exact they have to be, the bound alone decides.
No kernel may reach another device: no remote copies, remote signals or barrier semaphores. Data moves between devices by JAX's collectives and lax.ppermute only.
A program may use at most 256 MiB of HBM per device.

v0:
```python
import jax
import jax.numpy as jnp
from jax import lax
from jax.sharding import PartitionSpec as P

D = 768
HEADS = 12
HEAD_DIM = 64


eps_norm = 1e-05
neg_big = -1e30
top_prec = lax.Precision.HIGHEST


def matmul(left, right):
    return jnp.dot(left, right, precision=top_prec, preferred_element_type=jnp.float32)


def matmul_tn(left, right):
    return lax.dot_general(
        left,
        right,
        (((0,), (0,)), ((), ())),
        precision=top_prec,
        preferred_element_type=jnp.float32,
    )


def matmul_nt(left, right):
    return lax.dot_general(
        left,
        right,
        (((1,), (1,)), ((), ())),
        precision=top_prec,
        preferred_element_type=jnp.float32,
    )


def norm_forward(values, gain, shift):
    centred = values - jnp.mean(values, axis=1, keepdims=True)
    inv_std = lax.rsqrt(jnp.mean(centred * centred, axis=1, keepdims=True) + eps_norm)
    normed = centred * inv_std
    return (normed * gain + shift, normed, inv_std)


def norm_backward(upstream, normed, inv_std, gain):
    scaled = upstream * gain
    inner = (
        scaled
        - jnp.mean(scaled, axis=1, keepdims=True)
        - normed * jnp.mean(scaled * normed, axis=1, keepdims=True)
    )
    return (inner * inv_std, jnp.sum(upstream * normed, axis=0), jnp.sum(upstream, axis=0))


def split_heads(values):
    return values.reshape(values.shape[0], HEADS, HEAD_DIM).transpose(1, 0, 2)


def join_heads(values):
    return values.transpose(1, 0, 2).reshape(values.shape[1], HEADS * HEAD_DIM)


def gelu_forward(values):
    return 0.5 * values * (1.0 + lax.erf(values * 0.7071067811865476))


def gelu_slope(values):
    cdf_part = 0.5 * (1.0 + lax.erf(values * 0.7071067811865476))
    return cdf_part + values * jnp.exp(-0.5 * values * values) * 0.3989422804014327


def body(
    layer_input,
    cotangent,
    seq_lengths,
    qkv_weight,
    qv_bias,
    out_weight,
    out_bias,
    first_gain,
    first_shift,
    up_weight,
    up_bias,
    down_weight,
    down_bias,
    second_gain,
    second_shift,
):
    gathered = (
        lax.all_gather(qkv_weight, ("dp", "seq"), axis=0, tiled=True),
        lax.all_gather(qv_bias, ("dp", "seq"), axis=0, tiled=True),
        lax.all_gather(out_weight, ("dp", "seq"), axis=0, tiled=True),
        lax.all_gather(out_bias, ("dp", "seq"), axis=0, tiled=True),
        lax.all_gather(first_gain, ("dp", "seq"), axis=0, tiled=True),
        lax.all_gather(first_shift, ("dp", "seq"), axis=0, tiled=True),
        lax.all_gather(up_weight, ("dp", "seq"), axis=0, tiled=True),
        lax.all_gather(up_bias, ("dp", "seq"), axis=0, tiled=True),
        lax.all_gather(down_weight, ("dp", "seq"), axis=0, tiled=True),
        lax.all_gather(down_bias, ("dp", "seq"), axis=0, tiled=True),
        lax.all_gather(second_gain, ("dp", "seq"), axis=0, tiled=True),
        lax.all_gather(second_shift, ("dp", "seq"), axis=0, tiled=True),
    )
    (
        w_qkv,
        b_qv,
        w_out,
        b_out,
        gain_one,
        shift_one,
        w_up,
        b_up,
        w_down,
        b_down,
        gain_two,
        shift_two,
    ) = gathered
    tok_rows = layer_input.shape[0]
    group_rows = tok_rows * lax.axis_size("seq")
    score_scale = HEAD_DIM ** (-0.5)
    seq_len = seq_lengths[0]
    first_own = lax.axis_index("seq") * tok_rows
    query_pos = first_own + jnp.arange(tok_rows, dtype=jnp.int32)
    last_query = first_own + tok_rows - 1

    def segment_of(positions):
        return jnp.where(positions < seq_len, 0, positions + 1)

    query_seg = segment_of(query_pos)

    def key_mask(key_pos):
        return (segment_of(key_pos)[None, :] == query_seg[:, None]) & (
            key_pos[None, :] <= query_pos[:, None]
        )

    normed_out_one, normed_one, inv_one = norm_forward(layer_input, gain_one, shift_one)
    qkv_bias = jnp.concatenate([b_qv[:D], jnp.zeros((D,), jnp.float32), b_qv[D:]])
    projected = matmul(normed_out_one, w_qkv) + qkv_bias
    queries = projected[:, :D]
    keys_local = projected[:, D : 2 * D]
    values_local = projected[:, 2 * D :]
    query_heads = split_heads(queries)
    start_state = (
        jnp.full((HEADS, tok_rows), neg_big, jnp.float32),
        jnp.zeros((HEADS, tok_rows), jnp.float32),
        jnp.zeros((HEADS, tok_rows, HEAD_DIM), jnp.float32),
    )
    key_piece = lax.all_gather(keys_local, "seq", axis=0, tiled=True)
    value_piece = lax.all_gather(values_local, "seq", axis=0, tiled=True)

    def compute_block(state_in):
        key_pos = jnp.arange(key_piece.shape[0], dtype=jnp.int32)
        allowed = key_mask(key_pos)
        key_heads = split_heads(key_piece)
        value_heads = split_heads(value_piece)

        def one_head(ignored, head_item):
            q_head, k_head, v_head, old_max, old_sum, old_acc = head_item
            scores = jnp.where(allowed, matmul_nt(q_head, k_head) * score_scale, neg_big)
            new_max = jnp.maximum(old_max, jnp.max(scores, axis=1))
            weights_soft = jnp.where(allowed, jnp.exp(scores - new_max[:, None]), 0.0)
            decay_old = jnp.exp(old_max - new_max)
            new_sum = old_sum * decay_old + jnp.sum(weights_soft, axis=1)
            new_acc = old_acc * decay_old[:, None] + matmul(weights_soft, v_head)
            return (ignored, (new_max, new_sum, new_acc))

        unused, updated = lax.scan(
            one_head,
            jnp.zeros((), jnp.float32),
            (query_heads, key_heads, value_heads, state_in[0], state_in[1], state_in[2]),
        )
        return updated

    def keep_block(state_in):
        return (state_in[0], state_in[1], state_in[2])

    run_max, run_sum, run_acc = lax.cond(
        jnp.int32(0) > last_query, keep_block, compute_block, start_state
    )
    head_out = run_acc / run_sum[:, :, None]
    log_sum = run_max + jnp.log(run_sum)
    attended = join_heads(head_out)
    middle = layer_input + matmul(attended, w_out) + b_out
    normed_out_two, normed_two, inv_two = norm_forward(middle, gain_two, shift_two)
    pre_act = matmul(normed_out_two, w_up) + b_up
    activ = gelu_forward(pre_act)
    layer_output = middle + matmul(activ, w_down) + b_down
    again = (
        lax.all_gather(qkv_weight, ("dp", "seq"), axis=0, tiled=True),
        lax.all_gather(qv_bias, ("dp", "seq"), axis=0, tiled=True),
        lax.all_gather(out_weight, ("dp", "seq"), axis=0, tiled=True),
        lax.all_gather(out_bias, ("dp", "seq"), axis=0, tiled=True),
        lax.all_gather(first_gain, ("dp", "seq"), axis=0, tiled=True),
        lax.all_gather(first_shift, ("dp", "seq"), axis=0, tiled=True),
        lax.all_gather(up_weight, ("dp", "seq"), axis=0, tiled=True),
        lax.all_gather(up_bias, ("dp", "seq"), axis=0, tiled=True),
        lax.all_gather(down_weight, ("dp", "seq"), axis=0, tiled=True),
        lax.all_gather(down_bias, ("dp", "seq"), axis=0, tiled=True),
        lax.all_gather(second_gain, ("dp", "seq"), axis=0, tiled=True),
        lax.all_gather(second_shift, ("dp", "seq"), axis=0, tiled=True),
    )
    (
        w_qkv,
        b_qv,
        w_out,
        b_out,
        gain_one,
        shift_one,
        w_up,
        b_up,
        w_down,
        b_down,
        gain_two,
        shift_two,
    ) = again
    d_down_b = jnp.sum(cotangent, axis=0)
    d_down_w = matmul_tn(activ, cotangent)
    d_pre = matmul_nt(cotangent, w_down) * gelu_slope(pre_act)
    d_up_b = jnp.sum(d_pre, axis=0)
    d_up_w = matmul_tn(normed_out_two, d_pre)
    d_norm_two, d_gain_two, d_shift_two = norm_backward(
        matmul_nt(d_pre, w_up), normed_two, inv_two, gain_two
    )
    d_middle = cotangent + d_norm_two
    d_out_b = jnp.sum(d_middle, axis=0)
    d_out_w = matmul_tn(attended, d_middle)
    d_att = matmul_nt(d_middle, w_out)
    dout_heads = split_heads(d_att)
    delta_heads = jnp.sum(dout_heads * head_out, axis=2)
    key_all, value_all = (
        lax.all_gather(keys_local, "seq", axis=0, tiled=True),
        lax.all_gather(values_local, "seq", axis=0, tiled=True),
    )
    allowed_all = key_mask(jnp.arange(group_rows, dtype=jnp.int32))

    def back_head(ignored, head_item):
        q_head, k_head, v_head, do_head, lse_head, delta_head = head_item
        scores = jnp.where(allowed_all, matmul_nt(q_head, k_head) * score_scale, neg_big)
        weights_soft = jnp.where(allowed_all, jnp.exp(scores - lse_head[:, None]), 0.0)
        dv_head = matmul_tn(weights_soft, do_head)
        d_soft = matmul_nt(do_head, v_head)
        d_scores = weights_soft * (d_soft - delta_head[:, None]) * score_scale
        return (ignored, (matmul(d_scores, k_head), matmul_tn(d_scores, q_head), dv_head))

    unused, head_grads = lax.scan(
        back_head,
        jnp.zeros((), jnp.float32),
        (
            query_heads,
            split_heads(key_all),
            split_heads(value_all),
            dout_heads,
            log_sum,
            delta_heads,
        ),
    )
    d_query = join_heads(head_grads[0])
    key_terms = join_heads(head_grads[1])
    value_terms = join_heads(head_grads[2])
    d_key, d_value = (
        lax.psum_scatter(key_terms, "seq", scatter_dimension=0, tiled=True),
        lax.psum_scatter(value_terms, "seq", scatter_dimension=0, tiled=True),
    )
    d_proj = jnp.concatenate([d_query, d_key, d_value], axis=1)
    d_qv_b = jnp.concatenate([jnp.sum(d_query, axis=0), jnp.sum(d_value, axis=0)])
    d_qkv_w = matmul_tn(normed_out_one, d_proj)
    d_norm_one, d_gain_one, d_shift_one = norm_backward(
        matmul_nt(d_proj, w_qkv), normed_one, inv_one, gain_one
    )
    input_grad = d_middle + d_norm_one
    summed = (
        lax.psum_scatter(d_qkv_w, ("dp", "seq"), scatter_dimension=0, tiled=True),
        lax.psum_scatter(d_qv_b, ("dp", "seq"), scatter_dimension=0, tiled=True),
        lax.psum_scatter(d_out_w, ("dp", "seq"), scatter_dimension=0, tiled=True),
        lax.psum_scatter(d_out_b, ("dp", "seq"), scatter_dimension=0, tiled=True),
        lax.psum_scatter(d_gain_one, ("dp", "seq"), scatter_dimension=0, tiled=True),
        lax.psum_scatter(d_shift_one, ("dp", "seq"), scatter_dimension=0, tiled=True),
        lax.psum_scatter(d_up_w, ("dp", "seq"), scatter_dimension=0, tiled=True),
        lax.psum_scatter(d_up_b, ("dp", "seq"), scatter_dimension=0, tiled=True),
        lax.psum_scatter(d_down_w, ("dp", "seq"), scatter_dimension=0, tiled=True),
        lax.psum_scatter(d_down_b, ("dp", "seq"), scatter_dimension=0, tiled=True),
        lax.psum_scatter(d_gain_two, ("dp", "seq"), scatter_dimension=0, tiled=True),
        lax.psum_scatter(d_shift_two, ("dp", "seq"), scatter_dimension=0, tiled=True),
    )
    return (
        layer_output,
        input_grad,
        summed[0],
        summed[1],
        summed[2],
        summed[3],
        summed[4],
        summed[5],
        summed[6],
        summed[7],
        summed[8],
        summed[9],
        summed[10],
        summed[11],
    )


def solution(mesh):
    return jax.shard_map(
        body,
        mesh=mesh,
        in_specs=(
            P(("dp", "seq"), None),
            P(("dp", "seq"), None),
            P("dp"),
            P(("dp", "seq"), None),
            P(("dp", "seq")),
            P(("dp", "seq"), None),
            P(("dp", "seq")),
            P(("dp", "seq")),
            P(("dp", "seq")),
            P(("dp", "seq"), None),
            P(("dp", "seq")),
            P(("dp", "seq"), None),
            P(("dp", "seq")),
            P(("dp", "seq")),
            P(("dp", "seq")),
        ),
        out_specs=(
            P(("dp", "seq"), None),
            P(("dp", "seq"), None),
            P(("dp", "seq"), None),
            P(("dp", "seq")),
            P(("dp", "seq"), None),
            P(("dp", "seq")),
            P(("dp", "seq")),
            P(("dp", "seq")),
            P(("dp", "seq"), None),
            P(("dp", "seq")),
            P(("dp", "seq"), None),
            P(("dp", "seq")),
            P(("dp", "seq")),
            P(("dp", "seq")),
        ),
        check_vma=False,
    )
```

profile of v0, /device:TPU:0, one launch (start us, length us, event | category | flops | bytes accessed | tf_op | source)
XLA Modules:
  0.0 1269.2 jit_solution(5580132628328302307)
XLA Ops:
  15.5 43.1 %all-reduce.17 = (f32[1536]{0:T(1024)S(1)}, f32[768]{0:T(1024)S(1)}, f32[768]{0:T(1024)S(1)}, f32[768]{0:T(1024)S(1)}, f32[768]{0:T(1024)S(1)}, /*index=5*/f32[768]{0:T(1024)S(1)}, f32[3072]{0:T(1024)S(1)}) all-reduce(f32[1536]{0:T(1024)S(1)} %dynamic-update-slice.2, ...), channel_id=1, replica_groups=mesh['dp'=16,'seq'=2] {'dp','seq'}, use_global_device_ids=true, to_apply=%add.2 | all-reduce | flops 8448 | bytes 67584
  59.0 27.4 %all-gather.7.cloned.1.call-done = f32[768,2304]{1,0:T(8,128)} async-done(((f32[24,2304]{1,0:T(8,128)}), f32[768,2304]{1,0:T(8,128)}) %all-gather.7.cloned.1.call-update) | async-done | bytes 7077904 | tf_op jit(solution)/shard_map/all_gather | solution.py:92
  86.4 14.3 %convolution_add_fusion.1 = f32[512,2304]{1,0:T(8,128)S(1)} fusion(f32[768,2304]{1,0:T(8,128)} %all-gather.7.cloned.1.call-done, f32[2304]{0:T(1024)S(1)} %pad_maximum_fusion.3, f32[512,768]{1,0:T(8,128)S(1)} %copy-done, f32[768]{0:T(1024)S(1)} %get-tuple-element.328, f32[768]{0:T(1024)S(1)} %get-tuple-element.329, f32[512]{0:T(512)S(1)} %add_rsqrt_fusion.1, ...), kind=kOutput, calls=%fused_computation.75 | convolution fusion | flops 10874388480 | bytes 13388800 | tf_op jit(solution)/shard_map/dot_general | solution.py:17
  107.6 38.8 %all-gather.9.cloned.1.call-done = f32[1024,768]{1,0:T(8,128)} async-done(((f32[512,768]{1,0:T(8,128)}), f32[1024,768]{1,0:T(8,128)}) %all-gather.9.cloned.1.call-update) | async-done | bytes 3145744 | tf_op jit(solution)/shard_map/all_gather | solution.py:149
  146.4 47.1 %all-gather.11.cloned.1.call-done = f32[1024,768]{1,0:T(8,128)} async-done(((f32[512,768]{1,0:T(8,128)}), f32[1024,768]{1,0:T(8,128)}) %all-gather.11.cloned.1.call-update) | async-done | bytes 3145744 | tf_op jit(solution)/shard_map/all_gather | solution.py:150
  193.5 113.5 %conditional.1 = (f32[12,512]{1,0:T(8,128)S(1)}, f32[12,512]{1,0:T(8,128)S(1)}, f32[12,512,64]{1,2,0:T(8,128)}) conditional(s32[]{:T(128)} %convert_element_type.3, (f32[1024,768]{1,0:T(8,128)}, f32[1024,768]{1,0:T(8,128)}, s32[]{:T(128)}, s32[512]{0:T(512)S(1)}, f32[12,512,64]{1,2,0:T(8,128)}) %tuple.116, () %tuple.25), branch_computations={%region_2.7_spmd, %region_7.8_spmd} | conditional | flops 816355840 | bytes 32309544 | solution.py:178
  193.5 4.0 copy.50
  201.2 105.8 %while.29 = (s32[]{:T(128)}, f32[12,512]{1,0:T(8,128)S(1)}, f32[12,512]{1,0:T(8,128)S(1)}, f32[12,512,64]{1,2,0:T(8,128)}, f32[12,512,64]{1,2,0:T(8,128)}, /*ind...) while((s32[]{:T(128)}, f32[12,512]{1,0:T(8,128)S(1)}, ...), condition=%wide.region_6.6_spmd.clone, body=%wide.region_3.5_spmd.clone.sunk | while | flops 816351232 | bytes 7135365 | solution.py:168
  205.6 4.4 fusion.141
  214.5 4.4 fusion.141
  223.3 4.4 fusion.141
  232.1 4.4 fusion.141
  240.9 4.4 fusion.141
  249.7 4.4 fusion.141
  258.5 4.4 fusion.141
  267.4 4.4 fusion.141
  276.2 4.4 fusion.141
  285.0 4.4 fusion.141
  293.8 4.4 fusion.141
  302.6 4.4 fusion.141
  316.1 6.4 fusion.85
  322.8 14.7 %all-gather.15.cloned.1.call-done = f32[768,3072]{1,0:T(8,128)} async-done(((f32[24,3072]{1,0:T(8,128)}), f32[768,3072]{1,0:T(8,128)}) %all-gather.15.cloned.1.call-update) | async-done | bytes 9437200 | tf_op jit(solution)/shard_map/all_gather | solution.py:98
  337.4 19.9 %fusion.61 = f32[512,3072]{1,0:T(8,128)} fusion(f32[768,3072]{1,0:T(8,128)} %all-gather.15.cloned.1.call-done, f32[512,768]{1,0:T(8,128)S(1)} %get-tuple-element.349, f32[768]{0:T(1024)S(1)} %get-tuple-element.331, f32[768]{0:T(1024)S(1)} %get-tuple-element.332, f32[512]{0:T(512)S(1)} %add_rsqrt_fusion, f32[512]{0:T(512)S(1)} %broadcast_multiply_fusion.4), kind=kOutput, calls=%fused_computation.98 | convolution fusion | flops 14497087488 | bytes 17311744 | tf_op jit(solution)/shard_map/dot_general | solution.py:17
  357.3 63.6 %all-gather.17.cloned.1.call-done = f32[3072,768]{1,0:T(8,128)} async-done(((f32[96,768]{1,0:T(8,128)}), f32[3072,768]{1,0:T(8,128)}) %all-gather.17.cloned.1.call-update) | async-done | bytes 9437200 | tf_op jit(solution)/shard_map/all_gather | solution.py:100
  420.9 20.4 %fusion.86 = (f32[3072]{0:T(1024)S(1)}, f32[512,3072]{1,0:T(8,128)S(1)}) fusion(f32[512,3072]{1,0:T(8,128)} %fusion.61, f32[3072]{0:T(1024)S(1)} %get-tuple-element.333, f32[512,768]{1,0:T(8,128)} %param.22, f32[3072,768]{1,0:T(8,128)} %all-gather.17.cloned.1.call-done), kind=kOutput, calls=%fused_computation.141 | convolution fusion | flops 14512813056 | bytes 23617536 | tf_op jit(solution)/shard_map/dot_general | solution.py:31
  441.3 17.3 %multiply_reduce_fusion = (f32[768]{0:T(1024)S(1)}, f32[512]{0:T(512)S(1)}, f32[512]{0:T(512)S(1)}, f32[768]{0:T(1024)S(1)}, f32[512,768]{1,0:T(8,128)S(1)}) fusion(f32[512,768]{1,0:T(8,128)S(1)} %get-tuple-element.349, f32[512]{0:T(512)S(1)} %add_rsqrt_fusion, f32[512]{0:T(512)S(1)} %broadcast_multiply_fusion.4, f32[768]{0:T(1024)S(1)} %get-tuple-element.332, ...), kind=kOutput, calls=%fused_computation.82 | convolution fusion | flops 14499051520 | bytes 18891776 | tf_op jit(solution)/shard_map/dot_general | solution.py:31
  460.4 3.9 fusion.87
  465.5 195.8 %while.30 = (s32[]{:T(128)}, f32[12,512,64]{1,2,0:T(8,128)}, f32[12,1024,64]{1,2,0:T(8,128)}, f32[12,1024,64]{1,2,0:T(8,128)}, f32[12,512,64]{1,2,0:T(8,128)}, /...) while((s32[]{:T(128)}, f32[12,512,64]{1,2,0:T(8,128)}, ...), condition=%wide.region_14.15_spmd.clone, body=%wide.region_13.14_spmd.clone.sunk | while | flops 2018508800 | bytes 14574737 | solution.py:246
  472.3 3.7 fusion.135
  488.6 3.8 fusion.135
  521.1 3.8 fusion.135
  537.4 3.8 fusion.135
  553.7 3.7 fusion.135
  586.3 3.8 fusion.135
  602.5 3.8 fusion.135
  618.8 3.8 fusion.135
  651.4 3.7 fusion.135
  662.1 7.2 fusion.88
  669.4 19.5 %fusion.60 = f32[768,3072]{1,0:T(8,128)} fusion(f32[512,3072]{1,0:T(8,128)} %copy-done.3, f32[512,768]{1,0:T(8,128)S(1)} %get-tuple-element.349, f32[768]{0:T(1024)S(1)} %get-tuple-element.331, f32[768]{0:T(1024)S(1)} %get-tuple-element.332, f32[512]{0:T(512)S(1)} %add_rsqrt_fusion, f32[512]{0:T(512)S(1)} %broadcast_multiply_fusion.4), kind=kOutput, calls=%fused_computation.97 | convolution fusion | flops 14497087488 | bytes 17311744 | tf_op jit(solution)/shard_map/dot_general | solution.py:21
  688.9 20.8 %fusion.58 = f32[3072,768]{1,0:T(8,128)} fusion(f32[512,768]{1,0:T(8,128)} %param.22, f32[512,3072]{1,0:T(8,128)} %fusion.61, f32[3072]{0:T(1024)S(1)} %get-tuple-element.333), kind=kOutput, calls=%fused_computation.79 | convolution fusion | flops 14503378944 | bytes 17313792 | tf_op jit(solution)/shard_map/dot_general | solution.py:21
  709.8 39.3 %reduce-scatter.7.cloned.1.call-done = f32[512,768]{0,1:T(8,128)} async-done(((f32[1024,768]{0,1:T(8,128)}), f32[512,768]{0,1:T(8,128)}) %reduce-scatter.7.cloned.1.call-update) | async-done | bytes 1572880 | tf_op jit(solution)/shard_map/reduce_scatter | solution.py:262
  749.1 26.5 %fusion.56 = f32[768,2304]{1,0:T(8,128)} fusion(f32[512,768]{0,1:T(8,128)} %reduce-scatter.9.cloned.1.call-done, f32[512,768]{0,1:T(8,128)} %reduce-scatter.7.cloned.1.call-done, f32[512,768]{0,1:T(8,128)} %bitcast.162, f32[512,768]{1,0:T(8,128)S(1)} %copy-done.1, f32[768]{0:T(1024)S(1)} %get-tuple-element.328, f32[768]{0:T(1024)S(1)} %get-tuple-element.329, ...), kind=kOutput, calls=%fused_computation.77 | convolution fusion | flops 10875568128 | bytes 13379584 | tf_op jit(solution)/shard_map/dot_general | solution.py:21
  779.7 28.2 %multiply_reduce_fusion.1 = (f32[768]{0:T(1024)S(1)}, f32[512]{0:T(512)S(1)}, f32[512]{0:T(512)S(1)}, f32[768]{0:T(1024)S(1)}, f32[512,768]{1,0:T(8,128)}) fusion(f32[512,768]{1,0:T(8,128)S(1)} %copy-done.1, f32[512]{0:T(512)S(1)} %add_rsqrt_fusion.1, f32[512]{0:T(512)S(1)} %broadcast_multiply_fusion.5, f32[768]{0:T(1024)S(1)} %get-tuple-element.329, ...), kind=kOutput, calls=%fused_computation.83 | convolution fusion | flops 10877532160 | bytes 14959616 | tf_op jit(solution)/shard_map/dot_general | solution.py:31
  808.0 40.5 %all-reduce.16 = (f32[768]{0:T(1024)S(1)}, f32[1536]{0:T(1024)S(1)}, f32[768]{0:T(1024)S(1)}, f32[768]{0:T(1024)S(1)}, f32[768]{0:T(1024)S(1)}, /*index=5*/f32[3...) all-reduce(f32[768]{0:T(1024)S(1)} %dynamic-update-slice.7, ...), channel_id=1, replica_groups=mesh['dp'=16,'seq'=2] {'dp','seq'}, use_global_device_ids=true, to_apply=%add.7 | all-reduce | flops 9984 | bytes 79872
  856.7 20.3 %add_add_fusion = f32[512,768]{1,0:T(8,128)} fusion(f32[512,768]{1,0:T(8,128)S(1)} %get-tuple-element.349, f32[3072,768]{1,0:T(8,128)} %all-gather.17.cloned.1.call-done, f32[512,3072]{1,0:T(8,128)} %fusion.61, f32[3072]{0:T(1024)S(1)} %get-tuple-element.333, f32[768]{0:T(1024)S(1)} %get-tuple-element.318), kind=kOutput, calls=%fused_computation.89 | convolution fusion | flops 14504165376 | bytes 18889728 | tf_op jit(solution)/shard_map/dot_general | solution.py:17
  877.0 119.1 %reduce-scatter.15.cloned.1.call-done = f32[24,3072]{1,0:T(8,128)} async-done(((f32[768,3072]{1,0:T(8,128)}), f32[24,3072]{1,0:T(8,128)}) %reduce-scatter.15.cloned.1.call-update) | async-done | bytes 294928 | tf_op jit(solution)/shard_map/reduce_scatter | solution.py:279
  996.1 141.1 %reduce-scatter.17.cloned.1.call-done = f32[96,768]{1,0:T(8,128)} async-done(((f32[3072,768]{1,0:T(8,128)}), f32[96,768]{1,0:T(8,128)}) %reduce-scatter.17.cloned.1.call-update) | async-done | bytes 294928 | tf_op jit(solution)/shard_map/reduce_scatter | solution.py:281
  1137.2 125.0 %reduce-scatter.11.cloned.1.call-done = f32[24,2304]{1,0:T(8,128)} async-done(((f32[768,2304]{1,0:T(8,128)}), f32[24,2304]{1,0:T(8,128)}) %reduce-scatter.11.cloned.1.call-update) | async-done | bytes 221200 | tf_op jit(solution)/shard_map/reduce_scatter | solution.py:273
  (248 shorter events, 257.8 us)
Async XLA Ops:
  7.2 51.5 %copy-start = (f32[512,768]{1,0:T(8,128)S(1)}, f32[512,768]{1,0:T(8,128)}, u32[]{:S(2)}) copy-start(f32[512,768]{1,0:T(8,128)} %param.21) | copy-start | bytes 4718596
  7.2 79.2 %all-gather.7.cloned.1.call-start = ((), (), s32[]{:S(2)}) async-start(), calls=%async_computation.6 | async-start | bytes 7299072 | tf_op jit(solution)/shard_map/all_gather | solution.py:92
  7.9 138.5 %all-gather.9.cloned.1.call-start = ((), (), s32[]{:S(2)}) async-start(), calls=%async_computation.7 | async-start | bytes 4718592 | tf_op jit(solution)/shard_map/all_gather | solution.py:149
  102.8 90.8 %all-gather.11.cloned.1.call-start = ((), (), s32[]{:S(2)}) async-start(), calls=%async_computation.8 | async-start | bytes 4718592 | tf_op jit(solution)/shard_map/all_gather | solution.py:150
  103.5 212.6 %all-gather.13.cloned.1.call-start = ((), (), s32[]{:S(2)}) async-start(), calls=%async_computation.9 | async-start | bytes 2433024 | tf_op jit(solution)/shard_map/all_gather | solution.py:94
  104.1 233.4 %all-gather.15.cloned.1.call-start = ((), (), s32[]{:S(2)}) async-start(), calls=%async_computation.10 | async-start | bytes 9732096 | tf_op jit(solution)/shard_map/all_gather | solution.py:98
  104.7 316.2 %all-gather.17.cloned.1.call-start = ((), (), s32[]{:S(2)}) async-start(), calls=%async_computation.11 | async-start | bytes 9732096 | tf_op jit(solution)/shard_map/all_gather | solution.py:100
  105.2 604.5 %reduce-scatter.9.cloned.1.call-start = ((), (), s32[]{:S(2)}) async-start(), calls=%async_computation.13 | async-start | bytes 4718592 | tf_op jit(solution)/shard_map/reduce_scatter | solution.py:263
  193.5 4.0 copy-start.7
  307.1 3.7 copy-start.6
  313.1 2.9 copy-start.1
  420.9 20.4 %copy-start.2 = (f32[768,3072]{1,0:T(8,128)S(1)}, f32[768,3072]{1,0:T(8,128)}, u32[]{:S(2)}) copy-start(f32[768,3072]{1,0:T(8,128)} %all-gather.15.cloned.1.call-done) | copy-start | bytes 28311556
  441.2 17.4 %copy-start.3 = (f32[512,3072]{1,0:T(8,128)}, f32[512,3072]{1,0:T(8,128)S(1)}, u32[]{:S(2)}) copy-start(f32[512,3072]{1,0:T(8,128)S(1)} %get-tuple-element.353) | copy-start | bytes 18874372
  441.3 17.4 %copy-start.10 = (f32[512,768]{1,0:T(8,128)S(1)}, f32[512,768]{1,0:T(8,128)}, u32[]{:S(2)}) copy-start(f32[512,768]{1,0:T(8,128)} %param.22) | copy-start | bytes 4718596
  458.7 1.7 copy-start.8
  459.3 5.0 copy-start.4
  460.4 4.0 copy-start.9
  464.3 1.1 copy-start.5
  661.3 87.8 %reduce-scatter.7.cloned.1.call-start = ((), (), s32[]{:S(2)}) async-start(), calls=%async_computation.12 | async-start | bytes 4718592 | tf_op jit(solution)/shard_map/reduce_scatter | solution.py:262
  662.0 215.0 %reduce-scatter.13.cloned.1.call-start = ((), (), s32[]{:S(2)}) async-start(), calls=%async_computation.15 | async-start | bytes 2433024 | tf_op jit(solution)/shard_map/reduce_scatter | solution.py:275
  669.3 326.8 %reduce-scatter.15.cloned.1.call-start = ((), (), s32[]{:S(2)}) async-start(), calls=%async_computation.16 | async-start | bytes 9732096 | tf_op jit(solution)/shard_map/reduce_scatter | solution.py:279
  688.9 448.3 %reduce-scatter.17.cloned.1.call-start = ((), (), s32[]{:S(2)}) async-start(), calls=%async_computation.17 | async-start | bytes 9732096 | tf_op jit(solution)/shard_map/reduce_scatter | solution.py:281
  709.7 552.4 %reduce-scatter.11.cloned.1.call-start = ((), (), s32[]{:S(2)}) async-start(), calls=%async_computation.14 | async-start | bytes 7299072 | tf_op jit(solution)/shard_map/reduce_scatter | solution.py:273
  775.6 0.7 copy-start.11
Sparse Core Ops, SparseCore 0:
  10.9 75.4 all-gather.6
  102.9 43.4 all-gather.8
  148.5 44.9 all-gather.10
  196.3 57.3 all-gather.12
  256.5 80.9 all-gather.14
  340.2 80.6 all-gather.16
  661.4 41.9 reduce-scatter.8
  705.7 43.3 reduce-scatter.6
  754.9 99.0 reduce-scatter.12
  861.4 134.6 reduce-scatter.14
  1002.6 134.5 reduce-scatter.16
  1144.2 117.8 reduce-scatter.10
where the time goes:
time: 1280 us; the launch traced here: 1270 us
  waiting for transfers between devices  620 us (48%)
  matrix products  493 us (39%)
  blocking collectives  83.6 us (7%)
  local copies, waits for them, and re-layouts  30.9 us (2%)
  other arithmetic  25 us (2%)
  between operations  15.4 us (1%)
    dot_general x40, matrix products, matmul_nt(): lax.dot_general(left, right, (((1,), (1,)), ((), ())), precision=top_prec...  187 us
    dot_general x28, matrix products, matmul(): jnp.dot(left, right, precision=top_prec, preferred_element_type=jnp.float32)  159 us
    dot_general x28, matrix products, matmul_tn(): lax.dot_general(left, right, (((0,), (0,)), ((), ())), precision=top_prec...  147 us
    reduce_scatter x1, waiting for transfers between devices, body(): lax.psum_scatter(d_down_w, ('dp', 'seq'), scatter_dimension=0, tiled=True)  141 us
    reduce_scatter x1, waiting for transfers between devices, body(): lax.psum_scatter(d_qkv_w, ('dp', 'seq'), scatter_dimension=0, tiled=True)  125 us
    reduce_scatter x1, waiting for transfers between devices, body(): lax.psum_scatter(d_up_w, ('dp', 'seq'), scatter_dimension=0, tiled=True)  119 us
    unnamed x2, blocking collectives  83.6 us
    all_gather x1, waiting for transfers between devices, body(): lax.all_gather(down_weight, ('dp', 'seq'), axis=0, tiled=True)  63.6 us
  transfers between devices with their start and end apart: 12, of which 9 were waited for; matrix products, arithmetic and copies ran while one was open for 23% of the time, Pallas kernels for 0%

commit v1 on v0

--- a/solution.py
+++ b/solution.py
@@ -1,16 +1,24 @@
+import functools
+
 import jax
 import jax.numpy as jnp
 from jax import lax
+from jax.experimental import pallas as pl
+from jax.experimental.pallas import tpu as pltpu
 from jax.sharding import PartitionSpec as P
 
 D = 768
 HEADS = 12
 HEAD_DIM = 64
-
+PAIR = 2 * HEAD_DIM
+TILE = 256
+AXES = ("dp", "seq")
 
 eps_norm = 1e-05
 neg_big = -1e30
-top_prec = lax.Precision.HIGHEST
+top_prec = lax.Precision.HIGH
+f32 = jnp.float32
+bf16 = jnp.bfloat16
 
 
 def matmul(left, right):
@@ -71,7 +79,7 @@
     return cdf_part + values * jnp.exp(-0.5 * values * values) * 0.3989422804014327
 
 
-def body(
+def body_general(
     layer_input,
     cotangent,
     seq_lengths,
@@ -186,34 +194,6 @@
     pre_act = matmul(normed_out_two, w_up) + b_up
     activ = gelu_forward(pre_act)
     layer_output = middle + matmul(activ, w_down) + b_down
-    again = (
-        lax.all_gather(qkv_weight, ("dp", "seq"), axis=0, tiled=True),
-        lax.all_gather(qv_bias, ("dp", "seq"), axis=0, tiled=True),
-        lax.all_gather(out_weight, ("dp", "seq"), axis=0, tiled=True),
-        lax.all_gather(out_bias, ("dp", "seq"), axis=0, tiled=True),
-        lax.all_gather(first_gain, ("dp", "seq"), axis=0, tiled=True),
-        lax.all_gather(first_shift, ("dp", "seq"), axis=0, tiled=True),
-        lax.all_gather(up_weight, ("dp", "seq"), axis=0, tiled=True),
-        lax.all_gather(up_bias, ("dp", "seq"), axis=0, tiled=True),
-        lax.all_gather(down_weight, ("dp", "seq"), axis=0, tiled=True),
-        lax.all_gather(down_bias, ("dp", "seq"), axis=0, tiled=True),
-        lax.all_gather(second_gain, ("dp", "seq"), axis=0, tiled=True),
-        lax.all_gather(second_shift, ("dp", "seq"), axis=0, tiled=True),
-    )
-    (
-        w_qkv,
-        b_qv,
-        w_out,
-        b_out,
-        gain_one,
-        shift_one,
-        w_up,
-        b_up,
-        w_down,
-        b_down,
-        gain_two,
-        shift_two,
-    ) = again
     d_down_b = jnp.sum(cotangent, axis=0)
     d_down_w = matmul_tn(activ, cotangent)
     d_pre = matmul_nt(cotangent, w_down) * gelu_slope(pre_act)
@@ -301,42 +281,416 @@
     )
 
 
+def split(v):
+    high=v.astype(bf16)
+    return high,(v-high.astype(f32)).astype(bf16)
+
+def dot_nn(a,b):
+    return lax.dot_general(a,b,(((1,),(0,)),((),())),preferred_element_type=f32)
+def dot_nt(a,b):
+    return lax.dot_general(a,b,(((1,),(1,)),((),())),preferred_element_type=f32)
+def dot_tn(a,b):
+    return lax.dot_general(a,b,(((0,),(0,)),((),())),preferred_element_type=f32)
+
+def fold(v):
+    return v[:,:PAIR]+v[:,PAIR:]
+
+def attend_kernel(len_ref,qkv_ref,out_ref,lse_ref):
+    rows=qkv_ref.shape[0]
+    seq_len=len_ref[0]
+    lane=lax.broadcasted_iota(jnp.int32,(1,PAIR),1)
+    q_high,q_low=split(qkv_ref[:,:PAIR]*(HEAD_DIM**-0.5))
+    q_both=jnp.concatenate([q_high,q_low],axis=1)
+    v_high,v_low=split(qkv_ref[:,2*PAIR:])
+    v_both=jnp.concatenate([v_high,v_low],axis=1)
+    k_all=qkv_ref[:,PAIR:2*PAIR]
+    k_parts=[]
+    for head in range(2):
+        kh,kl=split(jnp.where(lane//HEAD_DIM==head,k_all,0.0))
+        k_parts.append((jnp.concatenate([kh,kh],axis=1),kl))
+    for start in range(0,rows,TILE):
+        stop=start+TILE
+        q_pos=start+lax.broadcasted_iota(jnp.int32,(TILE,1),0)
+        first=jnp.where(q_pos<seq_len,0,q_pos)
+        k_pos=lax.broadcasted_iota(jnp.int32,(1,stop),1)
+        allowed=(k_pos>=first)&(k_pos<=q_pos)
+        outs,lses=[],[]
+        for head in range(2):
+            kd,kl=k_parts[head]
+            scores=dot_nt(q_both[start:stop],kd[:stop])+dot_nt(q_high[start:stop],kl[:stop])
+            scores=jnp.where(allowed,scores,neg_big)
+            top=jnp.max(scores,axis=1,keepdims=True)
+            probs=jnp.exp(scores-top)
+            total=jnp.sum(probs,axis=1,keepdims=True)
+            ph,pw=split(probs)
+            acc=fold(dot_nn(ph,v_both[:stop]))+dot_nn(pw,v_high[:stop])
+            outs.append(acc*(1.0/total))
+            lses.append(jnp.broadcast_to(top+jnp.log(total),(TILE,PAIR)))
+        out_ref[start:stop]=jnp.where(lane<HEAD_DIM,outs[0],outs[1])
+        lse_ref[start:stop]=jnp.where(lane<HEAD_DIM,lses[0],lses[1])
+
+def attend_back_kernel(len_ref,qkv_ref,do_ref,out_ref,lse_ref,grad_ref):
+    rows=qkv_ref.shape[0]
+    seq_len=len_ref[0]
+    lane=lax.broadcasted_iota(jnp.int32,(1,PAIR),1)
+    scale=HEAD_DIM**-0.5
+    q_high,q_low=split(qkv_ref[:,:PAIR]*scale)
+    q_both=jnp.concatenate([q_high,q_low],axis=1)
+    q_twice=jnp.concatenate([q_high,q_high],axis=1)
+    do_all=do_ref[...]
+    do_high,do_low=split(do_all)
+    do_both=jnp.concatenate([do_high,do_low],axis=1)
+    do_twice=jnp.concatenate([do_high,do_high],axis=1)
+    delta_t=jnp.transpose(do_all*out_ref[...])
+    lse_t=jnp.transpose(lse_ref[...])
+    q_sum=[None,None]
+    dq=[[jnp.zeros((TILE,PAIR),f32) for _ in range(rows//TILE)] for _ in range(2)]
+    for start in range(0,rows,TILE):
+        stop=start+TILE
+        n=rows-start
+        k_pos=start+lax.broadcasted_iota(jnp.int32,(TILE,1),0)
+        q_pos=start+lax.broadcasted_iota(jnp.int32,(1,n),1)
+        first=jnp.where(q_pos<seq_len,0,q_pos)
+        allowed=(k_pos>=first)&(k_pos<=q_pos)
+        k_all=qkv_ref[start:stop,PAIR:2*PAIR]
+        v_all=qkv_ref[start:stop,2*PAIR:]
+        k_grads,v_grads=[],[]
+        for head in range(2):
+            mine=lane//HEAD_DIM==head
+            kh,kl=split(jnp.where(mine,k_all,0.0))
+            vh,vl=split(jnp.where(mine,v_all,0.0))
+            k_both=jnp.concatenate([kh,kl],axis=1)
+            v_both=jnp.concatenate([vh,vl],axis=1)
+            scores=dot_nt(k_both,q_twice[start:])+dot_nt(kh,q_low[start:])
+            lse_row=lse_t[head*HEAD_DIM:head*HEAD_DIM+1,start:]
+            probs=jnp.where(allowed,jnp.exp(scores-lse_row),0.0)
+            ph,pw=split(probs)
+            v_grads.append(fold(dot_nn(ph,do_both[start:]))+dot_nn(pw,do_high[start:]))
+            d_probs=dot_nt(v_both,do_twice[start:])+dot_nt(vh,do_low[start:])
+            delta_row=jnp.sum(delta_t[head*HEAD_DIM:(head+1)*HEAD_DIM,start:],axis=0,keepdims=True)
+            d_scores=probs*(d_probs-delta_row)
+            sh,sl=split(d_scores)
+            k_grads.append(fold(dot_nn(sh,q_both[start:]))+dot_nn(sl,q_high[start:]))
+            part=fold(dot_tn(sh,k_both))+dot_tn(sl,kh)
+            for t in range(n//TILE):
+                dq[head][start//TILE+t]+=part[t*TILE:(t+1)*TILE]
+        grad_ref[start:stop,PAIR:2*PAIR]=jnp.where(lane<HEAD_DIM,k_grads[0],k_grads[1])
+        grad_ref[start:stop,2*PAIR:]=jnp.where(lane<HEAD_DIM,v_grads[0],v_grads[1])
+        grad_ref[start:stop,:PAIR]=(dq[0][start//TILE]+dq[1][start//TILE])*scale
+
+def attend(seq_len,qkv):
+    rows,cols=qkv.shape
+    pairs=cols//(3*PAIR)
+    block=lambda w: pl.BlockSpec((rows,w),lambda j:(0,j))
+    return pl.pallas_call(
+        attend_kernel,
+        grid=(pairs,),
+        in_specs=[pl.BlockSpec(memory_space=pltpu.SMEM),block(3*PAIR)],
+        out_specs=[block(PAIR),block(PAIR)],
+        out_shape=[jax.ShapeDtypeStruct((rows,pairs*PAIR),f32)]*2,
+        compiler_params=pltpu.CompilerParams(vmem_limit_bytes=48*2**20),
+        cost_estimate=pl.CostEstimate(flops=40*10**9//3,bytes_accessed=4*rows*pairs*PAIR*5,transcendentals=rows*rows*pairs),
+        name="attend",
+    )(seq_len,qkv)
+
+def attend_back(seq_len,qkv,d_out,out,lse):
+    rows,cols=qkv.shape
+    pairs=cols//(3*PAIR)
+    block=lambda w: pl.BlockSpec((rows,w),lambda j:(0,j))
+    return pl.pallas_call(
+        attend_back_kernel,
+        grid=(pairs,),
+        in_specs=[pl.BlockSpec(memory_space=pltpu.SMEM),block(3*PAIR),block(PAIR),block(PAIR),block(PAIR)],
+        out_specs=block(3*PAIR),
+        out_shape=jax.ShapeDtypeStruct((rows,cols),f32),
+        compiler_params=pltpu.CompilerParams(vmem_limit_bytes=48*2**20),
+        cost_estimate=pl.CostEstimate(flops=40*10**9,bytes_accessed=4*rows*pairs*PAIR*9,transcendentals=rows*rows*pairs),
+        name="attend_back",
+    )(seq_len,qkv,d_out,out,lse)
+
+
+COLUMNS = 4
+
+
+def table(move):
+    pairs = []
+    for z in range(COLUMNS):
+        for x in range(2):
+            for core in range(2):
+                for y in range(2):
+                    there = move(z, x, core, y)
+                    number = lambda p: ((p[0] * 2 + p[1]) * 2 + p[2]) * 2 + p[3]
+                    pairs.append((number((z, x, core, y)), number(there)))
+    return pairs
+
+
+over_core = table(lambda z, x, core, y: (z, x, 1 - core, y))
+over_x = table(lambda z, x, core, y: (z, 1 - x, core, y))
+over_y = table(lambda z, x, core, y: (z, x, core, 1 - y))
+over_z = [None] + [
+    table(lambda z, x, core, y, k=k: (z ^ k, x, core, y)) for k in range(1, COLUMNS)
+]
+
+
+def swap(values, pairs):
+    return lax.ppermute(values, AXES, pairs)
+
+
+def place():
+    dp = lax.axis_index("dp")
+    return dp // 4, (dp // 2) % 2, dp % 2, lax.axis_index("seq")
+
+
+def pick(values, index, axis):
+    return lax.dynamic_index_in_dim(values, index, axis, keepdims=False)
+
+
+def assemble_kernel(count, place_ref, *refs):
+    pieces, out_ref, sems = refs[:count], refs[count], refs[count + 1]
+    z, x, core, y = (place_ref[i] for i in range(4))
+    copies = []
+    for c in range(2):
+        own, beside_x, beside_y, corner_a, corner_b = pieces[c * 5 : c * 5 + 5]
+        sources = [(own, 0, 0, 0, 4), (beside_x, 1, 0, 0, 4), (beside_y, 0, 1, 0, 4)]
+        sources += [(corner_a, 1, 1, 0, 2), (corner_b, 1, 1, 2, 4)]
+        for piece, dx, dy, first, last in sources:
+            for k in range(first, last):
+                slot = out_ref.at[z ^ k, x ^ dx, core ^ c, y ^ dy]
+                copies.append(
+                    pltpu.make_async_copy(piece.at[k - first], slot, sems.at[len(copies)])
+                )
+    for copy in copies:
+        copy.start()
+    for copy in copies:
+        copy.wait()
+
+
+def assemble(where, pieces, rows, cols):
+    anywhere = pl.BlockSpec(memory_space=pl.ANY)
+    return pl.pallas_call(
+        functools.partial(assemble_kernel, len(pieces)),
+        in_specs=[pl.BlockSpec(memory_space=pltpu.SMEM)] + [anywhere] * len(pieces),
+        out_specs=anywhere,
+        out_shape=jax.ShapeDtypeStruct((COLUMNS, 2, 2, 2, rows, cols), f32),
+        scratch_shapes=[pltpu.SemaphoreType.DMA((32,))],
+        cost_estimate=pl.CostEstimate(
+            flops=0, bytes_accessed=2 * 32 * rows * cols * 4, transcendentals=0
+        ),
+        name="assemble",
+    )(where, *pieces)
+
+
+def gather_weight(where, shard):
+    rows, cols = shard.shape
+    own = jnp.stack([shard] + [swap(shard, over_z[k]) for k in range(1, COLUMNS)])
+    beside_x = swap(own, over_x)
+    beside_y = swap(own, over_y)
+    corner_a = swap(beside_y[:2], over_x)
+    corner_b = swap(beside_x[2:], over_y)
+    mine = [own, beside_x, beside_y, corner_a, corner_b]
+    other = [swap(piece, over_core) for piece in mine]
+    return assemble(where, mine + other, rows, cols).reshape(32 * rows, cols)
+
+
+def scatter_grad(grad, z, x, core, y):
+    rows, cols = grad.shape[0] // 32, grad.shape[1]
+    grid = grad.reshape(COLUMNS, 2, 2, 2, rows, cols)
+    arrived = swap(pick(grid, 1 - core, 2), over_core)
+    chip = pick(grid, core, 2) + arrived
+    low, high = chip[:2], chip[2:]
+    from_x = swap(pick(low, 1 - x, 1), over_x)
+    from_y = swap(pick(high, 1 - y, 2), over_y)
+    low = pick(low, x, 1) + from_x
+    high = pick(high, y, 2) + from_y
+    from_y = swap(pick(low, 1 - y, 1), over_y)
+    from_x = swap(pick(high, 1 - x, 1), over_x)
+    low = pick(low, y, 1) + from_y
+    high = pick(high, x, 1) + from_x
+    return sum_column(jnp.concatenate([low, high]), z)
+
+
+def sum_column(column, z):
+    total = pick(column, z, 0)
+    for k in range(1, COLUMNS):
+        total = total + swap(pick(column, z ^ k, 0), over_z[k])
+    return total
+
+
+def body_grid(
+    layer_input,
+    cotangent,
+    seq_lengths,
+    qkv_weight,
+    qv_bias,
+    out_weight,
+    out_bias,
+    first_gain,
+    first_shift,
+    up_weight,
+    up_bias,
+    down_weight,
+    down_bias,
+    second_gain,
+    second_shift,
+):
+    z, x, core, y = place()
+    where = jnp.stack([z, x, core, y]).astype(jnp.int32)
+    rows = layer_input.shape[0]
+    shard = qkv_weight.shape[0]
+    half = D // 2
+    pairs = half // PAIR
+    wide = 3 * half
+
+    def both_rows(own, other):
+        return jnp.where(
+            y == 0, jnp.concatenate([own, other]), jnp.concatenate([other, own])
+        )
+
+    def rows_of(values, part):
+        return lax.dynamic_slice_in_dim(values, part * rows, rows, 0)
+
+    other_input = swap(layer_input, over_y)
+
+    by_head = qkv_weight.reshape(shard, 3, 2, pairs, PAIR).transpose(2, 0, 3, 1, 4)
+    by_head = by_head.reshape(2, shard, wide)
+    line_one = jnp.concatenate([qv_bias, out_bias, first_gain, first_shift])
+    line_two = jnp.concatenate([up_bias, down_bias])
+    line_three = jnp.concatenate([second_gain, second_shift])
+    lines = jnp.stack(
+        [jnp.pad(line, (0, PAIR - line.shape[0])) for line in (line_one, line_two, line_three)]
+    )
+    small = jnp.pad(lines, ((0, shard - 3), (0, 0)))
+    sent = swap(jnp.concatenate([pick(by_head, 1 - y, 0), small], axis=1), over_y)
+    kept = jnp.concatenate([pick(by_head, y, 0), small], axis=1)
+    block = jnp.where(y == 0, jnp.stack([kept, sent]), jnp.stack([sent, kept]))
+    column = [block] + [swap(block, over_z[k]) for k in range(1, COLUMNS)]
+    column = jnp.stack(column)
+    column = jnp.stack([pick(column, z ^ k, 0) for k in range(COLUMNS)])
+    beside = swap(column, over_x)
+    plane = jnp.where(x == 0, jnp.stack([column, beside], 1), jnp.stack([beside, column], 1))
+    beside = swap(plane, over_core)
+    whole = jnp.where(core == 0, jnp.stack([plane, beside], 2), jnp.stack([beside, plane], 2))
+    whole = whole.reshape(32, shard, wide + PAIR)
+    w_qkv = whole[:, :, :wide].reshape(D, wide)
+    lines = whole[:, :3, wide:]
+    b_qv = lines[:, 0, : 2 * shard].reshape(2 * D)
+    b_out = lines[:, 0, 2 * shard : 3 * shard].reshape(D)
+    gain_one = lines[:, 0, 3 * shard : 4 * shard].reshape(D)
+    shift_one = lines[:, 0, 4 * shard : 5 * shard].reshape(D)
+    b_up = lines[:, 1, : 4 * shard].reshape(4 * D)
+    b_down = lines[:, 1, 4 * shard : 5 * shard].reshape(D)
+    gain_two = lines[:, 2, :shard].reshape(D)
+    shift_two = lines[:, 2, shard : 2 * shard].reshape(D)
+
+    w_out = gather_weight(where, out_weight)
+    w_up = gather_weight(where, up_weight)
+    w_down = gather_weight(where, down_weight)
+
+    inputs = both_rows(layer_input, other_input)
+    normed_out_one, normed_one, inv_one = norm_forward(inputs, gain_one, shift_one)
+    bias = pick(b_qv.reshape(2, 2, pairs, PAIR), y, 1)
+    qkv_bias = jnp.stack([bias[0], jnp.zeros_like(bias[0]), bias[1]], axis=1).reshape(wide)
+    projected = matmul(normed_out_one, w_qkv) + qkv_bias
+    head_out, log_sum = attend(seq_lengths, projected)
+    there = swap(rows_of(head_out, 1 - y), over_y)
+    here = rows_of(head_out, y)
+    attended = jnp.where(
+        y == 0, jnp.concatenate([here, there], 1), jnp.concatenate([there, here], 1)
+    )
+    middle = layer_input + matmul(attended, w_out) + b_out
+    normed_out_two, normed_two, inv_two = norm_forward(middle, gain_two, shift_two)
+    pre_act = matmul(normed_out_two, w_up) + b_up
+    activ = gelu_forward(pre_act)
+    layer_output = middle + matmul(activ, w_down) + b_down
+
+    d_down_b = jnp.sum(cotangent, axis=0)
+    d_pre = matmul_nt(cotangent, w_down) * gelu_slope(pre_act)
+    d_norm_two, d_gain_two, d_shift_two = norm_backward(
+        matmul_nt(d_pre, w_up), normed_two, inv_two, gain_two
+    )
+    d_middle = cotangent + d_norm_two
+    d_att = matmul_nt(d_middle, w_out)
+    d_heads = d_att.reshape(rows, 2, half)
+    there = swap(pick(d_heads, 1 - y, 1), over_y)
+    d_out = both_rows(pick(d_heads, y, 1), there)
+    d_down_w = matmul_tn(activ, cotangent)
+    down_grad = scatter_grad(d_down_w, z, x, core, y)
+    d_up_b = jnp.sum(d_pre, axis=0)
+    d_up_w = matmul_tn(normed_out_two, d_pre)
+    up_grad = scatter_grad(d_up_w, z, x, core, y)
+    d_out_b = jnp.sum(d_middle, axis=0)
+    d_out_w = matmul_tn(attended, d_middle)
+    out_grad = scatter_grad(d_out_w, z, x, core, y)
+
+    d_proj = attend_back(seq_lengths, projected, d_out, head_out, log_sum)
+    d_qkv_w = matmul_tn(normed_out_one, d_proj)
+    d_norm = matmul_nt(d_proj, w_qkv)
+    d_gain_one = jnp.sum(d_norm * normed_one, axis=0)
+    d_shift_one = jnp.sum(d_norm, axis=0)
+    d_norm_own = rows_of(d_norm, y) + swap(rows_of(d_norm, 1 - y), over_y)
+    d_norm_one, unused, unused = norm_backward(
+        d_norm_own, rows_of(normed_one, y), rows_of(inv_one, y), gain_one
+    )
+    input_grad = d_middle + d_norm_one
+
+    d_bias = jnp.sum(d_proj, axis=0).reshape(pairs, 3, PAIR)
+    d_bias = jnp.stack([d_bias[:, 0], d_bias[:, 2]]).reshape(2, 1, half)
+    blank = jnp.zeros_like(d_bias)
+    d_qv_b = jnp.where(
+        y == 0, jnp.concatenate([d_bias, blank], 1), jnp.concatenate([blank, d_bias], 1)
+    )
+
+    def lanes(*vectors):
+        line = jnp.concatenate([v.reshape(32, -1) for v in vectors], axis=1)
+        return jnp.pad(line, ((0, 0), (0, PAIR - line.shape[1])))
+
+    lines = jnp.stack(
+        [
+            lanes(d_qv_b, d_out_b, d_gain_one, d_shift_one),
+            lanes(d_up_b, d_down_b),
+            lanes(d_gain_two, d_shift_two),
+        ],
+        axis=1,
+    )
+    small = jnp.pad(lines, ((0, 0), (0, shard - 3), (0, 0)))
+    grid = jnp.concatenate([d_qkv_w.reshape(32, shard, wide), small], axis=2)
+    grid = grid.reshape(COLUMNS, 2, 2, 2, shard, wide + PAIR)
+    grid = pick(grid, core, 2) + swap(pick(grid, 1 - core, 2), over_core)
+    grid = pick(grid, x, 1) + swap(pick(grid, 1 - x, 1), over_x)
+    grid = sum_column(grid, z)
+    here = pick(grid, y, 0)
+    there = swap(pick(grid, 1 - y, 0), over_y)
+    lines = here[:, wide:] + there[:, wide:]
+    here, there = here[:, :wide], there[:, :wide]
+    qkv_grad = jnp.where(y == 0, jnp.stack([here, there]), jnp.stack([there, here]))
+    qkv_grad = qkv_grad.reshape(2, shard, pairs, 3, PAIR).transpose(1, 3, 0, 2, 4)
+    return (
+        layer_output,
+        input_grad,
+        qkv_grad.reshape(shard, 3 * D),
+        lines[0, : 2 * shard],
+        out_grad,
+        lines[0, 2 * shard : 3 * shard],
+        lines[0, 3 * shard : 4 * shard],
+        lines[0, 4 * shard : 5 * shard],
+        up_grad,
+        lines[1, : 4 * shard],
+        down_grad,
+        lines[1, 4 * shard : 5 * shard],
+        lines[2, :shard],
+        lines[2, shard : 2 * shard],
+    )
+
+
 def solution(mesh):
+    shape = (mesh.shape["dp"], mesh.shape["seq"])
+    body = body_grid if shape == (COLUMNS * 4, 2) else body_general
+    row = P(AXES, None)
+    vec = P(AXES)
     return jax.shard_map(
         body,
         mesh=mesh,
-        in_specs=(
-            P(("dp", "seq"), None),
-            P(("dp", "seq"), None),
-            P("dp"),
-            P(("dp", "seq"), None),
-            P(("dp", "seq")),
-            P(("dp", "seq"), None),
-            P(("dp", "seq")),
-            P(("dp", "seq")),
-            P(("dp", "seq")),
-            P(("dp", "seq"), None),
-            P(("dp", "seq")),
-            P(("dp", "seq"), None),
-            P(("dp", "seq")),
-            P(("dp", "seq")),
-            P(("dp", "seq")),
-        ),
-        out_specs=(
-            P(("dp", "seq"), None),
-            P(("dp", "seq"), None),
-            P(("dp", "seq"), None),
-            P(("dp", "seq")),
-            P(("dp", "seq"), None),
-            P(("dp", "seq")),
-            P(("dp", "seq")),
-            P(("dp", "seq")),
-            P(("dp", "seq"), None),
-            P(("dp", "seq")),
-            P(("dp", "seq"), None),
-            P(("dp", "seq")),
-            P(("dp", "seq")),
-            P(("dp", "seq")),
-        ),
+        in_specs=(row, row, P("dp"), row, vec, row, vec, vec, vec, row, vec, row, vec, vec, vec),
+        out_specs=(row, row, row, vec, row, vec, vec, vec, row, vec, row, vec, vec, vec),
         check_vma=False,
     )

time: 1280 us -> 1290 us (level)
  Pallas kernels: 0 us -> 693 us
  matrix products: 493 us -> 120 us
  waiting for transfers between devices: 620 us -> 262 us
  starting transfers between devices: 0.48 us -> 105 us
  blocking collectives: 83.6 us -> 0 us
  local copies, waits for them, and re-layouts: 30.9 us -> 53.7 us
  other arithmetic: 25 us -> 41 us
    pallas_call x0 -> x5, Pallas kernels: none -> 693 us  [the longest x3 649 us: assemble(): pl.pallas_call(functools.partial(assemble_kernel, len(pieces)), in_specs=...]
    reduce_scatter x6 -> x0, waiting for transfers between devices: 424 us -> none  [the longest x1 141 us: body(): lax.psum_scatter(d_down_w, ('dp', 'seq'), scatter_dimension=0, tiled=True)]
    ppermute x0 -> x76, waiting for transfers between devices: none -> 262 us  [swap(): return lax.ppermute(values, AXES, pairs)]
    all_gather x6 -> x0, waiting for transfers between devices: 192 us -> none  [the longest x1 63.6 us: body(): lax.all_gather(down_weight, ('dp', 'seq'), axis=0, tiled=True)]
    dot_general x40 -> x4, matrix products: 187 us -> 37.1 us  [matmul_nt(): lax.dot_general(left, right, (((1,), (1,)), ((), ())), precision=top_prec...]
    dot_general x28 -> x4, matrix products: 159 us -> 42.7 us  [matmul(): jnp.dot(left, right, precision=top_prec, preferred_element_type=jnp.float32)]
    dot_general x28 -> x4, matrix products: 147 us -> 40.5 us  [matmul_tn(): lax.dot_general(left, right, (((0,), (0,)), ((), ())), precision=top_prec...]
    ppermute x0 -> x76, starting transfers between devices: none -> 105 us  [swap(): return lax.ppermute(values, AXES, pairs)]
  transfers between devices with their start and end apart: 12 -> 76, of which waited for: 9 -> 30; matrix products, arithmetic and copies ran while one was open for 23% -> 11% of each run, Pallas kernels for 0% -> 54%
where the time goes in v1:
time: 1290 us; the launch traced here: 1280 us
  Pallas kernels  693 us (54%)
  waiting for transfers between devices  262 us (20%)
  matrix products  120 us (9%)
  starting transfers between devices  105 us (8%)
  local copies, waits for them, and re-layouts  53.7 us (4%)
  other arithmetic  41 us (3%)
    pallas_call x3, Pallas kernels, assemble(): pl.pallas_call(functools.partial(assemble_kernel, len(pieces)), in_specs=...  649 us
    ppermute x76, waiting for transfers between devices, swap(): return lax.ppermute(values, AXES, pairs)  262 us
    ppermute x76, starting transfers between devices, swap(): return lax.ppermute(values, AXES, pairs)  105 us
    dot_general x4, matrix products, matmul(): jnp.dot(left, right, precision=top_prec, preferred_element_type=jnp.float32)  42.7 us
    dot_general x4, matrix products, matmul_tn(): lax.dot_general(left, right, (((0,), (0,)), ((), ())), precision=top_prec...  40.5 us
    dot_general x4, matrix products, matmul_nt(): lax.dot_general(left, right, (((1,), (1,)), ((), ())), precision=top_prec...  37.1 us
    pallas_call x1, Pallas kernels, attend_back(): pl.pallas_call(attend_back_kernel, grid=(pairs,), in_specs=[pl.BlockSpec(...  27.6 us
  transfers between devices with their start and end apart: 76, of which 30 were waited for; matrix products, arithmetic and copies ran while one was open for 11% of the time, Pallas kernels for 54%

profile of v1, /device:TPU:0, one launch (start us, length us, event | category | flops | bytes accessed | tf_op | source)
XLA Modules:
  0.0 1277.5 jit_solution(16577620254735865729)
XLA Ops:
  6.6 3.3 collective-permute-done.1
  10.0 3.9 collective-permute-start.4
  20.9 11.4 collective-permute-start.33
  32.3 3.5 collective-permute-done.3
  44.1 3.8 collective-permute-start.10
  47.9 14.5 %collective-permute-done.33 = f32[96,768]{1,0:T(8,128)S(1)} collective-permute-done((f32[96,768]{1,0:T(8,128)S(1)}, f32[96,768]{1,0:T(8,128)S(1)}, u32[]{:S(2)}, u32[]{:S(2)}) %collective-permute-start.33) | collective-permute-done | bytes 294944 | tf_op jit(solution)/shard_map/ppermute | solution.py:436
  65.2 10.6 collective-permute-start.21
  75.8 4.8 collective-permute-done.9
  84.3 7.1 collective-permute-done.21
  92.9 23.2 %collective-permute-done.12.refs_2_ = f32[4,24,768]{2,1,0:T(8,128)} collective-permute-done((f32[4,24,768]{2,1,0:T(8,128)S(1)}, f32[4,24,768]{2,1,0:T(8,128)}, u32[]{:S(2)}, u32[]{:S(2)}) %collective-permute-start.12) | collective-permute-done | bytes 294944 | tf_op jit(solution)/shard_map/ppermute | solution.py:436
  120.9 3.7 maximum_select_fusion.3
  131.6 4.9 collective-permute-done.35.refs_1_
  138.5 19.0 %collective-permute-done.24.refs_2_ = f32[4,24,3072]{2,1,0:T(8,128)} collective-permute-done((f32[4,24,3072]{2,1,0:T(8,128)}, f32[4,24,3072]{2,1,0:T(8,128)}, u32[]{:S(2)}, u32[]{:S(2)}) %collective-permute-start.24) | collective-permute-done | bytes 1179680 | tf_op jit(solution)/shard_map/ppermute | solution.py:436
  174.9 4.0 slice.161
  185.1 10.3 convolution_add_fusion.qkv_ref
  198.0 11.6 collective-permute-done.25.refs_3_
  210.3 16.1 %attend.1 = (f32[1024,384]{1,0:T(8,128)S(1)}, f32[1024,384]{1,0:T(8,128)S(1)}) custom-call(s32[1]{0:T(128)S(6)} %copy.109.len_ref, f32[1024,1152]{1,0:T(8,128)} %convolution_add_fusion.qkv_ref), custom_call_target="tpu_custom_call" | custom-call | flops 13333332992 | bytes 7864320 | tf_op jit(solution)/shard_map/attend/pallas_call | solution.py:385
  230.9 73.5 %assemble.3 = f32[4,2,2,2,24,768]{5,4,3,2,1,0:T(8,128)} custom-call(s32[4]{0:T(128)} %pad_add_fusion.place_ref, f32[4,24,768]{2,1,0:T(8,128)} %copy-done.23, f32[4,24,768]{2,1,0:T(8,128)} %collective-permute-done.11.refs_1_, f32[4,24,768]{2,1,0:T(8,128)} %collective-permute-done.12.refs_2_, f32[2,24,768]{2,1,0:T(8,128)} %copy-done.32, ...), custom_call_target="tpu_custom_call" | custom-call | bytes 4718592 | tf_op jit(solution)/shard_map/assemble/pallas_call | solution.py:470
  304.6 287.9 %assemble.5 = f32[4,2,2,2,96,768]{5,4,3,2,1,0:T(8,128)} custom-call(s32[4]{0:T(128)} %pad_add_fusion.place_ref, f32[4,96,768]{2,1,0:T(8,128)} %pad_maximum_fusion.1.refs_0_, f32[4,96,768]{2,1,0:T(8,128)} %collective-permute-done.35.refs_1_, f32[4,96,768]{2,1,0:T(8,128)} %collective-permute-done.36.refs_2_, f32[2,96,768]{2,1,0:T(8,128)} %copy-done.24, ...), custom_call_target="tpu_custom_call" | custom-call | bytes 18874368 | tf_op jit(solution)/shard_map/assemble/pallas_call | solution.py:470
  592.5 287.9 %assemble.4 = f32[4,2,2,2,24,3072]{5,4,3,2,1,0:T(8,128)} custom-call(s32[4]{0:T(128)} %pad_add_fusion.place_ref, f32[4,24,3072]{2,1,0:T(8,128)} %pad_maximum_fusion.refs_0_, f32[4,24,3072]{2,1,0:T(8,128)} %collective-permute-done.23.refs_1_, f32[4,24,3072]{2,1,0:T(8,128)} %collective-permute-done.24.refs_2_, f32[2,24,3072]{2,1,0:T(8,128)} %collective-permute-done.25.refs_3_, ...), custom_call_target="tpu_custom_call" | custom-call | bytes 18874368 | tf_op jit(solution)/shard_map/assemble/pallas_call | solution.py:470
  881.9 5.3 fusion.91
  887.6 13.5 %fusion.20 = f32[512,3072]{1,0:T(8,128)} fusion(f32[768,3072]{1,0:T(8,128)} %bitcast.250, f32[512,768]{1,0:T(8,128)S(1)} %get-tuple-element.95, f32[768]{0:T(1024)S(1)} %add.368, f32[768]{0:T(1024)S(1)} %mul.153, f32[512]{0:T(512)S(1)} %add_rsqrt_fusion.1, f32[512]{0:T(512)S(1)} %broadcast_multiply_fusion.5), kind=kOutput, calls=%fused_computation.70 | convolution fusion | flops 7249330176 | bytes 17311744 | tf_op jit(solution)/shard_map/dot_general | solution.py:25
  901.1 13.6 %add_add_fusion = f32[512,768]{1,0:T(8,128)} fusion(f32[512,768]{1,0:T(8,128)S(1)} %get-tuple-element.95, f32[3072,768]{1,0:T(8,128)S(1)} %bitcast.270, f32[512,3072]{1,0:T(8,128)} %fusion.20, f32[3072]{0:T(1024)S(1)} %add.371, f32[768]{0:T(1024)S(1)} %add.376), kind=kOutput, calls=%fused_computation.60 | convolution fusion | flops 7256408064 | bytes 18889728 | tf_op jit(solution)/shard_map/dot_general | solution.py:25
  914.7 12.5 fusion.92
  927.2 12.7 multiply_reduce_fusion.2
  948.0 4.8 fusion.21
  955.7 12.5 fusion.19
  968.4 27.6 %attend_back.1 = f32[1024,1152]{1,0:T(8,128)} custom-call(s32[1]{0:T(128)S(6)} %copy.109.len_ref, f32[1024,1152]{1,0:T(8,128)} %convolution_add_fusion.qkv_ref, f32[1024,384]{1,0:T(8,128)S(1)} %maximum_select_fusion.5.do_ref, f32[1024,384]{1,0:T(8,128)S(1)} %get-tuple-element.16.out_ref, f32[1024,384]{1,0:T(8,128)S(1)} %get-tuple-element.17.lse_ref), custom_call_target="tpu_custom_call" | custom-call | flops 40000000000 | bytes 14155776 | tf_op jit(solution)/shard_map/attend_back/pallas_call | solution.py:400
  995.9 9.7 multiply_reduce_fusion
  1009.1 10.1 fusion.5
  1036.1 40.2 %collective-permute-done.55 = f32[2,2,24,768]{3,2,1,0:T(8,128)S(1)} collective-permute-done((f32[2,2,24,768]{3,2,1,0:T(8,128)S(1)}, f32[2,2,24,768]{3,2,1,0:T(8,128)S(1)}, u32[]{:S(2)}, u32[]{:S(2)}) %collective-permute-start.55) | collective-permute-done | bytes 294944 | tf_op jit(solution)/shard_map/ppermute | solution.py:436
  1081.7 10.1 collective-permute-start.57
  1095.4 13.2 %fusion.6 = f32[3072,768]{1,0:T(8,128)} fusion(f32[512,768]{1,0:T(8,128)S(1)} %copy-done.22, f32[512,3072]{1,0:T(8,128)} %fusion.20, f32[3072]{0:T(1024)S(1)} %add.371), kind=kOutput, calls=%fused_computation.24 | convolution fusion | flops 7255621632 | bytes 17313792 | tf_op jit(solution)/shard_map/dot_general | solution.py:29
  1108.6 3.4 collective-permute-start.58
  1111.9 6.9 constant_dynamic-slice_fusion.4
  1123.6 3.3 collective-permute-start.50
  1127.4 4.0 collective-permute-done.48
  1131.3 7.6 collective-permute-done.50
  1139.0 10.5 collective-permute-done.49
  1157.3 4.5 bitcast_add_fusion.1
  1170.4 21.1 %collective-permute-done.61 = f32[2,2,24,3072]{3,2,1,0:T(8,128)S(1)} collective-permute-done((f32[2,2,24,3072]{3,2,1,0:T(8,128)S(1)}, f32[2,2,24,3072]{3,2,1,0:T(8,128)S(1)}, u32[]{:S(2)}, u32[]{:S(2)}) %collective-permute-start.61) | collective-permute-done | bytes 1179680 | tf_op jit(solution)/shard_map/ppermute | solution.py:436
  1194.4 22.5 %collective-permute-done.69 = f32[2,2,96,768]{3,2,1,0:T(8,128)S(1)} collective-permute-done((f32[2,2,96,768]{3,2,1,0:T(8,128)S(1)}, f32[2,2,96,768]{3,2,1,0:T(8,128)S(1)}, u32[]{:S(2)}, u32[]{:S(2)}) %collective-permute-start.69) | collective-permute-done | bytes 1179680 | tf_op jit(solution)/shard_map/ppermute | solution.py:436
  1219.7 11.1 collective-permute-done.62
  1231.2 3.1 collective-permute-start.66
  1235.6 5.3 collective-permute-done.70
  1243.9 3.5 collective-permute-done.65
  1247.4 7.2 collective-permute-done.66
  1257.6 18.8 %collective-permute-done.74 = f32[96,768]{1,0:T(8,128)S(1)} collective-permute-done((f32[96,768]{1,0:T(8,128)S(1)}, f32[96,768]{1,0:T(8,128)S(1)}, u32[]{:S(2)}, u32[]{:S(2)}) %collective-permute-start.74) | collective-permute-done | bytes 294944 | tf_op jit(solution)/shard_map/ppermute | solution.py:436
  (361 shorter events, 151.2 us)
Async XLA Ops:
  13.9 21.9 %collective-permute-start.3 = (f32[2,24,1280]{2,1,0:T(8,128)S(1)}, f32[2,24,1280]{2,1,0:T(8,128)S(1)}, u32[]{:S(2)}, u32[]{:S(2)}) collective-permute-start(f32[2,24,1280]{2,1,0:T(8,128)S(1)} %maximum_select_fusion.10), channel_id=1, source_target_pairs={{0,16},{1,17},{2,18},{3,19},{4,20},{5,21},{6,22},{7,23},{8,24},{9,... | collective-permute-start | bytes 737288 | tf_op jit(solution)/shard_map/ppermute | solution.py:436
  14.5 25.0 %collective-permute-start.32 = (f32[96,768]{1,0:T(8,128)S(1)}, f32[96,768]{1,0:T(8,128)S(1)}, u32[]{:S(2)}, u32[]{:S(2)}) collective-permute-start(f32[96,768]{1,0:T(8,128)S(1)} %copy-done.28), channel_id=1, source_target_pairs={{0,8},{1,9},{2,10},{3,11},{4,12},{5,13},{6,14},{7,15},{8,0},{9,1},... | collective-permute-start | bytes 884744 | tf_op jit(solution)/shard_map/ppermute | solution.py:436
  15.9 28.2 %collective-permute-start.34 = (f32[96,768]{1,0:T(8,128)S(1)}, f32[96,768]{1,0:T(8,128)S(1)}, u32[]{:S(2)}, u32[]{:S(2)}) collective-permute-start(f32[96,768]{1,0:T(8,128)S(1)} %copy-done.28), channel_id=1, source_target_pairs={{0,24},{1,25},{2,26},{3,27},{4,28},{5,29},{6,30},{7,31},{8,16},{9,... | collective-permute-start | bytes 884744 | tf_op jit(solution)/shard_map/ppermute | solution.py:436
  20.9 41.5 %collective-permute-start.33 = (f32[96,768]{1,0:T(8,128)S(1)}, f32[96,768]{1,0:T(8,128)S(1)}, u32[]{:S(2)}, u32[]{:S(2)}) collective-permute-start(f32[96,768]{1,0:T(8,128)S(1)} %copy-done.28), channel_id=1, source_target_pairs={{0,16},{1,17},{2,18},{3,19},{4,20},{5,21},{6,22},{7,23},{8,24},{9,... | collective-permute-start | bytes 884744 | tf_op jit(solution)/shard_map/ppermute | solution.py:436
  37.5 82.8 %collective-permute-start.5 = (f32[4,2,24,1280]{3,2,1,0:T(8,128)S(1)}, f32[4,2,24,1280]{3,2,1,0:T(8,128)}, u32[]{:S(2)}, u32[]{:S(2)}) collective-permute-start(f32[4,2,24,1280]{3,2,1,0:T(8,128)S(1)} %get-tuple-element.67), channel_id=1, source_target_pairs={{0,4},{1,5},{2,6},{3,7},{4,0},{5,1},{6,2},{7,3},{8,12},{9,13},{10,... | collective-permute-start | bytes 2949128 | tf_op jit(solution)/shard_map/ppermute | solution.py:436
  39.3 42.9 %collective-permute-start.20 = (f32[24,3072]{1,0:T(8,128)S(1)}, f32[24,3072]{1,0:T(8,128)S(1)}, u32[]{:S(2)}, u32[]{:S(2)}) collective-permute-start(f32[24,3072]{1,0:T(8,128)S(1)} %copy-done.29), channel_id=1, source_target_pairs={{0,8},{1,9},{2,10},{3,11},{4,12},{5,13},{6,14},{7,15},{8,0},{9,1},... | collective-permute-start | bytes 884744 | tf_op jit(solution)/shard_map/ppermute | solution.py:436
  39.5 24.0 %collective-permute-start.8 = (f32[24,768]{1,0:T(8,128)S(1)}, f32[24,768]{1,0:T(8,128)S(1)}, u32[]{:S(2)}, u32[]{:S(2)}) collective-permute-start(f32[24,768]{1,0:T(8,128)S(1)} %copy-done.33), channel_id=1, source_target_pairs={{0,8},{1,9},{2,10},{3,11},{4,12},{5,13},{6,14},{7,15},{8,0},{9,1},... | collective-permute-start | bytes 221192 | tf_op jit(solution)/shard_map/ppermute | solution.py:436
  65.2 26.1 %collective-permute-start.21 = (f32[24,3072]{1,0:T(8,128)S(1)}, f32[24,3072]{1,0:T(8,128)S(1)}, u32[]{:S(2)}, u32[]{:S(2)}) collective-permute-start(f32[24,3072]{1,0:T(8,128)S(1)} %copy-done.29), channel_id=1, source_target_pairs={{0,16},{1,17},{2,18},{3,19},{4,20},{5,21},{6,22},{7,23},{8,24},{9,... | collective-permute-start | bytes 884744 | tf_op jit(solution)/shard_map/ppermute | solution.py:436
  80.6 44.0 %collective-permute-start.36 = (f32[4,96,768]{2,1,0:T(8,128)}, f32[4,96,768]{2,1,0:T(8,128)}, u32[]{:S(2)}, u32[]{:S(2)}) collective-permute-start(f32[4,96,768]{2,1,0:T(8,128)} %pad_maximum_fusion.1.refs_0_), channel_id=1, source_target_pairs={{0,1},{1,0},{2,3},{3,2},{4,5},{5,4},{6,7},{7,6},{8,9},{9,8},{10,11... | collective-permute-start | bytes 3538952 | tf_op jit(solution)/shard_map/ppermute | solution.py:436
  82.2 33.9 %collective-permute-start.12 = (f32[4,24,768]{2,1,0:T(8,128)S(1)}, f32[4,24,768]{2,1,0:T(8,128)}, u32[]{:S(2)}, u32[]{:S(2)}) collective-permute-start(f32[4,24,768]{2,1,0:T(8,128)S(1)} %pad_maximum_fusion.4.refs_0_), channel_id=1, source_target_pairs={{0,1},{1,0},{2,3},{3,2},{4,5},{5,4},{6,7},{7,6},{8,9},{9,8},{10,11... | collective-permute-start | bytes 884744 | tf_op jit(solution)/shard_map/ppermute | solution.py:436
  82.7 79.1 %collective-permute-start = (f32[512,768]{1,0:T(8,128)S(1)}, f32[512,768]{1,0:T(8,128)S(1)}, u32[]{:S(2)}, u32[]{:S(2)}) collective-permute-start(f32[512,768]{1,0:T(8,128)S(1)} %copy-done.7), channel_id=1, source_target_pairs={{0,1},{1,0},{2,3},{3,2},{4,5},{5,4},{6,7},{7,6},{8,9},{9,8},{10,11... | collective-permute-start | bytes 4718600 | tf_op jit(solution)/shard_map/ppermute | solution.py:436
  91.3 27.4 %collective-permute-start.11 = (f32[4,24,768]{2,1,0:T(8,128)S(1)}, f32[4,24,768]{2,1,0:T(8,128)}, u32[]{:S(2)}, u32[]{:S(2)}) collective-permute-start(f32[4,24,768]{2,1,0:T(8,128)S(1)} %pad_maximum_fusion.4.refs_0_), channel_id=1, source_target_pairs={{0,4},{1,5},{2,6},{3,7},{4,0},{5,1},{6,2},{7,3},{8,12},{9,13},{10,... | collective-permute-start | bytes 884744 | tf_op jit(solution)/shard_map/ppermute | solution.py:436
  118.8 38.7 %collective-permute-start.24 = (f32[4,24,3072]{2,1,0:T(8,128)}, f32[4,24,3072]{2,1,0:T(8,128)}, u32[]{:S(2)}, u32[]{:S(2)}) collective-permute-start(f32[4,24,3072]{2,1,0:T(8,128)} %pad_maximum_fusion.refs_0_), channel_id=1, source_target_pairs={{0,1},{1,0},{2,3},{3,2},{4,5},{5,4},{6,7},{7,6},{8,9},{9,8},{10,11... | collective-permute-start | bytes 3538952 | tf_op jit(solution)/shard_map/ppermute | solution.py:436
  120.3 39.1 %collective-permute-start.23 = (f32[4,24,3072]{2,1,0:T(8,128)}, f32[4,24,3072]{2,1,0:T(8,128)}, u32[]{:S(2)}, u32[]{:S(2)}) collective-permute-start(f32[4,24,3072]{2,1,0:T(8,128)} %pad_maximum_fusion.refs_0_), channel_id=1, source_target_pairs={{0,4},{1,5},{2,6},{3,7},{4,0},{5,1},{6,2},{7,3},{8,12},{9,13},{10,... | collective-permute-start | bytes 3538952 | tf_op jit(solution)/shard_map/ppermute | solution.py:436
  124.6 43.1 %collective-permute-start.6 = (f32[4,2,2,24,1280]{4,3,2,0,1:T(8,128)}, f32[4,2,2,24,1280]{4,3,2,0,1:T(8,128)}, u32[]{:S(2)}, u32[]{:S(2)}) collective-permute-start(f32[4,2,2,24,1280]{4,3,2,0,1:T(8,128)} %maximum_select_fusion.3), channel_id=1, source_target_pairs={{0,2},{1,3},{2,0},{3,1},{4,6},{5,7},{6,4},{7,5},{8,10},{9,11},{10,... | collective-permute-start | bytes 5898248 | tf_op jit(solution)/shard_map/ppermute | solution.py:436
  136.5 34.4 %collective-permute-start.15 = (f32[4,24,768]{2,1,0:T(8,128)S(1)}, f32[4,24,768]{2,1,0:T(8,128)S(1)}, u32[]{:S(2)}, u32[]{:S(2)}) collective-permute-start(f32[4,24,768]{2,1,0:T(8,128)S(1)} %pad_maximum_fusion.4.refs_0_), channel_id=1, source_target_pairs={{0,2},{1,3},{2,0},{3,1},{4,6},{5,7},{6,4},{7,5},{8,10},{9,11},{10,... | collective-permute-start | bytes 884744 | tf_op jit(solution)/shard_map/ppermute | solution.py:436
  157.5 25.1 %collective-permute-start.39 = (f32[4,96,768]{2,1,0:T(8,128)}, f32[4,96,768]{2,1,0:T(8,128)}, u32[]{:S(2)}, u32[]{:S(2)}) collective-permute-start(f32[4,96,768]{2,1,0:T(8,128)} %pad_maximum_fusion.1.refs_0_), channel_id=1, source_target_pairs={{0,2},{1,3},{2,0},{3,1},{4,6},{5,7},{6,4},{7,5},{8,10},{9,11},{10,... | collective-permute-start | bytes 3538952 | tf_op jit(solution)/shard_map/ppermute | solution.py:436
  159.4 24.7 %collective-permute-start.27 = (f32[4,24,3072]{2,1,0:T(8,128)}, f32[4,24,3072]{2,1,0:T(8,128)}, u32[]{:S(2)}, u32[]{:S(2)}) collective-permute-start(f32[4,24,3072]{2,1,0:T(8,128)} %pad_maximum_fusion.refs_0_), channel_id=1, source_target_pairs={{0,2},{1,3},{2,0},{3,1},{4,6},{5,7},{6,4},{7,5},{8,10},{9,11},{10,... | collective-permute-start | bytes 3538952 | tf_op jit(solution)/shard_map/ppermute | solution.py:436
  173.3 36.7 %collective-permute-start.41 = (f32[4,96,768]{2,1,0:T(8,128)}, f32[4,96,768]{2,1,0:T(8,128)}, u32[]{:S(2)}, u32[]{:S(2)}) collective-permute-start(f32[4,96,768]{2,1,0:T(8,128)} %collective-permute-done.36.refs_2_), channel_id=1, source_target_pairs={{0,2},{1,3},{2,0},{3,1},{4,6},{5,7},{6,4},{7,5},{8,10},{9,11},{10,... | collective-permute-start | bytes 3538952 | tf_op jit(solution)/shard_map/ppermute | solution.py:436
  182.6 26.9 %collective-permute-start.25 = (f32[2,24,3072]{2,1,0:T(8,128)}, f32[2,24,3072]{2,1,0:T(8,128)}, u32[]{:S(2)}, u32[]{:S(2)}) collective-permute-start(f32[2,24,3072]{2,1,0:T(8,128)} %slice.168), channel_id=1, source_target_pairs={{0,4},{1,5},{2,6},{3,7},{4,0},{5,1},{6,2},{7,3},{8,12},{9,13},{10,... | collective-permute-start | bytes 1769480 | tf_op jit(solution)/shard_map/ppermute | solution.py:436
  184.1 25.7 %collective-permute-start.26 = (f32[2,24,3072]{2,1,0:T(8,128)}, f32[2,24,3072]{2,1,0:T(8,128)}, u32[]{:S(2)}, u32[]{:S(2)}) collective-permute-start(f32[2,24,3072]{2,1,0:T(8,128)} %slice.169), channel_id=1, source_target_pairs={{0,1},{1,0},{2,3},{3,2},{4,5},{5,4},{6,7},{7,6},{8,9},{9,8},{10,11... | collective-permute-start | bytes 1769480 | tf_op jit(solution)/shard_map/ppermute | solution.py:436
  197.4 30.3 %collective-permute-start.40 = (f32[4,96,768]{2,1,0:T(8,128)}, f32[4,96,768]{2,1,0:T(8,128)}, u32[]{:S(2)}, u32[]{:S(2)}) collective-permute-start(f32[4,96,768]{2,1,0:T(8,128)} %collective-permute-done.35.refs_1_), channel_id=1, source_target_pairs={{0,2},{1,3},{2,0},{3,1},{4,6},{5,7},{6,4},{7,5},{8,10},{9,11},{10,... | collective-permute-start | bytes 3538952 | tf_op jit(solution)/shard_map/ppermute | solution.py:436
  198.0 394.5 %collective-permute-start.29 = (f32[4,24,3072]{2,1,0:T(8,128)}, f32[4,24,3072]{2,1,0:T(8,128)}, u32[]{:S(2)}, u32[]{:S(2)}) collective-permute-start(f32[4,24,3072]{2,1,0:T(8,128)} %collective-permute-done.24.refs_2_), channel_id=1, source_target_pairs={{0,2},{1,3},{2,0},{3,1},{4,6},{5,7},{6,4},{7,5},{8,10},{9,11},{10,... | collective-permute-start | bytes 3538952 | tf_op jit(solution)/shard_map/ppermute | solution.py:436
  209.5 383.0 %collective-permute-start.28 = (f32[4,24,3072]{2,1,0:T(8,128)}, f32[4,24,3072]{2,1,0:T(8,128)}, u32[]{:S(2)}, u32[]{:S(2)}) collective-permute-start(f32[4,24,3072]{2,1,0:T(8,128)} %collective-permute-done.23.refs_1_), channel_id=1, source_target_pairs={{0,2},{1,3},{2,0},{3,1},{4,6},{5,7},{6,4},{7,5},{8,10},{9,11},{10,... | collective-permute-start | bytes 3538952 | tf_op jit(solution)/shard_map/ppermute | solution.py:436
  227.6 654.2 %collective-permute-start.7 = (f32[512,384]{1,0:T(8,128)}, f32[512,384]{1,0:T(8,128)}, u32[]{:S(2)}, u32[]{:S(2)}) collective-permute-start(f32[512,384]{1,0:T(8,128)} %get-tuple-element.53), channel_id=1, source_target_pairs={{0,1},{1,0},{2,3},{3,2},{4,5},{5,4},{6,7},{7,6},{8,9},{9,8},{10,11... | collective-permute-start | bytes 2359304 | tf_op jit(solution)/shard_map/ppermute | solution.py:436
  228.7 363.8 %collective-permute-start.30 = (f32[2,24,3072]{2,1,0:T(8,128)}, f32[2,24,3072]{2,1,0:T(8,128)}, u32[]{:S(2)}, u32[]{:S(2)}) collective-permute-start(f32[2,24,3072]{2,1,0:T(8,128)} %collective-permute-done.25.refs_3_), channel_id=1, source_target_pairs={{0,2},{1,3},{2,0},{3,1},{4,6},{5,7},{6,4},{7,5},{8,10},{9,11},{10,... | collective-permute-start | bytes 1769480 | tf_op jit(solution)/shard_map/ppermute | solution.py:436
  230.3 362.2 %collective-permute-start.31 = (f32[2,24,3072]{2,1,0:T(8,128)}, f32[2,24,3072]{2,1,0:T(8,128)}, u32[]{:S(2)}, u32[]{:S(2)}) collective-permute-start(f32[2,24,3072]{2,1,0:T(8,128)} %collective-permute-done.26.refs_4_), channel_id=1, source_target_pairs={{0,2},{1,3},{2,0},{3,1},{4,6},{5,7},{6,4},{7,5},{8,10},{9,11},{10,... | collective-permute-start | bytes 1769480 | tf_op jit(solution)/shard_map/ppermute | solution.py:436
  955.0 67.1 %collective-permute-start.52 = (f32[4,2,2,24,768]{4,3,2,0,1:T(8,128)}, f32[4,2,2,24,768]{4,3,2,0,1:T(8,128)}, u32[]{:S(2)}, u32[]{:S(2)}) collective-permute-start(f32[4,2,2,24,768]{4,3,2,0,1:T(8,128)} %bitcast.245), channel_id=1, source_target_pairs={{0,2},{1,3},{2,0},{3,1},{4,6},{5,7},{6,4},{7,5},{8,10},{9,11},{10,... | collective-permute-start | bytes 3538952 | tf_op jit(solution)/shard_map/ppermute | solution.py:436
  1021.8 70.0 %collective-permute-start.46 = (f32[4,2,2,24,1280]{4,3,2,1,0:T(8,128)}, f32[4,2,2,24,1280]{4,3,2,1,0:T(8,128)}, u32[]{:S(2)}, u32[]{:S(2)}) collective-permute-start(f32[4,2,2,24,1280]{4,3,2,1,0:T(8,128)} %fusion.9), channel_id=1, source_target_pairs={{0,2},{1,3},{2,0},{3,1},{4,6},{5,7},{6,4},{7,5},{8,10},{9,11},{10,... | collective-permute-start | bytes 5898248 | tf_op jit(solution)/shard_map/ppermute | solution.py:436
  1031.8 125.5 %collective-permute-start.60 = (f32[4,2,2,24,3072]{4,3,2,0,1:T(8,128)}, f32[4,2,2,24,3072]{4,3,2,0,1:T(8,128)}, u32[]{:S(2)}, u32[]{:S(2)}) collective-permute-start(f32[4,2,2,24,3072]{4,3,2,0,1:T(8,128)} %bitcast.241), channel_id=1, source_target_pairs={{0,2},{1,3},{2,0},{3,1},{4,6},{5,7},{6,4},{7,5},{8,10},{9,11},{10,... | collective-permute-start | bytes 14155784 | tf_op jit(solution)/shard_map/ppermute | solution.py:436
  1032.7 89.5 %collective-permute-start.45 = (f32[512,768]{1,0:T(8,128)S(1)}, f32[512,768]{1,0:T(8,128)S(1)}, u32[]{:S(2)}, u32[]{:S(2)}) collective-permute-start(f32[512,768]{1,0:T(8,128)S(1)} %constant_dynamic-slice_fusion.13), channel_id=1, source_target_pairs={{0,1},{1,0},{2,3},{3,2},{4,5},{5,4},{6,7},{7,6},{8,9},{9,8},{10,11... | collective-permute-start | bytes 4718600 | tf_op jit(solution)/shard_map/ppermute | solution.py:436
  1033.9 42.5 %collective-permute-start.55 = (f32[2,2,24,768]{3,2,1,0:T(8,128)S(1)}, f32[2,2,24,768]{3,2,1,0:T(8,128)S(1)}, u32[]{:S(2)}, u32[]{:S(2)}) collective-permute-start(f32[2,2,24,768]{3,2,1,0:T(8,128)S(1)} %bitcast.287), channel_id=1, source_target_pairs={{0,1},{1,0},{2,3},{3,2},{4,5},{5,4},{6,7},{7,6},{8,9},{9,8},{10,11... | collective-permute-start | bytes 884744 | tf_op jit(solution)/shard_map/ppermute | solution.py:436
  1035.1 43.5 %collective-permute-start.54 = (f32[2,24,768]{2,1,0:T(8,128)S(1)}, f32[2,24,768]{2,1,0:T(8,128)S(1)}, u32[]{:S(2)}, u32[]{:S(2)}) collective-permute-start(f32[2,24,768]{2,1,0:T(8,128)S(1)} %dynamic-slice_bitcast_fusion.14), channel_id=1, source_target_pairs={{0,1},{1,0},{2,3},{3,2},{4,5},{5,4},{6,7},{7,6},{8,9},{9,8},{10,11... | collective-permute-start | bytes 442376 | tf_op jit(solution)/shard_map/ppermute | solution.py:436
  1081.7 30.2 %collective-permute-start.57 = (f32[24,768]{1,0:T(8,128)S(1)}, f32[24,768]{1,0:T(8,128)S(1)}, u32[]{:S(2)}, u32[]{:S(2)}) collective-permute-start(f32[24,768]{1,0:T(8,128)S(1)} %get-tuple-element.74), channel_id=1, source_target_pairs={{0,8},{1,9},{2,10},{3,11},{4,12},{5,13},{6,14},{7,15},{8,0},{9,1},... | collective-permute-start | bytes 221192 | tf_op jit(solution)/shard_map/ppermute | solution.py:436
  1094.7 28.1 %collective-permute-start.47 = (f32[4,2,24,1280]{3,2,1,0:T(8,128)}, f32[4,2,24,1280]{3,2,1,0:T(8,128)S(1)}, u32[]{:S(2)}, u32[]{:S(2)}) collective-permute-start(f32[4,2,24,1280]{3,2,1,0:T(8,128)} %dynamic-slice_bitcast_fusion.2), channel_id=1, source_target_pairs={{0,4},{1,5},{2,6},{3,7},{4,0},{5,1},{6,2},{7,3},{8,12},{9,13},{10,... | collective-permute-start | bytes 2949128 | tf_op jit(solution)/shard_map/ppermute | solution.py:436
  1121.6 43.4 %collective-permute-start.68 = (f32[4,2,2,96,768]{4,3,2,0,1:T(8,128)}, f32[4,2,2,96,768]{4,3,2,0,1:T(8,128)}, u32[]{:S(2)}, u32[]{:S(2)}) collective-permute-start(f32[4,2,2,96,768]{4,3,2,0,1:T(8,128)} %bitcast.240), channel_id=1, source_target_pairs={{0,2},{1,3},{2,0},{3,1},{4,6},{5,7},{6,4},{7,5},{8,10},{9,11},{10,... | collective-permute-start | bytes 14155784 | tf_op jit(solution)/shard_map/ppermute | solution.py:436
  1126.9 22.6 %collective-permute-start.49 = (f32[2,24,1280]{2,1,0:T(8,128)S(1)}, f32[2,24,1280]{2,1,0:T(8,128)S(1)}, u32[]{:S(2)}, u32[]{:S(2)}) collective-permute-start(f32[2,24,1280]{2,1,0:T(8,128)S(1)} %get-tuple-element.64), channel_id=1, source_target_pairs={{0,16},{1,17},{2,18},{3,19},{4,20},{5,21},{6,22},{7,23},{8,24},{9,... | collective-permute-start | bytes 737288 | tf_op jit(solution)/shard_map/ppermute | solution.py:436
  1162.6 29.0 %collective-permute-start.61 = (f32[2,2,24,3072]{3,2,1,0:T(8,128)S(1)}, f32[2,2,24,3072]{3,2,1,0:T(8,128)S(1)}, u32[]{:S(2)}, u32[]{:S(2)}) collective-permute-start(f32[2,2,24,3072]{3,2,1,0:T(8,128)S(1)} %dynamic-slice_bitcast_fusion.1), channel_id=1, source_target_pairs={{0,4},{1,5},{2,6},{3,7},{4,0},{5,1},{6,2},{7,3},{8,12},{9,13},{10,... | collective-permute-start | bytes 3538952 | tf_op jit(solution)/shard_map/ppermute | solution.py:436
  1164.0 28.9 %collective-permute-start.63 = (f32[2,2,24,3072]{3,2,1,0:T(8,128)S(1)}, f32[2,2,24,3072]{3,2,1,0:T(8,128)S(1)}, u32[]{:S(2)}, u32[]{:S(2)}) collective-permute-start(f32[2,2,24,3072]{3,2,1,0:T(8,128)S(1)} %bitcast.274), channel_id=1, source_target_pairs={{0,1},{1,0},{2,3},{3,2},{4,5},{5,4},{6,7},{7,6},{8,9},{9,8},{10,11... | collective-permute-start | bytes 3538952 | tf_op jit(solution)/shard_map/ppermute | solution.py:436
  1168.6 48.2 %collective-permute-start.69 = (f32[2,2,96,768]{3,2,1,0:T(8,128)S(1)}, f32[2,2,96,768]{3,2,1,0:T(8,128)S(1)}, u32[]{:S(2)}, u32[]{:S(2)}) collective-permute-start(f32[2,2,96,768]{3,2,1,0:T(8,128)S(1)} %dynamic-slice_bitcast_fusion), channel_id=1, source_target_pairs={{0,4},{1,5},{2,6},{3,7},{4,0},{5,1},{6,2},{7,3},{8,12},{9,13},{10,... | collective-permute-start | bytes 3538952 | tf_op jit(solution)/shard_map/ppermute | solution.py:436
  1169.4 48.7 %collective-permute-start.71 = (f32[2,2,96,768]{3,2,1,0:T(8,128)S(1)}, f32[2,2,96,768]{3,2,1,0:T(8,128)S(1)}, u32[]{:S(2)}, u32[]{:S(2)}) collective-permute-start(f32[2,2,96,768]{3,2,1,0:T(8,128)S(1)} %bitcast.275), channel_id=1, source_target_pairs={{0,1},{1,0},{2,3},{3,2},{4,5},{5,4},{6,7},{7,6},{8,9},{9,8},{10,11... | collective-permute-start | bytes 3538952 | tf_op jit(solution)/shard_map/ppermute | solution.py:436
  1191.8 39.0 %collective-permute-start.62 = (f32[2,24,3072]{2,1,0:T(8,128)S(1)}, f32[2,24,3072]{2,1,0:T(8,128)S(1)}, u32[]{:S(2)}, u32[]{:S(2)}) collective-permute-start(f32[2,24,3072]{2,1,0:T(8,128)S(1)} %dynamic-slice_bitcast_fusion.8), channel_id=1, source_target_pairs={{0,1},{1,0},{2,3},{3,2},{4,5},{5,4},{6,7},{7,6},{8,9},{9,8},{10,11... | collective-permute-start | bytes 1769480 | tf_op jit(solution)/shard_map/ppermute | solution.py:436
  1193.0 37.8 %collective-permute-start.64 = (f32[2,24,3072]{2,1,0:T(8,128)S(1)}, f32[2,24,3072]{2,1,0:T(8,128)S(1)}, u32[]{:S(2)}, u32[]{:S(2)}) collective-permute-start(f32[2,24,3072]{2,1,0:T(8,128)S(1)} %dynamic-slice_bitcast_fusion.7), channel_id=1, source_target_pairs={{0,4},{1,5},{2,6},{3,7},{4,0},{5,1},{6,2},{7,3},{8,12},{9,13},{10,... | collective-permute-start | bytes 1769480 | tf_op jit(solution)/shard_map/ppermute | solution.py:436
  1217.1 23.9 %collective-permute-start.70 = (f32[2,96,768]{2,1,0:T(8,128)S(1)}, f32[2,96,768]{2,1,0:T(8,128)S(1)}, u32[]{:S(2)}, u32[]{:S(2)}) collective-permute-start(f32[2,96,768]{2,1,0:T(8,128)S(1)} %dynamic-slice_bitcast_fusion.6), channel_id=1, source_target_pairs={{0,1},{1,0},{2,3},{3,2},{4,5},{5,4},{6,7},{7,6},{8,9},{9,8},{10,11... | collective-permute-start | bytes 1769480 | tf_op jit(solution)/shard_map/ppermute | solution.py:436
  1218.4 22.7 %collective-permute-start.72 = (f32[2,96,768]{2,1,0:T(8,128)S(1)}, f32[2,96,768]{2,1,0:T(8,128)S(1)}, u32[]{:S(2)}, u32[]{:S(2)}) collective-permute-start(f32[2,96,768]{2,1,0:T(8,128)S(1)} %dynamic-slice_bitcast_fusion.5), channel_id=1, source_target_pairs={{0,4},{1,5},{2,6},{3,7},{4,0},{5,1},{6,2},{7,3},{8,12},{9,13},{10,... | collective-permute-start | bytes 1769480 | tf_op jit(solution)/shard_map/ppermute | solution.py:436
  1231.2 23.4 %collective-permute-start.66 = (f32[24,3072]{1,0:T(8,128)S(1)}, f32[24,3072]{1,0:T(8,128)S(1)}, u32[]{:S(2)}, u32[]{:S(2)}) collective-permute-start(f32[24,3072]{1,0:T(8,128)S(1)} %get-tuple-element.58), channel_id=1, source_target_pairs={{0,16},{1,17},{2,18},{3,19},{4,20},{5,21},{6,22},{7,23},{8,24},{9,... | collective-permute-start | bytes 884744 | tf_op jit(solution)/shard_map/ppermute | solution.py:436
  1241.4 35.0 %collective-permute-start.74 = (f32[96,768]{1,0:T(8,128)S(1)}, f32[96,768]{1,0:T(8,128)S(1)}, u32[]{:S(2)}, u32[]{:S(2)}) collective-permute-start(f32[96,768]{1,0:T(8,128)S(1)} %get-tuple-element.55), channel_id=1, source_target_pairs={{0,16},{1,17},{2,18},{3,19},{4,20},{5,21},{6,22},{7,23},{8,24},{9,... | collective-permute-start | bytes 884744 | tf_op jit(solution)/shard_map/ppermute | solution.py:436
  1247.4 29.0 %collective-permute-start.75 = (f32[96,768]{1,0:T(8,128)S(1)}, f32[96,768]{1,0:T(8,128)S(1)}, u32[]{:S(2)}, u32[]{:S(2)}) collective-permute-start(f32[96,768]{1,0:T(8,128)S(1)} %get-tuple-element.56), channel_id=1, source_target_pairs={{0,24},{1,25},{2,26},{3,27},{4,28},{5,29},{6,30},{7,31},{8,16},{9,... | collective-permute-start | bytes 884744 | tf_op jit(solution)/shard_map/ppermute | solution.py:436
  (73 other events, 960.4 us)

commit v2 on v1

--- a/solution.py
+++ b/solution.py
@@ -295,7 +295,8 @@
 def fold(v):
     return v[:,:PAIR]+v[:,PAIR:]
 
-def attend_kernel(len_ref,qkv_ref,out_ref,lse_ref):
+def attend_kernel(len_ref,qkv_ref,*refs):
+    out_ref,lse_ref=refs[-2:]
     rows=qkv_ref.shape[0]
     seq_len=len_ref[0]
     lane=lax.broadcasted_iota(jnp.int32,(1,PAIR),1)
@@ -329,7 +330,8 @@
         out_ref[start:stop]=jnp.where(lane<HEAD_DIM,outs[0],outs[1])
         lse_ref[start:stop]=jnp.where(lane<HEAD_DIM,lses[0],lses[1])
 
-def attend_back_kernel(len_ref,qkv_ref,do_ref,out_ref,lse_ref,grad_ref):
+def attend_back_kernel(len_ref,qkv_ref,do_ref,out_ref,lse_ref,*refs):
+    grad_ref=refs[-1]
     rows=qkv_ref.shape[0]
     seq_len=len_ref[0]
     lane=lax.broadcasted_iota(jnp.int32,(1,PAIR),1)
@@ -343,7 +345,6 @@
     do_twice=jnp.concatenate([do_high,do_high],axis=1)
     delta_t=jnp.transpose(do_all*out_ref[...])
     lse_t=jnp.transpose(lse_ref[...])
-    q_sum=[None,None]
     dq=[[jnp.zeros((TILE,PAIR),f32) for _ in range(rows//TILE)] for _ in range(2)]
     for start in range(0,rows,TILE):
         stop=start+TILE
@@ -378,35 +379,37 @@
         grad_ref[start:stop,2*PAIR:]=jnp.where(lane<HEAD_DIM,v_grads[0],v_grads[1])
         grad_ref[start:stop,:PAIR]=(dq[0][start//TILE]+dq[1][start//TILE])*scale
 
-def attend(seq_len,qkv):
+def attend(seq_len,qkv,*earlier):
     rows,cols=qkv.shape
     pairs=cols//(3*PAIR)
     block=lambda w: pl.BlockSpec((rows,w),lambda j:(0,j))
     return pl.pallas_call(
         attend_kernel,
         grid=(pairs,),
-        in_specs=[pl.BlockSpec(memory_space=pltpu.SMEM),block(3*PAIR)],
+        in_specs=[pl.BlockSpec(memory_space=pltpu.SMEM),block(3*PAIR)]
+        +[pl.BlockSpec(memory_space=pl.ANY)]*len(earlier),
         out_specs=[block(PAIR),block(PAIR)],
         out_shape=[jax.ShapeDtypeStruct((rows,pairs*PAIR),f32)]*2,
         compiler_params=pltpu.CompilerParams(vmem_limit_bytes=48*2**20),
-        cost_estimate=pl.CostEstimate(flops=40*10**9//3,bytes_accessed=4*rows*pairs*PAIR*5,transcendentals=rows*rows*pairs),
+        cost_estimate=pl.CostEstimate(flops=0,bytes_accessed=0,transcendentals=0),
         name="attend",
-    )(seq_len,qkv)
-
-def attend_back(seq_len,qkv,d_out,out,lse):
+    )(seq_len,qkv,*earlier)
+
+def attend_back(seq_len,qkv,d_out,out,lse,*earlier):
     rows,cols=qkv.shape
     pairs=cols//(3*PAIR)
     block=lambda w: pl.BlockSpec((rows,w),lambda j:(0,j))
     return pl.pallas_call(
         attend_back_kernel,
         grid=(pairs,),
-        in_specs=[pl.BlockSpec(memory_space=pltpu.SMEM),block(3*PAIR),block(PAIR),block(PAIR),block(PAIR)],
+        in_specs=[pl.BlockSpec(memory_space=pltpu.SMEM),block(3*PAIR),block(PAIR),block(PAIR),block(PAIR)]
+        +[pl.BlockSpec(memory_space=pl.ANY)]*len(earlier),
         out_specs=block(3*PAIR),
         out_shape=jax.ShapeDtypeStruct((rows,cols),f32),
         compiler_params=pltpu.CompilerParams(vmem_limit_bytes=48*2**20),
-        cost_estimate=pl.CostEstimate(flops=40*10**9,bytes_accessed=4*rows*pairs*PAIR*9,transcendentals=rows*rows*pairs),
+        cost_estimate=pl.CostEstimate(flops=0,bytes_accessed=0,transcendentals=0),
         name="attend_back",
-    )(seq_len,qkv,d_out,out,lse)
+    )(seq_len,qkv,d_out,out,lse,*earlier)
 
 
 COLUMNS = 4
@@ -445,75 +448,118 @@
     return lax.dynamic_index_in_dim(values, index, axis, keepdims=False)
 
 
-def assemble_kernel(count, place_ref, *refs):
-    pieces, out_ref, sems = refs[:count], refs[count], refs[count + 1]
-    z, x, core, y = (place_ref[i] for i in range(4))
+def order_kernel(*refs):
+    pass
+
+
+def after(values, *earlier):
+    anywhere = pl.BlockSpec(memory_space=pl.ANY)
+    return pl.pallas_call(
+        order_kernel,
+        in_specs=[anywhere] * (1 + len(earlier)),
+        out_specs=anywhere,
+        out_shape=jax.ShapeDtypeStruct(values.shape, values.dtype),
+        input_output_aliases={0: 0},
+        cost_estimate=pl.CostEstimate(flops=0, bytes_accessed=0, transcendentals=0),
+        name="after",
+    )(values, *earlier)
+
+
+def assemble_kernel(plan, place_ref, *refs):
+    count, copies_of = plan
+    pieces, outs, sems = refs[:count], refs[count:-1], refs[-1]
+    mine = [place_ref[i] for i in range(4)]
     copies = []
-    for c in range(2):
-        own, beside_x, beside_y, corner_a, corner_b = pieces[c * 5 : c * 5 + 5]
-        sources = [(own, 0, 0, 0, 4), (beside_x, 1, 0, 0, 4), (beside_y, 0, 1, 0, 4)]
-        sources += [(corner_a, 1, 1, 0, 2), (corner_b, 1, 1, 2, 4)]
-        for piece, dx, dy, first, last in sources:
-            for k in range(first, last):
-                slot = out_ref.at[z ^ k, x ^ dx, core ^ c, y ^ dy]
-                copies.append(
-                    pltpu.make_async_copy(piece.at[k - first], slot, sems.at[len(copies)])
-                )
+    for piece, source, out, shift, axes in copies_of:
+        slot = tuple(mine[axis] ^ move for axis, move in zip(axes, shift))
+        copies.append(
+            pltpu.make_async_copy(
+                pieces[piece].at[source], outs[out].at[slot], sems.at[len(copies)]
+            )
+        )
     for copy in copies:
         copy.start()
     for copy in copies:
         copy.wait()
 
 
-def assemble(where, pieces, rows, cols):
+def assemble(where, pieces, shapes, copies):
     anywhere = pl.BlockSpec(memory_space=pl.ANY)
+    whole = pl.BlockSpec(memory_space=pltpu.VMEM)
+    size = 4 * sum(functools.reduce(lambda m, n: m * n, shape) for shape in shapes)
     return pl.pallas_call(
-        functools.partial(assemble_kernel, len(pieces)),
+        functools.partial(assemble_kernel, (len(pieces), copies)),
         in_specs=[pl.BlockSpec(memory_space=pltpu.SMEM)] + [anywhere] * len(pieces),
-        out_specs=anywhere,
-        out_shape=jax.ShapeDtypeStruct((COLUMNS, 2, 2, 2, rows, cols), f32),
-        scratch_shapes=[pltpu.SemaphoreType.DMA((32,))],
-        cost_estimate=pl.CostEstimate(
-            flops=0, bytes_accessed=2 * 32 * rows * cols * 4, transcendentals=0
-        ),
+        out_specs=[whole] * len(shapes),
+        out_shape=[jax.ShapeDtypeStruct(shape, f32) for shape in shapes],
+        scratch_shapes=[pltpu.SemaphoreType.DMA((len(copies),))],
+        compiler_params=pltpu.CompilerParams(vmem_limit_bytes=size + 4 * 2**20),
+        cost_estimate=pl.CostEstimate(flops=0, bytes_accessed=0, transcendentals=0),
         name="assemble",
     )(where, *pieces)
 
 
-def gather_weight(where, shard):
-    rows, cols = shard.shape
-    own = jnp.stack([shard] + [swap(shard, over_z[k]) for k in range(1, COLUMNS)])
-    beside_x = swap(own, over_x)
-    beside_y = swap(own, over_y)
-    corner_a = swap(beside_y[:2], over_x)
-    corner_b = swap(beside_x[2:], over_y)
-    mine = [own, beside_x, beside_y, corner_a, corner_b]
-    other = [swap(piece, over_core) for piece in mine]
-    return assemble(where, mine + other, rows, cols).reshape(32 * rows, cols)
-
-
-def scatter_grad(grad, z, x, core, y):
-    rows, cols = grad.shape[0] // 32, grad.shape[1]
-    grid = grad.reshape(COLUMNS, 2, 2, 2, rows, cols)
-    arrived = swap(pick(grid, 1 - core, 2), over_core)
-    chip = pick(grid, core, 2) + arrived
-    low, high = chip[:2], chip[2:]
-    from_x = swap(pick(low, 1 - x, 1), over_x)
-    from_y = swap(pick(high, 1 - y, 2), over_y)
-    low = pick(low, x, 1) + from_x
-    high = pick(high, y, 2) + from_y
-    from_y = swap(pick(low, 1 - y, 1), over_y)
-    from_x = swap(pick(high, 1 - x, 1), over_x)
-    low = pick(low, y, 1) + from_y
-    high = pick(high, x, 1) + from_x
-    return sum_column(jnp.concatenate([low, high]), z)
-
-
-def sum_column(column, z):
+def plane_pieces():
+    for k in range(COLUMNS):
+        yield 0, k, k, 0, 0
+        yield 1, k, k, 1, 0
+        yield 2, k, k, 0, 1
+        yield 3 + k // 2, k % 2, k, 1, 1
+
+
+def gather_column(shard):
+    return jnp.stack([shard] + [swap(shard, over_z[k]) for k in range(1, COLUMNS)])
+
+
+def gather_sides(own):
+    return swap(own, over_x), swap(own, over_y)
+
+
+def gather_corners(beside_x, beside_y, before_x, before_y):
+    return (
+        swap(after(beside_y[:2], *before_x), over_x),
+        swap(after(beside_x[2:], *before_y), over_y),
+    )
+
+
+def by_core(own, other, core, axis):
+    return jnp.where(
+        core == 0, jnp.stack([own, other], axis), jnp.stack([other, own], axis)
+    )
+
+
+def plane_sent(chip, x, y, y_axis):
+    return pick(chip[:2], 1 - x, 1), pick(chip[2:], 1 - y, y_axis)
+
+
+def over_plane(chip, sent, x, y, y_axis, earlier):
+    low = pick(chip[:2], x, 1) + after(swap(sent[0], over_x), earlier)
+    high = pick(chip[2:], y, y_axis) + after(swap(sent[1], over_y), earlier)
+    return low, high
+
+
+def corner_sent(low, high, x, y, y_axis):
+    return pick(low, 1 - y, y_axis - 1), pick(high, 1 - x, 1)
+
+
+def over_corner(low, high, sent, x, y, y_axis, earlier):
+    from_y = after(swap(sent[0], over_y), earlier)
+    from_x = after(swap(sent[1], over_x), earlier)
+    return jnp.concatenate([pick(low, y, y_axis - 1) + from_y, pick(high, x, 1) + from_x])
+
+
+def sum_column(column, z, *earlier):
     total = pick(column, z, 0)
     for k in range(1, COLUMNS):
-        total = total + swap(pick(column, z ^ k, 0), over_z[k])
+        arrived = swap(pick(column, z ^ k, 0), over_z[k])
+        total = total + (after(arrived, *earlier) if earlier else arrived)
     return total
+
+
+def normalise(values):
+    centred = values - jnp.mean(values, axis=1, keepdims=True)
+    inv_std = lax.rsqrt(jnp.mean(centred * centred, axis=1, keepdims=True) + eps_norm)
+    return centred * inv_std, inv_std
 
 
 def body_grid(
@@ -540,6 +586,7 @@
     half = D // 2
     pairs = half // PAIR
     wide = 3 * half
+    hidden = 2 * D
 
     def both_rows(own, other):
         return jnp.where(
@@ -549,7 +596,9 @@
     def rows_of(values, part):
         return lax.dynamic_slice_in_dim(values, part * rows, rows, 0)
 
-    other_input = swap(layer_input, over_y)
+    normed_own, inv_one = normalise(layer_input)
+    other_normed = swap(normed_own, over_y)
+    other_cotangent = swap(cotangent, over_core)
 
     by_head = qkv_weight.reshape(shard, 3, 2, pairs, PAIR).transpose(2, 0, 3, 1, 4)
     by_head = by_head.reshape(2, shard, wide)
@@ -563,73 +612,156 @@
     sent = swap(jnp.concatenate([pick(by_head, 1 - y, 0), small], axis=1), over_y)
     kept = jnp.concatenate([pick(by_head, y, 0), small], axis=1)
     block = jnp.where(y == 0, jnp.stack([kept, sent]), jnp.stack([sent, kept]))
-    column = [block] + [swap(block, over_z[k]) for k in range(1, COLUMNS)]
-    column = jnp.stack(column)
-    column = jnp.stack([pick(column, z ^ k, 0) for k in range(COLUMNS)])
+    column = gather_column(block)
     beside = swap(column, over_x)
-    plane = jnp.where(x == 0, jnp.stack([column, beside], 1), jnp.stack([beside, column], 1))
-    beside = swap(plane, over_core)
-    whole = jnp.where(core == 0, jnp.stack([plane, beside], 2), jnp.stack([beside, plane], 2))
-    whole = whole.reshape(32, shard, wide + PAIR)
-    w_qkv = whole[:, :, :wide].reshape(D, wide)
-    lines = whole[:, :3, wide:]
+
+    by_unit = up_weight.reshape(shard, 2 * COLUMNS, 2, 8 * shard).transpose(2, 0, 1, 3)
+    by_unit = by_unit.reshape(2, shard, hidden)
+    kept_up = pick(by_unit, core, 0)
+    arrived_up = swap(pick(by_unit, 1 - core, 0), over_core)
+    both_up = by_core(kept_up, arrived_up, core, 1).reshape(shard, 2 * hidden)
+    shard_a = after(jnp.concatenate([out_weight, both_up], axis=1), column)
+    arrived_a = [swap(shard_a, over_z[k]) for k in range(1, COLUMNS)]
+    own_a = jnp.stack([shard_a] + arrived_a)
+    beside = after(beside, arrived_a[0])
+    arrived_b = [swap(after(down_weight, own_a), over_z[k]) for k in range(1, COLUMNS)]
+    own_a = after(own_a, beside)
+    sides_a = gather_sides(own_a)
+
+    pieces = [column, beside]
+    pieces += [swap(column, over_core), swap(after(beside, other_normed), over_core)]
+    copies = []
+    for k in range(COLUMNS):
+        for piece in range(4):
+            shift = (k, piece % 2, piece // 2)
+            copies.append((piece, (k, slice(None), slice(None), slice(0, wide)), 0, shift, (0, 1, 2)))
+            copies.append(
+                (piece, (k, slice(None), slice(0, 8), slice(wide, wide + PAIR)), 1, shift, (0, 1, 2))
+            )
+    grid = (COLUMNS, 2, 2, 2)
+    w_qkv, lines = assemble(
+        where, pieces, [grid + (shard, wide), grid + (8, PAIR)], copies
+    )
+    w_qkv = w_qkv.reshape(D, wide)
+    lines = lines.reshape(32, 8, PAIR)
     b_qv = lines[:, 0, : 2 * shard].reshape(2 * D)
     b_out = lines[:, 0, 2 * shard : 3 * shard].reshape(D)
     gain_one = lines[:, 0, 3 * shard : 4 * shard].reshape(D)
     shift_one = lines[:, 0, 4 * shard : 5 * shard].reshape(D)
-    b_up = lines[:, 1, : 4 * shard].reshape(4 * D)
+    b_up = lines[:, 1, : 4 * shard].reshape(2 * COLUMNS, 2, 2, 4 * shard)
+    b_up = pick(b_up, core, 1).reshape(hidden)
     b_down = lines[:, 1, 4 * shard : 5 * shard].reshape(D)
     gain_two = lines[:, 2, :shard].reshape(D)
     shift_two = lines[:, 2, shard : 2 * shard].reshape(D)
 
-    w_out = gather_weight(where, out_weight)
-    w_up = gather_weight(where, up_weight)
-    w_down = gather_weight(where, down_weight)
-
-    inputs = both_rows(layer_input, other_input)
-    normed_out_one, normed_one, inv_one = norm_forward(inputs, gain_one, shift_one)
+    normed_one = both_rows(normed_own, other_normed)
+    normed_out_one = normed_one * gain_one + shift_one
     bias = pick(b_qv.reshape(2, 2, pairs, PAIR), y, 1)
     qkv_bias = jnp.stack([bias[0], jnp.zeros_like(bias[0]), bias[1]], axis=1).reshape(wide)
     projected = matmul(normed_out_one, w_qkv) + qkv_bias
-    head_out, log_sum = attend(seq_lengths, projected)
+    own_b = jnp.stack([down_weight] + [after(piece, projected) for piece in arrived_b])
+    head_out, log_sum = attend(seq_lengths, projected, own_b)
     there = swap(rows_of(head_out, 1 - y), over_y)
     here = rows_of(head_out, y)
     attended = jnp.where(
         y == 0, jnp.concatenate([here, there], 1), jnp.concatenate([there, here], 1)
     )
+
+    corners_a = gather_corners(*sides_a, [head_out], [there])
+    sides_b = swap(after(own_b, head_out), over_x), swap(after(own_b, there), over_y)
+    corners_b = gather_corners(*sides_b, corners_a, corners_a)
+    every = slice(None)
+    copies = []
+    for piece, at, dz, dx, dy in plane_pieces():
+        copies.append((piece, (at, every, slice(0, D)), 0, (dz, dx, dy), (0, 1, 3)))
+    w_out_half, = assemble(
+        where, [own_a, *sides_a, *corners_a], [(COLUMNS, 2, 2, shard, D)], copies
+    )
+    copies = []
+    for piece, at, dz, dx, dy in plane_pieces():
+        for c in range(2):
+            cols = slice(D + c * hidden, D + (c + 1) * hidden)
+            copies.append((piece, (at, every, cols), c, (dz, dx, dy), (0, 1, 3)))
+    w_up_parts = assemble(
+        where, [own_a, *sides_a, *corners_a], [(COLUMNS, 2, 2, shard, hidden)] * 2, copies
+    )
+    copies = []
+    for piece, at, dz, dx, dy in plane_pieces():
+        copies.append((piece, (at,), 0, (dz, dx, dy), (0, 1, 3)))
+    w_down, = assemble(
+        where, [own_b, *sides_b, *corners_b], [(COLUMNS, 2, 2, 4 * shard, D)], copies
+    )
+    w_out = by_core(w_out_half, swap(w_out_half, over_core), core, 2).reshape(D, D)
+    w_up = jnp.stack(w_up_parts, axis=2).reshape(D, hidden)
+    w_down = w_down.reshape(hidden, D)
+
     middle = layer_input + matmul(attended, w_out) + b_out
     normed_out_two, normed_two, inv_two = norm_forward(middle, gain_two, shift_two)
-    pre_act = matmul(normed_out_two, w_up) + b_up
+    both_normed = jnp.concatenate([normed_out_two, swap(normed_out_two, over_core)])
+    both_cotangent = jnp.concatenate([cotangent, other_cotangent])
+    raw_act = matmul(both_normed, w_up)
+    pre_act = raw_act + b_up
     activ = gelu_forward(pre_act)
-    layer_output = middle + matmul(activ, w_down) + b_down
 
     d_down_b = jnp.sum(cotangent, axis=0)
-    d_pre = matmul_nt(cotangent, w_down) * gelu_slope(pre_act)
+    d_down_w = matmul_tn(activ, both_cotangent)
+    chip_b = d_down_w.reshape(COLUMNS, 2, 2, 4 * shard, D)
+    d_pre = matmul_nt(both_cotangent, w_down) * gelu_slope(pre_act)
+    d_up_b = jnp.sum(d_pre, axis=0)
+    d_part = matmul_nt(d_pre, w_up)
     d_norm_two, d_gain_two, d_shift_two = norm_backward(
-        matmul_nt(d_pre, w_up), normed_two, inv_two, gain_two
+        d_part[:rows] + swap(d_part[rows:], over_core), normed_two, inv_two, gain_two
     )
     d_middle = cotangent + d_norm_two
     d_att = matmul_nt(d_middle, w_out)
     d_heads = d_att.reshape(rows, 2, half)
-    there = swap(pick(d_heads, 1 - y, 1), over_y)
-    d_out = both_rows(pick(d_heads, y, 1), there)
-    d_down_w = matmul_tn(activ, cotangent)
-    down_grad = scatter_grad(d_down_w, z, x, core, y)
-    d_up_b = jnp.sum(d_pre, axis=0)
-    d_up_w = matmul_tn(normed_out_two, d_pre)
-    up_grad = scatter_grad(d_up_w, z, x, core, y)
+    sent = pick(d_heads, 1 - y, 1)
+    d_out = both_rows(pick(d_heads, y, 1), swap(sent, over_y))
+    down_part = matmul(gelu_forward(raw_act + after(b_up, sent)), w_down)
+    layer_output = middle + down_part[:rows] + swap(down_part[rows:], over_core) + b_down
+    chip_a = matmul_tn(both_normed, d_pre).reshape(COLUMNS, 2, 2, 2, shard, hidden)
+    low_b, high_b = over_plane(chip_b, plane_sent(chip_b, x, y, 2), x, y, 2, chip_a)
+    sent_b = corner_sent(low_b, high_b, x, y, 2)
+    column_b = over_corner(low_b, high_b, sent_b, x, y, 2, sent)
+    low_a, high_a = over_plane(chip_a, plane_sent(chip_a, x, y, 3), x, y, 3, sent)
+    sent_a = corner_sent(low_a, high_a, x, y, 3)
     d_out_b = jnp.sum(d_middle, axis=0)
-    d_out_w = matmul_tn(attended, d_middle)
-    out_grad = scatter_grad(d_out_w, z, x, core, y)
-
-    d_proj = attend_back(seq_lengths, projected, d_out, head_out, log_sum)
+    d_out_w = matmul_tn(attended, d_middle).reshape(COLUMNS, 2, 2, 2, shard, D)
+
+    d_proj = attend_back(
+        seq_lengths, projected, d_out, head_out, log_sum, *sent_a, column_b
+    )
     d_qkv_w = matmul_tn(normed_out_one, d_proj)
-    d_norm = matmul_nt(d_proj, w_qkv)
+    grid = d_qkv_w.reshape(COLUMNS, 2, 2, 2, shard, wide)
+    first = pick(grid, 1 - core, 2)
+    grid = pick(grid, core, 2) + swap(first, over_core)
+    sent = pick(grid, 1 - x, 1)
+    grid = pick(grid, x, 1) + swap(sent, over_x)
+    column_a = over_corner(low_a, high_a, sent_a, x, y, 3, first)
+    down_grad = sum_column(column_b, z, first)
+    up_parts = sum_column(column_a, z, sent)
+    arrived = swap(pick(up_parts, 1 - core, 0), over_core)
+    up_grad = by_core(
+        pick(up_parts, core, 0).reshape(shard, 2 * COLUMNS, 8 * shard),
+        arrived.reshape(shard, 2 * COLUMNS, 8 * shard),
+        core,
+        2,
+    ).reshape(shard, 4 * D)
+
+    column_qkv = grid
+    grid = sum_column(column_qkv, z)
+    here = pick(grid, y, 0)
+    there = swap(pick(grid, 1 - y, 0), over_y)
+    qkv_grad = jnp.where(y == 0, jnp.stack([here, there]), jnp.stack([there, here]))
+    qkv_grad = qkv_grad.reshape(2, shard, pairs, 3, PAIR).transpose(1, 3, 0, 2, 4)
+
+    d_norm = matmul_nt(d_proj, after(w_qkv, first))
     d_gain_one = jnp.sum(d_norm * normed_one, axis=0)
     d_shift_one = jnp.sum(d_norm, axis=0)
-    d_norm_own = rows_of(d_norm, y) + swap(rows_of(d_norm, 1 - y), over_y)
+    d_norm_other = swap(after(rows_of(d_norm, 1 - y), sent), over_y)
+    d_norm_own = rows_of(d_norm, y) + after(d_norm_other, here)
     d_norm_one, unused, unused = norm_backward(
-        d_norm_own, rows_of(normed_one, y), rows_of(inv_one, y), gain_one
+        d_norm_own, normed_own, inv_one, gain_one
     )
     input_grad = d_middle + d_norm_one
 
@@ -639,6 +771,9 @@
     d_qv_b = jnp.where(
         y == 0, jnp.concatenate([d_bias, blank], 1), jnp.concatenate([blank, d_bias], 1)
     )
+
+    d_up_b = d_up_b.reshape(2 * COLUMNS, 8 * shard)
+    d_up_b = by_core(d_up_b, jnp.zeros_like(d_up_b), core, 1)
 
     def lanes(*vectors):
         line = jnp.concatenate([v.reshape(32, -1) for v in vectors], axis=1)
@@ -653,17 +788,13 @@
         axis=1,
     )
     small = jnp.pad(lines, ((0, 0), (0, shard - 3), (0, 0)))
-    grid = jnp.concatenate([d_qkv_w.reshape(32, shard, wide), small], axis=2)
-    grid = grid.reshape(COLUMNS, 2, 2, 2, shard, wide + PAIR)
-    grid = pick(grid, core, 2) + swap(pick(grid, 1 - core, 2), over_core)
+    small = small.reshape(COLUMNS, 2, 2, 2, shard, PAIR)
+    grid = jnp.concatenate([d_out_w, small], axis=-1)
+    grid = pick(grid, core, 2) + swap(after(pick(grid, 1 - core, 2), sent), over_core)
+    grid = pick(grid, y, 2) + after(swap(pick(grid, 1 - y, 2), over_y), column_qkv)
     grid = pick(grid, x, 1) + swap(pick(grid, 1 - x, 1), over_x)
     grid = sum_column(grid, z)
-    here = pick(grid, y, 0)
-    there = swap(pick(grid, 1 - y, 0), over_y)
-    lines = here[:, wide:] + there[:, wide:]
-    here, there = here[:, :wide], there[:, :wide]
-    qkv_grad = jnp.where(y == 0, jnp.stack([here, there]), jnp.stack([there, here]))
-    qkv_grad = qkv_grad.reshape(2, shard, pairs, 3, PAIR).transpose(1, 3, 0, 2, 4)
+    out_grad, lines = grid[:, :D], grid[:, D:]
     return (
         layer_output,
         input_grad,

time: 1290 us -> 541 us (0.42)
  Pallas kernels: 693 us -> 54.5 us
  waiting for transfers between devices: 262 us -> 169 us
  starting transfers between devices: 105 us -> 54.8 us
  local copies, waits for them, and re-layouts: 53.7 us -> 80.6 us
  other arithmetic: 41 us -> 63.8 us
    pallas_call x3 -> x38, Pallas kernels: 649 us -> 10.8 us  [the longest x4 10.8 us: assemble(): pl.pallas_call(functools.partial(assemble_kernel, (len(pieces), copies)),...]
    ppermute x76 -> x58, waiting for transfers between devices: 262 us -> 169 us  [swap(): return lax.ppermute(values, AXES, pairs)]
    ppermute x76 -> x58, starting transfers between devices: 105 us -> 54.8 us  [swap(): return lax.ppermute(values, AXES, pairs)]
    unnamed x90 -> x228, local copies, waits for them, and re-layouts: 5.69 us -> 35 us
    dynamic_slice x13 -> x3, local copies, waits for them, and re-layouts: 18.3 us -> 0.06 us  [pick(): return lax.dynamic_index_in_dim(values, index, axis, keepdims=False)]
    add x21 -> x18, other arithmetic: 14 us -> 30 us  [the longest x2 4.62 us: over_plane(): high = pick(chip[2:], y, y_axis) + after(swap(sent[1], over_y), earlier)]
  transfers between devices with their start and end apart: 76 -> 58, of which waited for: 30 -> 21; matrix products, arithmetic and copies ran while one was open for 11% -> 33% of each run, Pallas kernels for 54% -> 10%
where the time goes in v2:
time: 541 us; the launch traced here: 535 us
  waiting for transfers between devices  169 us (31%)
  matrix products  109 us (20%)
  local copies, waits for them, and re-layouts  80.6 us (15%)
  other arithmetic  63.8 us (12%)
  starting transfers between devices  54.8 us (10%)
  Pallas kernels  54.5 us (10%)
    ppermute x58, waiting for transfers between devices, swap(): return lax.ppermute(values, AXES, pairs)  169 us
    ppermute x58, starting transfers between devices, swap(): return lax.ppermute(values, AXES, pairs)  54.8 us
    dot_general x4, matrix products, matmul(): jnp.dot(left, right, precision=top_prec, preferred_element_type=jnp.float32)  40.7 us
    dot_general x4, matrix products, matmul_tn(): lax.dot_general(left, right, (((0,), (0,)), ((), ())), precision=top_prec...  36.3 us
    unnamed x228, local copies, waits for them, and re-layouts  35 us
    dot_general x4, matrix products, matmul_nt(): lax.dot_general(left, right, (((1,), (1,)), ((), ())), precision=top_prec...  32.2 us
    pallas_call x1, Pallas kernels, attend_back(): pl.pallas_call(attend_back_kernel, grid=(pairs,), in_specs=[pl.BlockSpec(...  27.2 us
    pallas_call x1, Pallas kernels, attend(): pl.pallas_call(attend_kernel, grid=(pairs,), in_specs=[pl.BlockSpec(memor...  16.5 us
  transfers between devices with their start and end apart: 58, of which 21 were waited for; matrix products, arithmetic and copies ran while one was open for 33% of the time, Pallas kernels for 10%

profile of v2, /device:TPU:0, one launch (start us, length us, event | category | flops | bytes accessed | tf_op | source)
XLA Modules:
  0.0 535.4 jit_solution(930741171624191422)
XLA Ops:
  2.4 3.0 collective-permute-start.1
  8.8 3.9 collective-permute-start.4
  14.9 4.8 collective-permute-done.4
  19.7 13.1 %collective-permute-done.3 = f32[2,24,1280]{2,1,0:T(8,128)S(1)} collective-permute-done((f32[2,24,1280]{2,1,0:T(8,128)S(1)}, f32[2,24,1280]{2,1,0:T(8,128)S(1)}, u32[]{:S(2)}, u32[]{:S(2)}) %collective-permute-start.3) | collective-permute-done | bytes 245792 | tf_op jit(solution)/shard_map/ppermute | solution.py:439
  35.7 9.5 %collective-permute-done.7.refs_1_ = f32[24,3840]{1,0:T(8,128)S(1)} collective-permute-done((f32[24,3840]{1,0:T(8,128)}, f32[24,3840]{1,0:T(8,128)S(1)}, u32[]{:S(2)}, u32[]{:S(2)}) %collective-permute-start.7) | collective-permute-done | bytes 368672 | tf_op jit(solution)/shard_map/ppermute | solution.py:439
  45.2 10.4 %collective-permute-done.5.refs_0_ = f32[4,2,24,1280]{3,2,1,0:T(8,128)S(1)} collective-permute-done((f32[4,2,24,1280]{3,2,1,0:T(8,128)S(1)}, f32[4,2,24,1280]{3,2,1,0:T(8,128)S(1)}, u32[]{:S(2)}, u32[]{:S(2)}) %collective-permute-start.5) | collective-permute-done | bytes 983072 | tf_op jit(solution)/shard_map/ppermute | solution.py:439
  62.8 10.5 %collective-permute-done.11 = f32[24,3840]{1,0:T(8,128)} collective-permute-done((f32[24,3840]{1,0:T(8,128)S(1)}, f32[24,3840]{1,0:T(8,128)}, u32[]{:S(2)}, u32[]{:S(2)}) %collective-permute-start.11) | collective-permute-done | bytes 368672 | tf_op jit(solution)/shard_map/ppermute | solution.py:439
  73.2 18.5 %collective-permute-done.10 = f32[24,3840]{1,0:T(8,128)} collective-permute-done((f32[24,3840]{1,0:T(8,128)S(1)}, f32[24,3840]{1,0:T(8,128)}, u32[]{:S(2)}, u32[]{:S(2)}) %collective-permute-start.10) | collective-permute-done | bytes 368672 | tf_op jit(solution)/shard_map/ppermute | solution.py:439
  91.8 2.3 pad_maximum_fusion.5.refs_1_.refs_0_
  94.1 2.4 collective-permute-start.14
  112.1 12.6 %convolution_add_fusion.refs_1_.qkv_ref = f32[1024,1152]{1,0:T(8,128)} fusion(f32[768,1152]{1,0:T(8,128)} %bitcast.265, f32[1152]{0:T(1024)S(1)} %add.337, f32[768]{0:T(1024)S(1)} %add.334, f32[768]{0:T(1024)S(1)} %mul.150, f32[512,768]{1,0:T(8,128)} %collective-permute-done.refs_1_, f32[512,768]{1,0:T(8,128)} %subtract_multiply_fusion.1, pred[]{:T(512)S(6)} %eq.7), kind=kOutput, calls=%fused_computation.19 | convolution fusion | flops 5440929792 | bytes 11414017 | tf_op jit(solution)/shard_map/dot_general | solution.py:25
  127.1 16.5 %attend.1 = (f32[1024,384]{1,0:T(8,128)S(1)}, f32[1024,384]{1,0:T(8,128)S(1)}) custom-call(s32[1]{0:T(128)S(6)} %copy.162.len_ref, f32[1024,1152]{1,0:T(8,128)} %convolution_add_fusion.refs_1_.qkv_ref, f32[4,96,768]{2,1,0:T(8,128)S(1)} %pad_maximum_fusion.6.refs_0_), custom_call_target="tpu_custom_call" | custom-call | tf_op jit(solution)/shard_map/attend/pallas_call | solution.py:386
  150.3 13.2 %collective-permute-done.15.refs_1_ = f32[512,384]{1,0:T(8,128)} collective-permute-done((f32[512,384]{1,0:T(8,128)}, f32[512,384]{1,0:T(8,128)}, u32[]{:S(2)}, u32[]{:S(2)}) %collective-permute-start.15) | collective-permute-done | bytes 786464 | tf_op jit(solution)/shard_map/ppermute | solution.py:439
  164.0 14.5 %collective-permute-done.19.refs_4_.refs_2_ = f32[2,24,3840]{2,1,0:T(8,128)S(1)} collective-permute-done((f32[2,24,3840]{2,1,0:T(8,128)}, f32[2,24,3840]{2,1,0:T(8,128)S(1)}, u32[]{:S(2)}, u32[]{:S(2)}) %collective-permute-start.19) | collective-permute-done | bytes 737312 | tf_op jit(solution)/shard_map/ppermute | solution.py:439
  179.9 2.9 assemble.5
  187.0 2.8 maximum_select_fusion.1
  192.2 3.8 fusion.90
  198.0 2.7 fusion.88
  201.4 12.8 %collective-permute-done.23.refs_1_ = f32[4,96,768]{2,1,0:T(8,128)} collective-permute-done((f32[4,96,768]{2,1,0:T(8,128)}, f32[4,96,768]{2,1,0:T(8,128)}, u32[]{:S(2)}, u32[]{:S(2)}) %collective-permute-start.23) | collective-permute-done | bytes 1179680 | tf_op jit(solution)/shard_map/ppermute | solution.py:439
  219.1 2.7 constant_dynamic-update-slice_fusion
  225.1 3.1 assemble.6
  233.1 2.7 assemble.7
  235.9 11.5 %fusion.24 = f32[1024,1536]{1,0:T(8,128)S(1)} fusion(f32[768,1536]{1,0:T(8,128)S(1)} %bitcast.287, f32[512,768]{1,0:T(8,128)} %collective-permute-done.21, f32[512,768]{1,0:T(8,128)} %multiply_add_fusion.5), kind=kOutput, calls=%fused_computation.32 | convolution fusion | flops 7248543744 | bytes 14155776 | tf_op jit(solution)/shard_map/dot_general | solution.py:25
  247.4 10.0 %fusion.5 = f32[1536,768]{1,0:T(8,128)S(1)} fusion(f32[1024,768]{1,0:T(8,128)S(1)} %copy-done.72, f32[1024,1536]{1,0:T(8,128)S(1)} %fusion.24, f32[1536]{0:T(1024)S(1)} %reshape.258.refs_0_), kind=kOutput, calls=%fused_computation.6 | convolution fusion | flops 7255621632 | bytes 14161920 | tf_op jit(solution)/shard_map/dot_general | solution.py:29
  257.4 10.6 %fusion.91 = (f32[1536]{0:T(1024)S(1)}, f32[1024,1536]{1,0:T(8,128)S(1)}) fusion(f32[1024,1536]{1,0:T(8,128)S(1)} %fusion.24, f32[1536]{0:T(1024)S(1)} %reshape.258.refs_0_, f32[1024,768]{1,0:T(8,128)S(1)} %copy-done.72, f32[1536,768]{1,0:T(8,128)S(1)} %bitcast.267), kind=kOutput, calls=%fused_computation.242 | convolution fusion | flops 7265057280 | bytes 20459520 | tf_op jit(solution)/shard_map/dot_general | solution.py:39
  268.0 7.9 %fusion.92 = f32[1024,768]{1,0:T(8,128)S(1)} fusion(f32[1024,1536]{1,0:T(8,128)S(1)} %get-tuple-element.90, f32[768,1536]{1,0:T(8,128)S(1)} %bitcast.288), kind=kOutput, calls=%fused_computation.243 | convolution fusion | flops 7247757312 | bytes 14155776 | tf_op jit(solution)/shard_map/dot_general | solution.py:39
  282.7 10.7 %fusion.23 = f32[768,1536]{1,0:T(8,128)S(1)} fusion(f32[1024,1536]{1,0:T(8,128)S(1)} %get-tuple-element.90, f32[512,768]{1,0:T(8,128)} %collective-permute-done.21, f32[512,768]{1,0:T(8,128)} %multiply_add_fusion.5), kind=kOutput, calls=%fused_computation.31 | convolution fusion | flops 7248543744 | bytes 14155776 | tf_op jit(solution)/shard_map/dot_general | solution.py:29
  302.9 5.7 %collective-permute-done.34.refs_0_ = f32[2,2,96,768]{3,2,1,0:T(8,128)} collective-permute-done((f32[2,2,96,768]{3,2,1,0:T(8,128)}, f32[2,2,96,768]{3,2,1,0:T(8,128)}, u32[]{:S(2)}, u32[]{:S(2)}) %collective-permute-start.34) | collective-permute-done | bytes 1179680 | tf_op jit(solution)/shard_map/ppermute | solution.py:439
  316.9 2.9 multiply_reduce_fusion.1
  319.8 2.7 fusion.85
  326.7 12.7 %fusion.8 = f32[1024,768]{1,0:T(8,128)S(1)} fusion(f32[1536,768]{1,0:T(8,128)} %bitcast.268, f32[1024,1536]{1,0:T(8,128)} %copy-done.110, f32[1536]{0:T(1024)} %after.48), kind=kOutput, calls=%fused_computation.9 | convolution fusion | flops 7255621632 | bytes 14161920 | tf_op jit(solution)/shard_map/dot_general | solution.py:25
  345.5 2.9 bitcast_add_fusion.4
  348.5 3.9 fusion.33
  362.3 2.4 collective-permute-start.57
  366.8 27.2 %attend_back.1 = f32[1024,1152]{1,0:T(8,128)} custom-call(s32[1]{0:T(128)S(6)} %copy.162.len_ref, f32[1024,1152]{1,0:T(8,128)} %convolution_add_fusion.refs_1_.qkv_ref, f32[1024,384]{1,0:T(8,128)S(1)} %maximum_select_fusion.3.do_ref, f32[1024,384]{1,0:T(8,128)S(1)} %copy-done.2, f32[1024,384]{1,0:T(8,128)} %copy-done.17, ...), custom_call_target="tpu_custom_call" | custom-call | tf_op jit(solution)/shard_map/attend_back/pallas_call | solution.py:402
  394.0 11.8 %fusion.22 = f32[768,1152]{1,0:T(8,128)} fusion(f32[1024,1152]{1,0:T(8,128)} %attend_back.1, f32[768]{0:T(1024)S(1)} %copy-done.101, f32[768]{0:T(1024)S(1)} %copy-done.93, f32[512,768]{1,0:T(8,128)} %collective-permute-done.refs_1_, f32[512,768]{1,0:T(8,128)} %subtract_multiply_fusion.1, pred[]{:T(512)S(6)} %eq.7), kind=kOutput, calls=%fused_computation.30 | convolution fusion | flops 5439750144 | bytes 11409409 | tf_op jit(solution)/shard_map/dot_general | solution.py:29
  405.8 2.6 reduce_sum.152
  408.4 2.8 dynamic-slice_bitcast_fusion.refs_1_
  418.2 11.5 %multiply_reduce_fusion = (f32[768]{0:T(1024)}, f32[768]{0:T(1024)}, f32[1024,768]{1,0:T(8,128)}) fusion(f32[512,768]{1,0:T(8,128)} %subtract_multiply_fusion.1, f32[512,768]{1,0:T(8,128)} %collective-permute-done.refs_1_, pred[]{:T(512)S(6)} %eq.7, f32[1024,1152]{1,0:T(8,128)} %attend_back.1, f32[768,1152]{1,0:T(8,128)S(1)} %copy-done.6), kind=kOutput, calls=%fused_computation.22 | convolution fusion | flops 5440535040 | bytes 14555137 | tf_op jit(solution)/shard_map/dot_general | solution.py:39
  433.4 2.4 collective-permute-start.53
  448.3 14.2 %collective-permute-done.52.refs_0_ = f32[2,24,1536]{2,1,0:T(8,128)} collective-permute-done((f32[2,24,1536]{2,1,0:T(8,128)}, f32[2,24,1536]{2,1,0:T(8,128)}, u32[]{:S(2)}, u32[]{:S(2)}) %collective-permute-start.52) | collective-permute-done | bytes 294944 | tf_op jit(solution)/shard_map/ppermute | solution.py:439
  466.7 2.5 collective-permute-start.41
  471.1 3.1 fusion.26
  477.1 10.8 %collective-permute-done.40 = f32[2,24,1152]{2,1,0:T(8,128)} collective-permute-done((f32[2,24,1152]{2,1,0:T(8,128)}, f32[2,24,1152]{2,1,0:T(8,128)}, u32[]{:S(2)}, u32[]{:S(2)}) %collective-permute-start.40) | collective-permute-done | bytes 221216 | tf_op jit(solution)/shard_map/ppermute | solution.py:439
  496.7 14.2 %collective-permute-done.42 = f32[24,1152]{1,0:T(8,128)S(1)} collective-permute-done((f32[24,1152]{1,0:T(8,128)S(1)}, f32[24,1152]{1,0:T(8,128)S(1)}, u32[]{:S(2)}, u32[]{:S(2)}) %collective-permute-start.42) | collective-permute-done | bytes 110624 | tf_op jit(solution)/shard_map/ppermute | solution.py:439
  513.3 2.4 fusion.84
  517.8 6.7 %collective-permute-done.45 = f32[4,24,896]{2,1,0:T(8,128)S(1)} collective-permute-done((f32[4,24,896]{2,1,0:T(8,128)S(1)}, f32[4,24,896]{2,1,0:T(8,128)S(1)}, u32[]{:S(2)}, u32[]{:S(2)}) %collective-permute-start.45) | collective-permute-done | bytes 344096 | tf_op jit(solution)/shard_map/ppermute | solution.py:439
  524.6 2.3 collective-permute-start.48
  (493 shorter events, 164.9 us)
Async XLA Ops:
  7.3 51.5 %collective-permute-start = (f32[512,768]{1,0:T(8,128)}, f32[512,768]{1,0:T(8,128)}, u32[]{:S(2)}, u32[]{:S(2)}) collective-permute-start(f32[512,768]{1,0:T(8,128)} %subtract_multiply_fusion.1), channel_id=1, source_target_pairs={{0,1},{1,0},{2,3},{3,2},{4,5},{5,4},{6,7},{7,6},{8,9},{9,8},{10,11... | collective-permute-start | bytes 4718600 | tf_op jit(solution)/shard_map/ppermute | solution.py:439
  8.8 10.9 %collective-permute-start.4 = (f32[2,24,1280]{2,1,0:T(8,128)S(1)}, f32[2,24,1280]{2,1,0:T(8,128)S(1)}, u32[]{:S(2)}, u32[]{:S(2)}) collective-permute-start(f32[2,24,1280]{2,1,0:T(8,128)S(1)} %maximum_select_fusion.12), channel_id=1, source_target_pairs={{0,24},{1,25},{2,26},{3,27},{4,28},{5,29},{6,30},{7,31},{8,16},{9,... | collective-permute-start | bytes 737288 | tf_op jit(solution)/shard_map/ppermute | solution.py:439
  12.7 20.0 %collective-permute-start.3 = (f32[2,24,1280]{2,1,0:T(8,128)S(1)}, f32[2,24,1280]{2,1,0:T(8,128)S(1)}, u32[]{:S(2)}, u32[]{:S(2)}) collective-permute-start(f32[2,24,1280]{2,1,0:T(8,128)S(1)} %maximum_select_fusion.12), channel_id=1, source_target_pairs={{0,16},{1,17},{2,18},{3,19},{4,20},{5,21},{6,22},{7,23},{8,24},{9,... | collective-permute-start | bytes 737288 | tf_op jit(solution)/shard_map/ppermute | solution.py:439
  12.7 20.0 %collective-permute-start.2 = (f32[2,24,1280]{2,1,0:T(8,128)S(1)}, f32[2,24,1280]{2,1,0:T(8,128)S(1)}, u32[]{:S(2)}, u32[]{:S(2)}) collective-permute-start(f32[2,24,1280]{2,1,0:T(8,128)S(1)} %maximum_select_fusion.12), channel_id=1, source_target_pairs={{0,8},{1,9},{2,10},{3,11},{4,12},{5,13},{6,14},{7,15},{8,0},{9,1},... | collective-permute-start | bytes 737288 | tf_op jit(solution)/shard_map/ppermute | solution.py:439
  32.8 22.8 %collective-permute-start.5 = (f32[4,2,24,1280]{3,2,1,0:T(8,128)S(1)}, f32[4,2,24,1280]{3,2,1,0:T(8,128)S(1)}, u32[]{:S(2)}, u32[]{:S(2)}) collective-permute-start(f32[4,2,24,1280]{3,2,1,0:T(8,128)S(1)} %pad_maximum_fusion.7.refs_1_.refs_0_), channel_id=1, source_target_pairs={{0,4},{1,5},{2,6},{3,7},{4,0},{5,1},{6,2},{7,3},{8,12},{9,13},{10,... | collective-permute-start | bytes 2949128 | tf_op jit(solution)/shard_map/ppermute | solution.py:439
  35.7 62.8 %collective-permute-start.8 = (f32[4,2,24,1280]{3,2,1,0:T(8,128)}, f32[4,2,24,1280]{3,2,1,0:T(8,128)S(1)}, u32[]{:S(2)}, u32[]{:S(2)}) collective-permute-start(f32[4,2,24,1280]{3,2,1,0:T(8,128)} %copy-done.14), channel_id=1, source_target_pairs={{0,2},{1,3},{2,0},{3,1},{4,6},{5,7},{6,4},{7,5},{8,10},{9,11},{10,... | collective-permute-start | bytes 2949128 | tf_op jit(solution)/shard_map/ppermute | solution.py:439
  58.8 42.2 %collective-permute-start.9 = (f32[4,2,24,1280]{3,2,1,0:T(8,128)}, f32[4,2,24,1280]{3,2,1,0:T(8,128)S(1)}, u32[]{:S(2)}, u32[]{:S(2)}) collective-permute-start(f32[4,2,24,1280]{3,2,1,0:T(8,128)} %after.36), channel_id=1, source_target_pairs={{0,2},{1,3},{2,0},{3,1},{4,6},{5,7},{6,4},{7,5},{8,10},{9,11},{10,... | collective-permute-start | bytes 2949128 | tf_op jit(solution)/shard_map/ppermute | solution.py:439
  59.8 13.5 %collective-permute-start.11 = (f32[24,3840]{1,0:T(8,128)S(1)}, f32[24,3840]{1,0:T(8,128)}, u32[]{:S(2)}, u32[]{:S(2)}) collective-permute-start(f32[24,3840]{1,0:T(8,128)S(1)} %copy-done.58), channel_id=1, source_target_pairs={{0,24},{1,25},{2,26},{3,27},{4,28},{5,29},{6,30},{7,31},{8,16},{9,... | collective-permute-start | bytes 1105928 | tf_op jit(solution)/shard_map/ppermute | solution.py:439
  61.2 30.5 %collective-permute-start.10 = (f32[24,3840]{1,0:T(8,128)S(1)}, f32[24,3840]{1,0:T(8,128)}, u32[]{:S(2)}, u32[]{:S(2)}) collective-permute-start(f32[24,3840]{1,0:T(8,128)S(1)} %copy-done.58), channel_id=1, source_target_pairs={{0,16},{1,17},{2,18},{3,19},{4,20},{5,21},{6,22},{7,23},{8,24},{9,... | collective-permute-start | bytes 1105928 | tf_op jit(solution)/shard_map/ppermute | solution.py:439
  94.1 30.7 %collective-permute-start.14 = (f32[96,768]{1,0:T(8,128)}, f32[96,768]{1,0:T(8,128)}, u32[]{:S(2)}, u32[]{:S(2)}) collective-permute-start(f32[96,768]{1,0:T(8,128)} %after.37), channel_id=1, source_target_pairs={{0,24},{1,25},{2,26},{3,27},{4,28},{5,29},{6,30},{7,31},{8,16},{9,... | collective-permute-start | bytes 884744 | tf_op jit(solution)/shard_map/ppermute | solution.py:439
  96.5 28.3 %collective-permute-start.13 = (f32[96,768]{1,0:T(8,128)}, f32[96,768]{1,0:T(8,128)}, u32[]{:S(2)}, u32[]{:S(2)}) collective-permute-start(f32[96,768]{1,0:T(8,128)} %after.37), channel_id=1, source_target_pairs={{0,16},{1,17},{2,18},{3,19},{4,20},{5,21},{6,22},{7,23},{8,24},{9,... | collective-permute-start | bytes 884744 | tf_op jit(solution)/shard_map/ppermute | solution.py:439
  96.5 28.3 %collective-permute-start.12 = (f32[96,768]{1,0:T(8,128)}, f32[96,768]{1,0:T(8,128)S(1)}, u32[]{:S(2)}, u32[]{:S(2)}) collective-permute-start(f32[96,768]{1,0:T(8,128)} %after.37), channel_id=1, source_target_pairs={{0,8},{1,9},{2,10},{3,11},{4,12},{5,13},{6,14},{7,15},{8,0},{9,1},... | collective-permute-start | bytes 884744 | tf_op jit(solution)/shard_map/ppermute | solution.py:439
  99.5 48.7 %collective-permute-start.16 = (f32[4,24,3840]{2,1,0:T(8,128)}, f32[4,24,3840]{2,1,0:T(8,128)}, u32[]{:S(2)}, u32[]{:S(2)}) collective-permute-start(f32[4,24,3840]{2,1,0:T(8,128)} %after.41.refs_0_), channel_id=1, source_target_pairs={{0,4},{1,5},{2,6},{3,7},{4,0},{5,1},{6,2},{7,3},{8,12},{9,13},{10,... | collective-permute-start | bytes 4423688 | tf_op jit(solution)/shard_map/ppermute | solution.py:439
  102.0 44.3 %collective-permute-start.17 = (f32[4,24,3840]{2,1,0:T(8,128)}, f32[4,24,3840]{2,1,0:T(8,128)S(1)}, u32[]{:S(2)}, u32[]{:S(2)}) collective-permute-start(f32[4,24,3840]{2,1,0:T(8,128)} %after.41.refs_0_), channel_id=1, source_target_pairs={{0,1},{1,0},{2,3},{3,2},{4,5},{5,4},{6,7},{7,6},{8,9},{9,8},{10,11... | collective-permute-start | bytes 4423688 | tf_op jit(solution)/shard_map/ppermute | solution.py:439
  145.8 17.7 %collective-permute-start.15 = (f32[512,384]{1,0:T(8,128)}, f32[512,384]{1,0:T(8,128)}, u32[]{:S(2)}, u32[]{:S(2)}) collective-permute-start(f32[512,384]{1,0:T(8,128)} %get-tuple-element.47), channel_id=1, source_target_pairs={{0,1},{1,0},{2,3},{3,2},{4,5},{5,4},{6,7},{7,6},{8,9},{9,8},{10,11... | collective-permute-start | bytes 2359304 | tf_op jit(solution)/shard_map/ppermute | solution.py:439
  147.7 16.3 %collective-permute-start.18 = (f32[2,24,3840]{2,1,0:T(8,128)}, f32[2,24,3840]{2,1,0:T(8,128)S(1)}, u32[]{:S(2)}, u32[]{:S(2)}) collective-permute-start(f32[2,24,3840]{2,1,0:T(8,128)} %after.42), channel_id=1, source_target_pairs={{0,4},{1,5},{2,6},{3,7},{4,0},{5,1},{6,2},{7,3},{8,12},{9,13},{10,... | collective-permute-start | bytes 2211848 | tf_op jit(solution)/shard_map/ppermute | solution.py:439
  163.5 15.1 %collective-permute-start.19 = (f32[2,24,3840]{2,1,0:T(8,128)}, f32[2,24,3840]{2,1,0:T(8,128)S(1)}, u32[]{:S(2)}, u32[]{:S(2)}) collective-permute-start(f32[2,24,3840]{2,1,0:T(8,128)} %after.43), channel_id=1, source_target_pairs={{0,1},{1,0},{2,3},{3,2},{4,5},{5,4},{6,7},{7,6},{8,9},{9,8},{10,11... | collective-permute-start | bytes 2211848 | tf_op jit(solution)/shard_map/ppermute | solution.py:439
  183.0 36.1 %collective-permute-start.22 = (f32[512,768]{1,0:T(8,128)}, f32[512,768]{1,0:T(8,128)}, u32[]{:S(2)}, u32[]{:S(2)}) collective-permute-start(f32[512,768]{1,0:T(8,128)} %param.16), channel_id=1, source_target_pairs={{0,2},{1,3},{2,0},{3,1},{4,6},{5,7},{6,4},{7,5},{8,10},{9,11},{10,... | collective-permute-start | bytes 4718600 | tf_op jit(solution)/shard_map/ppermute | solution.py:439
  185.8 28.3 %collective-permute-start.23 = (f32[4,96,768]{2,1,0:T(8,128)}, f32[4,96,768]{2,1,0:T(8,128)}, u32[]{:S(2)}, u32[]{:S(2)}) collective-permute-start(f32[4,96,768]{2,1,0:T(8,128)} %after.44), channel_id=1, source_target_pairs={{0,4},{1,5},{2,6},{3,7},{4,0},{5,1},{6,2},{7,3},{8,12},{9,13},{10,... | collective-permute-start | bytes 3538952 | tf_op jit(solution)/shard_map/ppermute | solution.py:439
  186.4 30.2 %collective-permute-start.24 = (f32[4,96,768]{2,1,0:T(8,128)}, f32[4,96,768]{2,1,0:T(8,128)}, u32[]{:S(2)}, u32[]{:S(2)}) collective-permute-start(f32[4,96,768]{2,1,0:T(8,128)} %after.45), channel_id=1, source_target_pairs={{0,1},{1,0},{2,3},{3,2},{4,5},{5,4},{6,7},{7,6},{8,9},{9,8},{10,11... | collective-permute-start | bytes 3538952 | tf_op jit(solution)/shard_map/ppermute | solution.py:439
  197.9 37.9 %collective-permute-start.21 = (f32[512,768]{1,0:T(8,128)}, f32[512,768]{1,0:T(8,128)}, u32[]{:S(2)}, u32[]{:S(2)}) collective-permute-start(f32[512,768]{1,0:T(8,128)} %multiply_add_fusion.5), channel_id=1, source_target_pairs={{0,2},{1,3},{2,0},{3,1},{4,6},{5,7},{6,4},{7,5},{8,10},{9,11},{10,... | collective-permute-start | bytes 4718600 | tf_op jit(solution)/shard_map/ppermute | solution.py:439
  216.1 14.8 %collective-permute-start.26 = (f32[2,96,768]{2,1,0:T(8,128)}, f32[2,96,768]{2,1,0:T(8,128)}, u32[]{:S(2)}, u32[]{:S(2)}) collective-permute-start(f32[2,96,768]{2,1,0:T(8,128)} %after.47), channel_id=1, source_target_pairs={{0,1},{1,0},{2,3},{3,2},{4,5},{5,4},{6,7},{7,6},{8,9},{9,8},{10,11... | collective-permute-start | bytes 1769480 | tf_op jit(solution)/shard_map/ppermute | solution.py:439
  218.6 14.5 %collective-permute-start.25 = (f32[2,96,768]{2,1,0:T(8,128)}, f32[2,96,768]{2,1,0:T(8,128)}, u32[]{:S(2)}, u32[]{:S(2)}) collective-permute-start(f32[2,96,768]{2,1,0:T(8,128)} %after.46), channel_id=1, source_target_pairs={{0,4},{1,5},{2,6},{3,7},{4,0},{5,1},{6,2},{7,3},{8,12},{9,13},{10,... | collective-permute-start | bytes 1769480 | tf_op jit(solution)/shard_map/ppermute | solution.py:439
  278.0 38.9 %collective-permute-start.27 = (f32[512,768]{1,0:T(8,128)}, f32[512,768]{1,0:T(8,128)}, u32[]{:S(2)}, u32[]{:S(2)}) collective-permute-start(f32[512,768]{1,0:T(8,128)} %slice.175), channel_id=1, source_target_pairs={{0,2},{1,3},{2,0},{3,1},{4,6},{5,7},{6,4},{7,5},{8,10},{9,11},{10,... | collective-permute-start | bytes 4718600 | tf_op jit(solution)/shard_map/ppermute | solution.py:439
  279.6 29.1 %collective-permute-start.34 = (f32[2,2,96,768]{3,2,1,0:T(8,128)}, f32[2,2,96,768]{3,2,1,0:T(8,128)}, u32[]{:S(2)}, u32[]{:S(2)}) collective-permute-start(f32[2,2,96,768]{3,2,1,0:T(8,128)} %dynamic-slice_bitcast_fusion.2), channel_id=1, source_target_pairs={{0,1},{1,0},{2,3},{3,2},{4,5},{5,4},{6,7},{7,6},{8,9},{9,8},{10,11... | collective-permute-start | bytes 3538952 | tf_op jit(solution)/shard_map/ppermute | solution.py:439
  282.2 30.7 %collective-permute-start.32 = (f32[2,2,96,768]{3,2,1,0:T(8,128)}, f32[2,2,96,768]{3,2,1,0:T(8,128)}, u32[]{:S(2)}, u32[]{:S(2)}) collective-permute-start(f32[2,2,96,768]{3,2,1,0:T(8,128)} %dynamic-slice_bitcast_fusion.3), channel_id=1, source_target_pairs={{0,4},{1,5},{2,6},{3,7},{4,0},{5,1},{6,2},{7,3},{8,12},{9,13},{10,... | collective-permute-start | bytes 3538952 | tf_op jit(solution)/shard_map/ppermute | solution.py:439
  296.8 44.8 %collective-permute-start.30 = (f32[2,2,2,24,1536]{4,3,2,1,0:T(8,128)}, f32[2,2,2,24,1536]{4,3,2,1,0:T(8,128)}, u32[]{:S(2)}, u32[]{:S(2)}) collective-permute-start(f32[2,2,2,24,1536]{4,3,2,1,0:T(8,128)} %dynamic-slice_bitcast_fusion.5), channel_id=1, source_target_pairs={{0,4},{1,5},{2,6},{3,7},{4,0},{5,1},{6,2},{7,3},{8,12},{9,13},{10,... | collective-permute-start | bytes 3538952 | tf_op jit(solution)/shard_map/ppermute | solution.py:439
  299.5 45.0 %collective-permute-start.31 = (f32[2,2,2,24,1536]{4,3,2,1,0:T(8,128)}, f32[2,2,2,24,1536]{4,3,2,1,0:T(8,128)S(1)}, u32[]{:S(2)}, u32[]{:S(2)}) collective-permute-start(f32[2,2,2,24,1536]{4,3,2,1,0:T(8,128)} %dynamic-slice_bitcast_fusion.4), channel_id=1, source_target_pairs={{0,1},{1,0},{2,3},{3,2},{4,5},{5,4},{6,7},{7,6},{8,9},{9,8},{10,11... | collective-permute-start | bytes 3538952 | tf_op jit(solution)/shard_map/ppermute | solution.py:439
  312.4 44.5 %collective-permute-start.35 = (f32[2,96,768]{2,1,0:T(8,128)}, f32[2,96,768]{2,1,0:T(8,128)}, u32[]{:S(2)}, u32[]{:S(2)}) collective-permute-start(f32[2,96,768]{2,1,0:T(8,128)} %dynamic-slice_bitcast_fusion.10), channel_id=1, source_target_pairs={{0,4},{1,5},{2,6},{3,7},{4,0},{5,1},{6,2},{7,3},{8,12},{9,13},{10,... | collective-permute-start | bytes 1769480 | tf_op jit(solution)/shard_map/ppermute | solution.py:439
  315.4 43.0 %collective-permute-start.33 = (f32[2,96,768]{2,1,0:T(8,128)}, f32[2,96,768]{2,1,0:T(8,128)}, u32[]{:S(2)}, u32[]{:S(2)}) collective-permute-start(f32[2,96,768]{2,1,0:T(8,128)} %dynamic-slice_bitcast_fusion.11), channel_id=1, source_target_pairs={{0,1},{1,0},{2,3},{3,2},{4,5},{5,4},{6,7},{7,6},{8,9},{9,8},{10,11... | collective-permute-start | bytes 1769480 | tf_op jit(solution)/shard_map/ppermute | solution.py:439
  326.1 38.8 %collective-permute-start.29 = (f32[512,384]{1,0:T(8,128)}, f32[512,384]{1,0:T(8,128)}, u32[]{:S(2)}, u32[]{:S(2)}) collective-permute-start(f32[512,384]{1,0:T(8,128)} %get-tuple-element.45.refs_1_), channel_id=1, source_target_pairs={{0,1},{1,0},{2,3},{3,2},{4,5},{5,4},{6,7},{7,6},{8,9},{9,8},{10,11... | collective-permute-start | bytes 2359304 | tf_op jit(solution)/shard_map/ppermute | solution.py:439
  341.6 127.6 %collective-permute-start.28 = (f32[512,768]{1,0:T(8,128)}, f32[512,768]{1,0:T(8,128)}, u32[]{:S(2)}, u32[]{:S(2)}) collective-permute-start(f32[512,768]{1,0:T(8,128)} %slice.177), channel_id=1, source_target_pairs={{0,2},{1,3},{2,0},{3,1},{4,6},{5,7},{6,4},{7,5},{8,10},{9,11},{10,... | collective-permute-start | bytes 4718600 | tf_op jit(solution)/shard_map/ppermute | solution.py:439
  355.5 56.3 %collective-permute-start.49 = (f32[2,2,24,1536]{3,2,1,0:T(8,128)S(1)}, f32[2,2,24,1536]{3,2,1,0:T(8,128)}, u32[]{:S(2)}, u32[]{:S(2)}) collective-permute-start(f32[2,2,24,1536]{3,2,1,0:T(8,128)S(1)} %dynamic-slice_bitcast_fusion.13.refs_0_), channel_id=1, source_target_pairs={{0,1},{1,0},{2,3},{3,2},{4,5},{5,4},{6,7},{7,6},{8,9},{9,8},{10,11... | collective-permute-start | bytes 1769480 | tf_op jit(solution)/shard_map/ppermute | solution.py:439
  356.9 59.0 %collective-permute-start.50 = (f32[2,2,24,1536]{3,2,1,0:T(8,128)S(1)}, f32[2,2,24,1536]{3,2,1,0:T(8,128)}, u32[]{:S(2)}, u32[]{:S(2)}) collective-permute-start(f32[2,2,24,1536]{3,2,1,0:T(8,128)S(1)} %dynamic-slice_bitcast_fusion.12.refs_1_), channel_id=1, source_target_pairs={{0,4},{1,5},{2,6},{3,7},{4,0},{5,1},{6,2},{7,3},{8,12},{9,13},{10,... | collective-permute-start | bytes 1769480 | tf_op jit(solution)/shard_map/ppermute | solution.py:439
  362.3 71.1 %collective-permute-start.57 = (f32[96,768]{1,0:T(8,128)}, f32[96,768]{1,0:T(8,128)}, u32[]{:S(2)}, u32[]{:S(2)}) collective-permute-start(f32[96,768]{1,0:T(8,128)} %get-tuple-element.50), channel_id=1, source_target_pairs={{0,24},{1,25},{2,26},{3,27},{4,28},{5,29},{6,30},{7,31},{8,16},{9,... | collective-permute-start | bytes 884744 | tf_op jit(solution)/shard_map/ppermute | solution.py:439
  364.8 71.0 %collective-permute-start.56 = (f32[96,768]{1,0:T(8,128)}, f32[96,768]{1,0:T(8,128)}, u32[]{:S(2)}, u32[]{:S(2)}) collective-permute-start(f32[96,768]{1,0:T(8,128)} %get-tuple-element.49), channel_id=1, source_target_pairs={{0,16},{1,17},{2,18},{3,19},{4,20},{5,21},{6,22},{7,23},{8,24},{9,... | collective-permute-start | bytes 884744 | tf_op jit(solution)/shard_map/ppermute | solution.py:439
  411.8 24.3 %collective-permute-start.55 = (f32[96,768]{1,0:T(8,128)}, f32[96,768]{1,0:T(8,128)}, u32[]{:S(2)}, u32[]{:S(2)}) collective-permute-start(f32[96,768]{1,0:T(8,128)} %get-tuple-element.48), channel_id=1, source_target_pairs={{0,8},{1,9},{2,10},{3,11},{4,12},{5,13},{6,14},{7,15},{8,0},{9,1},... | collective-permute-start | bytes 884744 | tf_op jit(solution)/shard_map/ppermute | solution.py:439
  415.8 25.4 %collective-permute-start.36 = (f32[4,2,2,24,1152]{4,3,2,1,0:T(8,128)}, f32[4,2,2,24,1152]{4,3,2,1,0:T(8,128)}, u32[]{:S(2)}, u32[]{:S(2)}) collective-permute-start(f32[4,2,2,24,1152]{4,3,2,1,0:T(8,128)} %dynamic-slice_bitcast_fusion.refs_1_), channel_id=1, source_target_pairs={{0,2},{1,3},{2,0},{3,1},{4,6},{5,7},{6,4},{7,5},{8,10},{9,11},{10,... | collective-permute-start | bytes 5308424 | tf_op jit(solution)/shard_map/ppermute | solution.py:439
  433.4 13.9 %collective-permute-start.53 = (f32[2,24,1536]{2,1,0:T(8,128)S(1)}, f32[2,24,1536]{2,1,0:T(8,128)S(1)}, u32[]{:S(2)}, u32[]{:S(2)}) collective-permute-start(f32[2,24,1536]{2,1,0:T(8,128)S(1)} %get-tuple-element.53), channel_id=1, source_target_pairs={{0,24},{1,25},{2,26},{3,27},{4,28},{5,29},{6,30},{7,31},{8,16},{9,... | collective-permute-start | bytes 884744 | tf_op jit(solution)/shard_map/ppermute | solution.py:439
  435.8 26.7 %collective-permute-start.52 = (f32[2,24,1536]{2,1,0:T(8,128)}, f32[2,24,1536]{2,1,0:T(8,128)}, u32[]{:S(2)}, u32[]{:S(2)}) collective-permute-start(f32[2,24,1536]{2,1,0:T(8,128)} %get-tuple-element.52), channel_id=1, source_target_pairs={{0,16},{1,17},{2,18},{3,19},{4,20},{5,21},{6,22},{7,23},{8,24},{9,... | collective-permute-start | bytes 884744 | tf_op jit(solution)/shard_map/ppermute | solution.py:439
  436.1 26.4 %collective-permute-start.51 = (f32[2,24,1536]{2,1,0:T(8,128)}, f32[2,24,1536]{2,1,0:T(8,128)}, u32[]{:S(2)}, u32[]{:S(2)}) collective-permute-start(f32[2,24,1536]{2,1,0:T(8,128)} %get-tuple-element.51), channel_id=1, source_target_pairs={{0,8},{1,9},{2,10},{3,11},{4,12},{5,13},{6,14},{7,15},{8,0},{9,1},... | collective-permute-start | bytes 884744 | tf_op jit(solution)/shard_map/ppermute | solution.py:439
  443.1 21.4 %collective-permute-start.38 = (f32[4,2,24,1152]{3,2,1,0:T(8,128)S(1)}, f32[4,2,24,1152]{3,2,1,0:T(8,128)}, u32[]{:S(2)}, u32[]{:S(2)}) collective-permute-start(f32[4,2,24,1152]{3,2,1,0:T(8,128)S(1)} %dynamic-slice_bitcast_fusion.6.refs_1_), channel_id=1, source_target_pairs={{0,4},{1,5},{2,6},{3,7},{4,0},{5,1},{6,2},{7,3},{8,12},{9,13},{10,... | collective-permute-start | bytes 2654216 | tf_op jit(solution)/shard_map/ppermute | solution.py:439
  447.3 64.5 %collective-permute-start.37 = (f32[512,768]{1,0:T(8,128)}, f32[512,768]{1,0:T(8,128)}, u32[]{:S(2)}, u32[]{:S(2)}) collective-permute-start(f32[512,768]{1,0:T(8,128)} %after.56), channel_id=1, source_target_pairs={{0,1},{1,0},{2,3},{3,2},{4,5},{5,4},{6,7},{7,6},{8,9},{9,8},{10,11... | collective-permute-start | bytes 4718600 | tf_op jit(solution)/shard_map/ppermute | solution.py:439
  462.6 26.6 %collective-permute-start.43 = (f32[4,2,2,24,896]{4,3,2,1,0:T(8,128)}, f32[4,2,2,24,896]{4,3,2,1,0:T(8,128)}, u32[]{:S(2)}, u32[]{:S(2)}) collective-permute-start(f32[4,2,2,24,896]{4,3,2,1,0:T(8,128)} %after.58), channel_id=1, source_target_pairs={{0,2},{1,3},{2,0},{3,1},{4,6},{5,7},{6,4},{7,5},{8,10},{9,11},{10,... | collective-permute-start | bytes 4128776 | tf_op jit(solution)/shard_map/ppermute | solution.py:439
  469.2 18.8 %collective-permute-start.40 = (f32[2,24,1152]{2,1,0:T(8,128)}, f32[2,24,1152]{2,1,0:T(8,128)}, u32[]{:S(2)}, u32[]{:S(2)}) collective-permute-start(f32[2,24,1152]{2,1,0:T(8,128)} %get-tuple-element.56), channel_id=1, source_target_pairs={{0,16},{1,17},{2,18},{3,19},{4,20},{5,21},{6,22},{7,23},{8,24},{9,... | collective-permute-start | bytes 663560 | tf_op jit(solution)/shard_map/ppermute | solution.py:439
  469.2 18.8 %collective-permute-start.39 = (f32[2,24,1152]{2,1,0:T(8,128)}, f32[2,24,1152]{2,1,0:T(8,128)}, u32[]{:S(2)}, u32[]{:S(2)}) collective-permute-start(f32[2,24,1152]{2,1,0:T(8,128)} %get-tuple-element.54), channel_id=1, source_target_pairs={{0,8},{1,9},{2,10},{3,11},{4,12},{5,13},{6,14},{7,15},{8,0},{9,1},... | collective-permute-start | bytes 663560 | tf_op jit(solution)/shard_map/ppermute | solution.py:439
  492.7 23.0 %collective-permute-start.44 = (f32[4,2,24,896]{3,2,1,0:T(8,128)}, f32[4,2,24,896]{3,2,1,0:T(8,128)}, u32[]{:S(2)}, u32[]{:S(2)}) collective-permute-start(f32[4,2,24,896]{3,2,1,0:T(8,128)} %dynamic-slice_bitcast_fusion.9), channel_id=1, source_target_pairs={{0,1},{1,0},{2,3},{3,2},{4,5},{5,4},{6,7},{7,6},{8,9},{9,8},{10,11... | collective-permute-start | bytes 2064392 | tf_op jit(solution)/shard_map/ppermute | solution.py:439
  493.6 17.2 %collective-permute-start.42 = (f32[24,1152]{1,0:T(8,128)S(1)}, f32[24,1152]{1,0:T(8,128)S(1)}, u32[]{:S(2)}, u32[]{:S(2)}) collective-permute-start(f32[24,1152]{1,0:T(8,128)S(1)} %get-tuple-element.64), channel_id=1, source_target_pairs={{0,1},{1,0},{2,3},{3,2},{4,5},{5,4},{6,7},{7,6},{8,9},{9,8},{10,11... | collective-permute-start | bytes 331784 | tf_op jit(solution)/shard_map/ppermute | solution.py:439
  (121 other events, 653.4 us)

commit v3 on v2

--- a/solution.py
+++ b/solution.py
@@ -331,7 +331,7 @@
         lse_ref[start:stop]=jnp.where(lane<HEAD_DIM,lses[0],lses[1])
 
 def attend_back_kernel(len_ref,qkv_ref,do_ref,out_ref,lse_ref,*refs):
-    grad_ref=refs[-1]
+    grad_ref,sum_ref=refs[-2:]
     rows=qkv_ref.shape[0]
     seq_len=len_ref[0]
     lane=lax.broadcasted_iota(jnp.int32,(1,PAIR),1)
@@ -378,6 +378,7 @@
         grad_ref[start:stop,PAIR:2*PAIR]=jnp.where(lane<HEAD_DIM,k_grads[0],k_grads[1])
         grad_ref[start:stop,2*PAIR:]=jnp.where(lane<HEAD_DIM,v_grads[0],v_grads[1])
         grad_ref[start:stop,:PAIR]=(dq[0][start//TILE]+dq[1][start//TILE])*scale
+    sum_ref[...]=jnp.broadcast_to(jnp.sum(grad_ref[...],axis=0,keepdims=True),sum_ref.shape)
 
 def attend(seq_len,qkv,*earlier):
     rows,cols=qkv.shape
@@ -404,8 +405,8 @@
         grid=(pairs,),
         in_specs=[pl.BlockSpec(memory_space=pltpu.SMEM),block(3*PAIR),block(PAIR),block(PAIR),block(PAIR)]
         +[pl.BlockSpec(memory_space=pl.ANY)]*len(earlier),
-        out_specs=block(3*PAIR),
-        out_shape=jax.ShapeDtypeStruct((rows,cols),f32),
+        out_specs=[block(3*PAIR),pl.BlockSpec((8,3*PAIR),lambda j:(0,j))],
+        out_shape=[jax.ShapeDtypeStruct((rows,cols),f32),jax.ShapeDtypeStruct((8,cols),f32)],
         compiler_params=pltpu.CompilerParams(vmem_limit_bytes=48*2**20),
         cost_estimate=pl.CostEstimate(flops=0,bytes_accessed=0,transcendentals=0),
         name="attend_back",
@@ -413,6 +414,7 @@
 
 
 COLUMNS = 4
+CUT = 3
 
 
 def table(move):
@@ -504,7 +506,7 @@
         yield 0, k, k, 0, 0
         yield 1, k, k, 1, 0
         yield 2, k, k, 0, 1
-        yield 3 + k // 2, k % 2, k, 1, 1
+        yield 3 + k // CUT, k % CUT, k, 1, 1
 
 
 def gather_column(shard):
@@ -513,13 +515,6 @@
 
 def gather_sides(own):
     return swap(own, over_x), swap(own, over_y)
-
-
-def gather_corners(beside_x, beside_y, before_x, before_y):
-    return (
-        swap(after(beside_y[:2], *before_x), over_x),
-        swap(after(beside_x[2:], *before_y), over_y),
-    )
 
 
 def by_core(own, other, core, axis):
@@ -528,32 +523,161 @@
     )
 
 
-def plane_sent(chip, x, y, y_axis):
-    return pick(chip[:2], 1 - x, 1), pick(chip[2:], 1 - y, y_axis)
-
-
-def over_plane(chip, sent, x, y, y_axis, earlier):
-    low = pick(chip[:2], x, 1) + after(swap(sent[0], over_x), earlier)
-    high = pick(chip[2:], y, y_axis) + after(swap(sent[1], over_y), earlier)
-    return low, high
-
-
-def corner_sent(low, high, x, y, y_axis):
-    return pick(low, 1 - y, y_axis - 1), pick(high, 1 - x, 1)
-
-
-def over_corner(low, high, sent, x, y, y_axis, earlier):
-    from_y = after(swap(sent[0], over_y), earlier)
-    from_x = after(swap(sent[1], over_x), earlier)
-    return jnp.concatenate([pick(low, y, y_axis - 1) + from_y, pick(high, x, 1) + from_x])
-
-
-def sum_column(column, z, *earlier):
-    total = pick(column, z, 0)
-    for k in range(1, COLUMNS):
-        arrived = swap(pick(column, z ^ k, 0), over_z[k])
-        total = total + (after(arrived, *earlier) if earlier else arrived)
-    return total
+def local_call(kernel, name, where, arrays, earlier, shapes, scratch=()):
+    whole = pl.BlockSpec(memory_space=pltpu.VMEM)
+    anywhere = pl.BlockSpec(memory_space=pl.ANY)
+    count = len(arrays)
+
+    def call(place_ref, *refs):
+        place = [place_ref[i] for i in range(4)]
+        kernel(place, *refs[:count], *refs[count + len(earlier) :])
+
+    return pl.pallas_call(
+        call,
+        in_specs=[pl.BlockSpec(memory_space=pltpu.SMEM)]
+        + [whole] * count
+        + [anywhere] * len(earlier),
+        out_specs=[whole] * len(shapes),
+        out_shape=[jax.ShapeDtypeStruct(shape, f32) for shape in shapes],
+        scratch_shapes=[pltpu.VMEM(shape, f32) for shape in scratch],
+        compiler_params=pltpu.CompilerParams(vmem_limit_bytes=30 * 2**20),
+        cost_estimate=pl.CostEstimate(flops=0, bytes_accessed=0, transcendentals=0),
+        name=name,
+    )(where, *arrays, *earlier)
+
+
+def lanes_of_up(part):
+    return slice(D + part * 2 * D, D + (part + 1) * 2 * D)
+
+
+def put_block(chip, place, target, at, z, x, y, *added):
+    def total(value, lanes):
+        for ref, index in added:
+            value = value + (ref[index] if lanes is None else ref[index + (slice(None), lanes)])
+        return value
+
+    if len(chip) == 1:
+        target[at] = total(chip[0][z, x, y], None)
+        return
+    up, out, arrived = chip
+    rows = (slice(None),)
+    target[at + rows + (slice(0, D),)] = total(
+        out[z, x, place[2], y] + arrived[z, x, y], slice(0, D)
+    )
+    for c in range(2):
+        target[at + rows + (lanes_of_up(c),)] = total(up[z, x, c, y], lanes_of_up(c))
+
+
+def plane_first(where, chip, block, cut, earlier=()):
+    def kernel(place, *refs):
+        chip_refs, (to_x, to_y) = refs[:-2], refs[-2:]
+        z, x, core, y = place
+        for other in range(2):
+            for row in range(cut):
+                put_block(chip_refs, place, to_x, (row, other), row, 1 - x, other)
+            for row in range(cut, COLUMNS):
+                put_block(chip_refs, place, to_y, (row - cut, other), row, other, 1 - y)
+
+    shapes = [(cut, 2) + block, (COLUMNS - cut, 2) + block]
+    return local_call(kernel, "plane_first", where, chip, earlier, shapes)
+
+
+def plane_second(where, chip, block, from_x, from_y, cut, earlier=()):
+    def kernel(place, *refs):
+        chip_refs = refs[:-5]
+        from_x, from_y, kept, to_y, to_x = refs[-5:]
+        z, x, core, y = place
+        for row in range(cut):
+            put_block(chip_refs, place, to_y, (row,), row, x, 1 - y, (from_x, (row, 1 - y)))
+            put_block(chip_refs, place, kept, (row,), row, x, y, (from_x, (row, y)))
+        for row in range(cut, COLUMNS):
+            low = row - cut
+            put_block(chip_refs, place, to_x, (low,), row, 1 - x, y, (from_y, (low, 1 - x)))
+            put_block(chip_refs, place, kept, (row,), row, x, y, (from_y, (low, x)))
+
+    return local_call(
+        kernel,
+        "plane_second",
+        where,
+        list(chip) + [from_x, from_y],
+        earlier,
+        [(COLUMNS,) + block, (cut,) + block, (COLUMNS - cut,) + block],
+    )
+
+
+def column_first(where, block, kept, from_y, from_x, cut, earlier=()):
+    def kernel(place, kept, from_y, from_x, *refs):
+        z, outs, column = place[0], refs[:-1], refs[-1]
+        for row in range(cut):
+            column[row] = kept[row] + from_y[row]
+        for row in range(cut, COLUMNS):
+            column[row] = kept[row] + from_x[row - cut]
+        for k in range(COLUMNS):
+            outs[k % 2][k // 2] = column[z ^ k]
+
+    return local_call(
+        kernel,
+        "column_first",
+        where,
+        [kept, from_y, from_x],
+        earlier,
+        [(2,) + block] * 2,
+        [(COLUMNS,) + block],
+    )
+
+
+def column_second(where, pair, arrived, earlier=()):
+    def kernel(place, pair, arrived, own, sent):
+        own[...] = pair[0] + arrived[0]
+        sent[...] = pair[1] + arrived[1]
+
+    block = pair.shape[1:]
+    return local_call(
+        kernel, "column_second", where, [pair, arrived], earlier, [block] * 2
+    )
+
+
+def sum_after(where, own, arrived, earlier):
+    def kernel(place, own, arrived, out):
+        out[...] = own[...] + arrived[...]
+
+    return local_call(kernel, "sum_after", where, [own, arrived], earlier, [own.shape])[0]
+
+
+def zero_after(where, *earlier):
+    def kernel(place, zero):
+        zero[...] = jnp.zeros_like(zero)
+
+    zero, = local_call(kernel, "zero_after", where, [], earlier, [(8, PAIR)])
+    return zero[0, 0]
+
+
+def copy_after(where, values, earlier):
+    def kernel(place, values, out):
+        out[...] = values[...]
+
+    return local_call(kernel, "copy_after", where, [values], earlier, [values.shape])[0]
+
+
+def gather_pair(where, shard, earlier=()):
+    def kernel(place, shard, beside, out):
+        out[0] = shard[...]
+        out[1] = beside[...]
+
+    return local_call(
+        kernel, "pair", where, [shard, swap(shard, over_z[2])], earlier, [(2,) + shard.shape]
+    )[0]
+
+
+def gather_pairs(where, pair, earlier):
+    beside = swap(pair, over_z[1])
+
+    def kernel(place, pair, beside, out):
+        for k in range(COLUMNS):
+            out[k] = (pair, beside)[k % 2][k // 2]
+
+    shapes = [(COLUMNS,) + pair.shape[1:]]
+    return local_call(kernel, "pairs", where, [pair, beside], earlier, shapes)[0]
 
 
 def normalise(values):
@@ -612,7 +736,7 @@
     sent = swap(jnp.concatenate([pick(by_head, 1 - y, 0), small], axis=1), over_y)
     kept = jnp.concatenate([pick(by_head, y, 0), small], axis=1)
     block = jnp.where(y == 0, jnp.stack([kept, sent]), jnp.stack([sent, kept]))
-    column = gather_column(block)
+    column = gather_column(after(block, normed_own))
     beside = swap(column, over_x)
 
     by_unit = up_weight.reshape(shard, 2 * COLUMNS, 2, 8 * shard).transpose(2, 0, 1, 3)
@@ -621,15 +745,13 @@
     arrived_up = swap(pick(by_unit, 1 - core, 0), over_core)
     both_up = by_core(kept_up, arrived_up, core, 1).reshape(shard, 2 * hidden)
     shard_a = after(jnp.concatenate([out_weight, both_up], axis=1), column)
-    arrived_a = [swap(shard_a, over_z[k]) for k in range(1, COLUMNS)]
-    own_a = jnp.stack([shard_a] + arrived_a)
-    beside = after(beside, arrived_a[0])
-    arrived_b = [swap(after(down_weight, own_a), over_z[k]) for k in range(1, COLUMNS)]
-    own_a = after(own_a, beside)
+    pair_a = gather_pair(where, shard_a)
+    shard_b = after(down_weight, pair_a)
+    own_a = gather_pairs(where, pair_a, [beside])
     sides_a = gather_sides(own_a)
 
     pieces = [column, beside]
-    pieces += [swap(column, over_core), swap(after(beside, other_normed), over_core)]
+    pieces += [swap(column, over_core), swap(copy_after(where, beside, [other_normed, own_a]), over_core)]
     copies = []
     for k in range(COLUMNS):
         for piece in range(4):
@@ -642,6 +764,7 @@
     w_qkv, lines = assemble(
         where, pieces, [grid + (shard, wide), grid + (8, PAIR)], copies
     )
+    pair_b = gather_pair(where, shard_b, [w_qkv])
     w_qkv = w_qkv.reshape(D, wide)
     lines = lines.reshape(32, 8, PAIR)
     b_qv = lines[:, 0, : 2 * shard].reshape(2 * D)
@@ -659,7 +782,8 @@
     bias = pick(b_qv.reshape(2, 2, pairs, PAIR), y, 1)
     qkv_bias = jnp.stack([bias[0], jnp.zeros_like(bias[0]), bias[1]], axis=1).reshape(wide)
     projected = matmul(normed_out_one, w_qkv) + qkv_bias
-    own_b = jnp.stack([down_weight] + [after(piece, projected) for piece in arrived_b])
+    own_b = gather_pairs(where, pair_b, [projected])
+    sides_b = gather_sides(own_b)
     head_out, log_sum = attend(seq_lengths, projected, own_b)
     there = swap(rows_of(head_out, 1 - y), over_y)
     here = rows_of(head_out, y)
@@ -667,9 +791,26 @@
         y == 0, jnp.concatenate([here, there], 1), jnp.concatenate([there, here], 1)
     )
 
-    corners_a = gather_corners(*sides_a, [head_out], [there])
-    sides_b = swap(after(own_b, head_out), over_x), swap(after(own_b, there), over_y)
-    corners_b = gather_corners(*sides_b, corners_a, corners_a)
+
+    def corner_first(place, beside_y, out):
+        out[...] = beside_y[:CUT]
+
+    def corner_rest(place, x_of_a, x_of_b, y_of_b, y_corner_a, x_corner_b, y_corner_b):
+        y_corner_a[...] = x_of_a[CUT:]
+        x_corner_b[...] = y_of_b[:CUT]
+        y_corner_b[...] = x_of_b[CUT:]
+
+    low, high = (CUT,), (COLUMNS - CUT,)
+    block_a, block_b = own_a.shape[1:], own_b.shape[1:]
+    x_corner_a, = local_call(
+        corner_first, "corner_first", where, [sides_a[1]], [head_out], [low + block_a]
+    )
+    y_corner_a, x_corner_b, y_corner_b = local_call(
+        corner_rest, "corner_rest", where, [sides_a[0], *sides_b], [there],
+        [high + block_a, low + block_b, high + block_b],
+    )
+    corners_a = swap(x_corner_a, over_x), swap(y_corner_a, over_y)
+    corners_b = swap(x_corner_b, over_x), swap(y_corner_b, over_y)
     every = slice(None)
     copies = []
     for piece, at, dz, dx, dy in plane_pieces():
@@ -713,33 +854,156 @@
         d_part[:rows] + swap(d_part[rows:], over_core), normed_two, inv_two, gain_two
     )
     d_middle = cotangent + d_norm_two
+    d_out_b = jnp.sum(d_middle, axis=0)
     d_att = matmul_nt(d_middle, w_out)
     d_heads = d_att.reshape(rows, 2, half)
     sent = pick(d_heads, 1 - y, 1)
-    d_out = both_rows(pick(d_heads, y, 1), swap(sent, over_y))
-    down_part = matmul(gelu_forward(raw_act + after(b_up, sent)), w_down)
+    d_up_b = d_up_b.reshape(2 * COLUMNS, 8 * shard)
+    d_up_b = by_core(d_up_b, jnp.zeros_like(d_up_b), core, 1)
+
+    def lanes(*vectors):
+        line = jnp.concatenate([v.reshape(32, -1) for v in vectors], axis=1)
+        return jnp.pad(line, ((0, 0), (0, PAIR - line.shape[1])))
+
+    small = jnp.stack(
+        [lanes(d_out_b, d_gain_two, d_shift_two), lanes(d_up_b, d_down_b)],
+        axis=1,
+    )
+    grid = (COLUMNS, 2, 2, 2)
+    scales = jnp.stack([gain_one, shift_one], axis=1).reshape(grid + (shard, 2))
+    small = jnp.pad(small, ((0, 0), (0, 6), (0, 0)))
+    chip_a = matmul_tn(both_normed + zero_after(where, sent, small, scales), d_pre).reshape(COLUMNS, 2, 2, 2, shard, hidden)
+    def join_rows(place, own, arrived, out):
+        y = place[3]
+        out[pl.ds(y * rows, rows)] = own[...]
+        out[pl.ds((1 - y) * rows, rows)] = arrived[...]
+
+    d_out, = local_call(
+        join_rows, "join_rows", where, [pick(d_heads, y, 1), swap(sent, over_y)],
+        [chip_a], [(2 * rows, half)],
+    )
+    block_b = (4 * shard, D)
+    block_a = (shard, 5 * D)
+    to_x, to_y = plane_first(where, [chip_b], block_b, CUT)
+    side_b = swap(to_x, over_x), swap(to_y, over_y)
+    d_out_w = matmul_tn(attended, d_middle).reshape(COLUMNS, 2, 2, 2, shard, D)
+    chip_a = [chip_a, d_out_w, swap(pick(d_out_w, 1 - core, 2), over_core)]
+    kept_b, *sent_b = plane_second(where, [chip_b], block_b, *side_b, CUT, [d_out])
+    first_a = plane_first(where, chip_a, block_a, 2, sent_b)
+    side_a = swap(first_a[0], over_x), swap(first_a[1], over_y)
+
+    d_proj, d_bias_all = attend_back(
+        seq_lengths, projected, d_out, head_out, log_sum, *first_a, *sent_b
+    )
+    corner = swap(sent_b[0], over_y), swap(sent_b[1], over_x)
+    pair_b, sent_b = column_first(where, block_b, kept_b, *corner, CUT, [d_proj])
+    kept_a, *sent_a = plane_second(where, chip_a, block_a, *side_a, 2, [sent_b])
+    corner_a = swap(sent_a[0], over_y), swap(sent_a[1], over_x)
+
+    moved = matmul_tn(normed_one + zero_after(where, *sent_a), d_proj)
+    last_lane = wide + PAIR - 1
+
+    def finish(place, moved, weight, scales, total, small, kept, sent):
+        core = place[2]
+        y = place[3]
+        total = total[:1]
+        for z in range(COLUMNS):
+            for xy in range(4):
+                for target, c in ((kept, core), (sent, 1 - core)):
+                    at = (z, xy // 2, c, xy % 2)
+                    to = (z, xy // 2, xy % 2)
+                    rows_of_grad, rows_of_weight = moved[at], weight[at]
+                    scale = scales[at]
+                    target[to + (slice(None), slice(0, wide))] = (
+                        rows_of_grad * scale[:, 0:1] + scale[:, 1:2] * total
+                    )
+                    gain_grad = jnp.sum(rows_of_grad * rows_of_weight, axis=1, keepdims=True)
+                    shift_grad = jnp.sum(total * rows_of_weight, axis=1, keepdims=True)
+                    lane = lax.broadcasted_iota(jnp.int32, (shard, PAIR), 1)
+                    side = jnp.where(lane == PAIR - 1, gain_grad, 0.0)
+                    side = jnp.where(lane == PAIR - 2, shift_grad, side)
+                    lines = jnp.concatenate(
+                        [small[at], jnp.zeros((shard - 8, PAIR), f32)], axis=0
+                    )
+                    target[to + (slice(None), slice(wide, wide + PAIR))] = side + lines
+
+        line = slice(wide, wide + 2 * shard)
+        for part, z in ((0, y), (2, 2 + y)):
+            column = jnp.concatenate(
+                [total[:, (3 * p + part) * PAIR : (3 * p + part + 1) * PAIR] for p in range(pairs)],
+                axis=1,
+            )
+            for xy in range(4):
+                x, side = xy // 2, xy % 2
+                low = column[:, 2 * shard * (4 * x + side) :][:, : 2 * shard]
+                high = column[:, 2 * shard * (4 * x + 2 + side) :][:, : 2 * shard]
+                kept[z, x, side, 2:3, line] = jnp.where(core == 0, low, high)
+                sent[z, x, side, 2:3, line] = jnp.where(core == 0, high, low)
+
+    block = (shard, wide + PAIR)
+    kept, first = local_call(
+        finish,
+        "finish",
+        where,
+        [
+            moved.reshape(grid + (shard, wide)),
+            w_qkv.reshape(grid + (shard, wide)),
+            scales,
+            d_bias_all,
+            small.reshape(grid + (8, PAIR)),
+        ],
+        (),
+        [(COLUMNS, 2, 2) + block] * 2,
+    )
+
+    def chip_sum(place, kept, arrived, mine, sent):
+        x = place[1]
+        for z in range(COLUMNS):
+            mine[z] = kept[z, x] + arrived[z, x]
+            sent[z] = kept[z, 1 - x] + arrived[z, 1 - x]
+
+    kept, second = local_call(
+        chip_sum,
+        "chip_sum",
+        where,
+        [kept, swap(first, over_core)],
+        (),
+        [(COLUMNS, 2) + block] * 2,
+    )
+    own_b, sent_b = column_second(where, pair_b, swap(sent_b, over_z[1]), [second])
+    pair_a, sent_a = column_first(where, block_a, kept_a, *corner_a, 2, [sent_b])
+    d_norm = matmul_nt(d_proj + zero_after(where, sent_a), w_qkv)
+    d_norm_sent = rows_of(d_norm, 1 - y)
+
+    def line_sum(place, kept, arrived, pair, sent):
+        z = place[0]
+        for k in range(COLUMNS):
+            (pair, sent)[k % 2][k // 2] = kept[z ^ k] + arrived[z ^ k]
+
+    pair_qkv, sent_qkv = local_call(
+        line_sum, "line_sum", where, [kept, swap(second, over_x)], [d_norm],
+        [(2, 2) + block] * 2,
+    )
+    own_a, sent_a = column_second(where, pair_a, swap(sent_a, over_z[1]), [sent_qkv])
+    down_part = matmul(gelu_forward(raw_act + (b_up + zero_after(where, sent_a))), w_down)
     layer_output = middle + down_part[:rows] + swap(down_part[rows:], over_core) + b_down
-    chip_a = matmul_tn(both_normed, d_pre).reshape(COLUMNS, 2, 2, 2, shard, hidden)
-    low_b, high_b = over_plane(chip_b, plane_sent(chip_b, x, y, 2), x, y, 2, chip_a)
-    sent_b = corner_sent(low_b, high_b, x, y, 2)
-    column_b = over_corner(low_b, high_b, sent_b, x, y, 2, sent)
-    low_a, high_a = over_plane(chip_a, plane_sent(chip_a, x, y, 3), x, y, 3, sent)
-    sent_a = corner_sent(low_a, high_a, x, y, 3)
-    d_out_b = jnp.sum(d_middle, axis=0)
-    d_out_w = matmul_tn(attended, d_middle).reshape(COLUMNS, 2, 2, 2, shard, D)
-
-    d_proj = attend_back(
-        seq_lengths, projected, d_out, head_out, log_sum, *sent_a, column_b
-    )
-    d_qkv_w = matmul_tn(normed_out_one, d_proj)
-    grid = d_qkv_w.reshape(COLUMNS, 2, 2, 2, shard, wide)
-    first = pick(grid, 1 - core, 2)
-    grid = pick(grid, core, 2) + swap(first, over_core)
-    sent = pick(grid, 1 - x, 1)
-    grid = pick(grid, x, 1) + swap(sent, over_x)
-    column_a = over_corner(low_a, high_a, sent_a, x, y, 3, first)
-    down_grad = sum_column(column_b, z, first)
-    up_parts = sum_column(column_a, z, sent)
+    own_qkv, sent_qkv = column_second(
+        where, pair_qkv, swap(sent_qkv, over_z[1]), [down_part]
+    )
+    down_grad = sum_after(where, own_b, swap(sent_b, over_z[2]), [sent_qkv])
+    grad_a = sum_after(where, own_a, swap(sent_a, over_z[2]), [sent_qkv])
+
+    def last_sum(place, own, arrived, here, sent):
+        y = place[3]
+        here[...] = own[y] + arrived[y]
+        sent[...] = own[1 - y] + arrived[1 - y]
+
+    here, third = local_call(
+        last_sum, "last_sum", where, [own_qkv, swap(sent_qkv, over_z[2])], (), [block] * 2
+    )
+    there = swap(third, over_y)
+    out_grad = grad_a[:, :D]
+    up_parts = jnp.stack([grad_a[:, lanes_of_up(0)], grad_a[:, lanes_of_up(1)]])
     arrived = swap(pick(up_parts, 1 - core, 0), over_core)
     up_grad = by_core(
         pick(up_parts, core, 0).reshape(shard, 2 * COLUMNS, 8 * shard),
@@ -748,68 +1012,42 @@
         2,
     ).reshape(shard, 4 * D)
 
-    column_qkv = grid
-    grid = sum_column(column_qkv, z)
-    here = pick(grid, y, 0)
-    there = swap(pick(grid, 1 - y, 0), over_y)
-    qkv_grad = jnp.where(y == 0, jnp.stack([here, there]), jnp.stack([there, here]))
-    qkv_grad = qkv_grad.reshape(2, shard, pairs, 3, PAIR).transpose(1, 3, 0, 2, 4)
-
-    d_norm = matmul_nt(d_proj, after(w_qkv, first))
-    d_gain_one = jnp.sum(d_norm * normed_one, axis=0)
-    d_shift_one = jnp.sum(d_norm, axis=0)
-    d_norm_other = swap(after(rows_of(d_norm, 1 - y), sent), over_y)
-    d_norm_own = rows_of(d_norm, y) + after(d_norm_other, here)
+
+    def place_qkv(place, here, there, grad, side):
+        y = place[3]
+        side[...] = here[:, wide:] + there[:, wide:]
+        for part in range(3):
+            for p in range(pairs):
+                source = slice((3 * p + part) * PAIR, (3 * p + part + 1) * PAIR)
+                mine, other = here[:, source], there[:, source]
+                target = part * D + p * PAIR
+                grad[:, target : target + PAIR] = jnp.where(y == 0, mine, other)
+                target = target + half
+                grad[:, target : target + PAIR] = jnp.where(y == 0, other, mine)
+
+    qkv_grad, side = local_call(
+        place_qkv, "place_qkv", where, [here, there], [up_grad, down_grad, layer_output], [(shard, 3 * D), (shard, PAIR)]
+    )
+    d_norm_own = rows_of(d_norm, y) + swap(d_norm_sent, over_y)
     d_norm_one, unused, unused = norm_backward(
         d_norm_own, normed_own, inv_one, gain_one
     )
     input_grad = d_middle + d_norm_one
-
-    d_bias = jnp.sum(d_proj, axis=0).reshape(pairs, 3, PAIR)
-    d_bias = jnp.stack([d_bias[:, 0], d_bias[:, 2]]).reshape(2, 1, half)
-    blank = jnp.zeros_like(d_bias)
-    d_qv_b = jnp.where(
-        y == 0, jnp.concatenate([d_bias, blank], 1), jnp.concatenate([blank, d_bias], 1)
-    )
-
-    d_up_b = d_up_b.reshape(2 * COLUMNS, 8 * shard)
-    d_up_b = by_core(d_up_b, jnp.zeros_like(d_up_b), core, 1)
-
-    def lanes(*vectors):
-        line = jnp.concatenate([v.reshape(32, -1) for v in vectors], axis=1)
-        return jnp.pad(line, ((0, 0), (0, PAIR - line.shape[1])))
-
-    lines = jnp.stack(
-        [
-            lanes(d_qv_b, d_out_b, d_gain_one, d_shift_one),
-            lanes(d_up_b, d_down_b),
-            lanes(d_gain_two, d_shift_two),
-        ],
-        axis=1,
-    )
-    small = jnp.pad(lines, ((0, 0), (0, shard - 3), (0, 0)))
-    small = small.reshape(COLUMNS, 2, 2, 2, shard, PAIR)
-    grid = jnp.concatenate([d_out_w, small], axis=-1)
-    grid = pick(grid, core, 2) + swap(after(pick(grid, 1 - core, 2), sent), over_core)
-    grid = pick(grid, y, 2) + after(swap(pick(grid, 1 - y, 2), over_y), column_qkv)
-    grid = pick(grid, x, 1) + swap(pick(grid, 1 - x, 1), over_x)
-    grid = sum_column(grid, z)
-    out_grad, lines = grid[:, :D], grid[:, D:]
     return (
         layer_output,
         input_grad,
-        qkv_grad.reshape(shard, 3 * D),
-        lines[0, : 2 * shard],
+        qkv_grad,
+        side[2, : 2 * shard],
         out_grad,
-        lines[0, 2 * shard : 3 * shard],
-        lines[0, 3 * shard : 4 * shard],
-        lines[0, 4 * shard : 5 * shard],
+        side[0, :shard],
+        side[:, PAIR - 1],
+        side[:, PAIR - 2],
         up_grad,
-        lines[1, : 4 * shard],
+        side[1, : 4 * shard],
         down_grad,
-        lines[1, 4 * shard : 5 * shard],
-        lines[2, :shard],
-        lines[2, shard : 2 * shard],
+        side[1, 4 * shard : 5 * shard],
+        side[0, shard : 2 * shard],
+        side[0, 2 * shard : 3 * shard],
     )
 
 

time: 541 us -> 494 us (0.913)
  Pallas kernels: 54.5 us -> 96.8 us
  other arithmetic: 63.8 us -> 30.9 us
  waiting for transfers between devices: 169 us -> 146 us
  local copies, waits for them, and re-layouts: 80.6 us -> 64.5 us
  starting transfers between devices: 54.8 us -> 43.6 us
    pallas_call x0 -> x28, Pallas kernels: none -> 41.2 us  [local_call(): pl.pallas_call(call, in_specs=[pl.BlockSpec(memory_space=pltpu.SMEM)] + [...]
    add x17 -> x1, other arithmetic: 25.4 us -> 0.65 us  [body_grid(): b_up + zero_after(where, sent_a)]
    ppermute x58 -> x48, waiting for transfers between devices: 169 us -> 146 us  [swap(): return lax.ppermute(values, AXES, pairs)]
    ppermute x58 -> x48, starting transfers between devices: 54.8 us -> 43.6 us  [swap(): return lax.ppermute(values, AXES, pairs)]
    squeeze x18 -> x3, local copies, waits for them, and re-layouts: 13.8 us -> 2.7 us  [pick(): return lax.dynamic_index_in_dim(values, index, axis, keepdims=False)]
    dot_general x4, matrix products: 40.7 us -> 33 us  [matmul(): jnp.dot(left, right, precision=top_prec, preferred_element_type=jnp.float32)]
    unnamed x228 -> x200, local copies, waits for them, and re-layouts: 35 us -> 28.2 us
  transfers between devices with their start and end apart: 58 -> 48, of which waited for: 21 -> 24; matrix products, arithmetic and copies ran while one was open for 33% -> 25% of each run, Pallas kernels for 10% -> 17%
where the time goes in v3:
time: 494 us; the launch traced here: 489 us
  waiting for transfers between devices  146 us (30%)
  matrix products  105 us (21%)
  Pallas kernels  96.8 us (20%)
  local copies, waits for them, and re-layouts  64.5 us (13%)
  starting transfers between devices  43.6 us (9%)
  other arithmetic  30.9 us (6%)
    ppermute x48, waiting for transfers between devices, swap(): return lax.ppermute(values, AXES, pairs)  146 us
    ppermute x48, starting transfers between devices, swap(): return lax.ppermute(values, AXES, pairs)  43.6 us
    pallas_call x28, Pallas kernels, local_call(): pl.pallas_call(call, in_specs=[pl.BlockSpec(memory_space=pltpu.SMEM)] + [...  41.2 us
    dot_general x4, matrix products, matmul_tn(): lax.dot_general(left, right, (((0,), (0,)), ((), ())), precision=top_prec...  37.7 us
    dot_general x4, matrix products, matmul_nt(): lax.dot_general(left, right, (((1,), (1,)), ((), ())), precision=top_prec...  33.9 us
    dot_general x4, matrix products, matmul(): jnp.dot(left, right, precision=top_prec, preferred_element_type=jnp.float32)  33 us
    unnamed x200, local copies, waits for them, and re-layouts  28.2 us
    pallas_call x1, Pallas kernels, attend_back(): pl.pallas_call(attend_back_kernel, grid=(pairs,), in_specs=[pl.BlockSpec(...  27.2 us
  transfers between devices with their start and end apart: 48, of which 24 were waited for; matrix products, arithmetic and copies ran while one was open for 25% of the time, Pallas kernels for 17%

profile of v3, /device:TPU:0, one launch (start us, length us, event | category | flops | bytes accessed | tf_op | source)
XLA Modules:
  0.0 488.8 jit_solution(10026174192847436018)
XLA Ops:
  4.0 3.0 collective-permute-start.1
  12.9 2.6 collective-permute-start.3
  16.9 6.8 %collective-permute-done.2 = f32[2,24,1280]{2,1,0:T(8,128)S(1)} collective-permute-done((f32[2,24,1280]{2,1,0:T(8,128)}, f32[2,24,1280]{2,1,0:T(8,128)S(1)}, u32[]{:S(2)}, u32[]{:S(2)}) %collective-permute-start.2) | collective-permute-done | bytes 245792 | tf_op jit(solution)/shard_map/ppermute | solution.py:441
  23.7 9.8 %collective-permute-done.3 = f32[2,24,1280]{2,1,0:T(8,128)S(1)} collective-permute-done((f32[2,24,1280]{2,1,0:T(8,128)}, f32[2,24,1280]{2,1,0:T(8,128)S(1)}, u32[]{:S(2)}, u32[]{:S(2)}) %collective-permute-start.3) | collective-permute-done | bytes 245792 | tf_op jit(solution)/shard_map/ppermute | solution.py:441
  34.5 5.4 %collective-permute-start.8 = (f32[24,3840]{1,0:T(8,128)}, f32[24,3840]{1,0:T(8,128)S(1)}, u32[]{:S(2)}, u32[]{:S(2)}) collective-permute-start(f32[24,3840]{1,0:T(8,128)} %after.4.refs_0_), channel_id=1, source_target_pairs={{0,16},{1,17},{2,18},{3,19},{4,20},{5,21},{6,22},{7,23},{8,24},{9,... | collective-permute-start | bytes 1105928 | tf_op jit(solution)/shard_map/ppermute | solution.py:441
  41.5 14.1 %collective-permute-done.8.refs_1_ = f32[24,3840]{1,0:T(8,128)S(1)} collective-permute-done((f32[24,3840]{1,0:T(8,128)}, f32[24,3840]{1,0:T(8,128)S(1)}, u32[]{:S(2)}, u32[]{:S(2)}) %collective-permute-start.8) | collective-permute-done | bytes 368672 | tf_op jit(solution)/shard_map/ppermute | solution.py:441
  57.3 5.0 %collective-permute-done.5.refs_2_.refs_0_.refs_1_ = f32[4,2,24,1280]{3,2,1,0:T(8,128)S(1)} collective-permute-done((f32[4,2,24,1280]{3,2,1,0:T(8,128)}, f32[4,2,24,1280]{3,2,1,0:T(8,128)S(1)}, u32[]{:S(2)}, u32[]{:S(2)}) %collective-permute-start.5) | collective-permute-done | bytes 983072 | tf_op jit(solution)/shard_map/ppermute | solution.py:441
  62.3 12.2 %collective-permute-done.9.refs_1_ = f32[2,24,3840]{2,1,0:T(8,128)S(1)} collective-permute-done((f32[2,24,3840]{2,1,0:T(8,128)S(1)}, f32[2,24,3840]{2,1,0:T(8,128)S(1)}, u32[]{:S(2)}, u32[]{:S(2)}) %collective-permute-start.9) | collective-permute-done | bytes 737312 | tf_op jit(solution)/shard_map/ppermute | solution.py:441
  81.0 3.2 assemble.4
  88.7 4.6 collective-permute-done.11.refs_1_
  101.1 10.5 %convolution_add_fusion.refs_2_.qkv_ref = f32[1024,1152]{1,0:T(8,128)S(1)} fusion(f32[768,1152]{1,0:T(8,128)} %bitcast.134, f32[1152]{0:T(1024)} %add.213, f32[512,768]{1,0:T(8,128)} %collective-permute-done.refs_1_, f32[512,768]{1,0:T(8,128)} %subtract_multiply_fusion.1.refs_1_, f32[768]{0:T(1024)S(1)} %add.210, f32[768]{0:T(1024)S(1)} %mul.147, pred[]{:T(512)S(6)} %eq.7), kind=kOutput, calls=%fused_computation.21 | convolution fusion | flops 5440929792 | bytes 11414017 | tf_op jit(solution)/shard_map/dot_general | solution.py:25
  112.2 2.6 pairs.3.refs_0_
  118.4 16.1 %attend.1 = (f32[1024,384]{1,0:T(8,128)S(1)}, f32[1024,384]{1,0:T(8,128)S(1)}) custom-call(s32[1]{0:T(128)S(6)} %copy.110.len_ref, f32[1024,1152]{1,0:T(8,128)} %copy-done, f32[4,96,768]{2,1,0:T(8,128)} %pairs.3.refs_0_), custom_call_target="tpu_custom_call" | custom-call | tf_op jit(solution)/shard_map/attend/pallas_call | solution.py:387
  138.6 21.9 %collective-permute-done.13.refs_3_ = f32[512,384]{1,0:T(8,128)S(1)} collective-permute-done((f32[512,384]{1,0:T(8,128)S(1)}, f32[512,384]{1,0:T(8,128)S(1)}, u32[]{:S(2)}, u32[]{:S(2)}) %collective-permute-start.13) | collective-permute-done | bytes 786464 | tf_op jit(solution)/shard_map/ppermute | solution.py:441
  160.5 2.9 corner_rest.1
  166.1 6.9 %collective-permute-done.19.refs_4_ = f32[1,24,3840]{2,1,0:T(8,128)S(1)} collective-permute-done((f32[1,24,3840]{2,1,0:T(8,128)S(1)}, f32[1,24,3840]{2,1,0:T(8,128)S(1)}, u32[]{:S(2)}, u32[]{:S(2)}) %collective-permute-start.19) | collective-permute-done | bytes 368672 | tf_op jit(solution)/shard_map/ppermute | solution.py:441
  173.0 3.0 assemble.5
  176.8 2.4 collective-permute-done.20
  179.2 2.8 maximum_select_fusion.1
  184.8 2.4 fusion.69
  189.6 2.8 fusion.67
  192.4 2.6 constant_dynamic-update-slice_fusion
  198.9 3.3 assemble.6
  205.3 6.0 %collective-permute-done.23.refs_3_ = f32[3,96,768]{2,1,0:T(8,128)} collective-permute-done((f32[3,96,768]{2,1,0:T(8,128)}, f32[3,96,768]{2,1,0:T(8,128)}, u32[]{:S(2)}, u32[]{:S(2)}) %collective-permute-start.23) | collective-permute-done | bytes 884768 | tf_op jit(solution)/shard_map/ppermute | solution.py:441
  211.3 2.9 assemble.7
  214.2 11.5 %fusion.30 = f32[1024,1536]{1,0:T(8,128)S(1)} fusion(f32[768,1536]{1,0:T(8,128)S(1)} %bitcast.151, f32[512,768]{1,0:T(8,128)} %collective-permute-done.21, f32[512,768]{1,0:T(8,128)} %multiply_add_fusion.2), kind=kOutput, calls=%fused_computation.36 | convolution fusion | flops 7248543744 | bytes 14155776 | tf_op jit(solution)/shard_map/dot_general | solution.py:25
  225.8 13.3 %fusion.70 = (f32[1536]{0:T(1024)}, f32[1024,1536]{1,0:T(8,128)S(1)}) fusion(f32[1024,1536]{1,0:T(8,128)S(1)} %fusion.30, f32[1536]{0:T(1024)S(1)} %reshape.179, f32[1024,768]{1,0:T(8,128)} %constant_dynamic-update-slice_fusion, f32[1536,768]{1,0:T(8,128)S(1)} %bitcast.136), kind=kOutput, calls=%fused_computation.159 | convolution fusion | flops 7265057280 | bytes 20459520 | tf_op jit(solution)/shard_map/dot_general | solution.py:39
  239.1 7.8 %fusion.71 = f32[1024,768]{1,0:T(8,128)S(1)} fusion(f32[1024,1536]{1,0:T(8,128)S(1)} %get-tuple-element.139, f32[768,1536]{1,0:T(8,128)S(1)} %bitcast.152), kind=kOutput, calls=%fused_computation.160 | convolution fusion | flops 7247757312 | bytes 14155776 | tf_op jit(solution)/shard_map/dot_general | solution.py:39
  254.4 11.9 %fusion.12 = f32[1536,768]{1,0:T(8,128)S(1)} fusion(f32[1024,768]{1,0:T(8,128)} %constant_dynamic-update-slice_fusion, f32[1024,1536]{1,0:T(8,128)} %copy-done.90, f32[1536]{0:T(1024)} %copy-done.74), kind=kOutput, calls=%fused_computation.13 | convolution fusion | flops 7255621632 | bytes 14161920 | tf_op jit(solution)/shard_map/dot_general | solution.py:29
  271.9 2.9 multiply_reduce_fusion.1
  274.8 2.7 fusion.66
  281.9 3.4 fusion.34
  291.4 13.1 %fusion.21 = f32[768,1536]{1,0:T(8,128)S(1)} fusion(f32[1024,1536]{1,0:T(8,128)} %copy-done.89, f32[512,768]{1,0:T(8,128)} %collective-permute-done.21, f32[512,768]{1,0:T(8,128)} %multiply_add_fusion.2, f32[]{:T(128)} %bitcast.37), kind=kOutput, calls=%fused_computation.27 | convolution fusion | flops 7249330176 | bytes 14155780 | tf_op jit(solution)/shard_map/dot_general | solution.py:29
  304.5 4.5 collective-permute-done.29.refs_1_
  310.5 2.8 plane_second.2
  319.8 27.2 %attend_back.1 = (f32[1024,1152]{1,0:T(8,128)}, f32[8,1152]{1,0:T(8,128)S(1)}) custom-call(s32[1]{0:T(128)S(6)} %copy.110.len_ref, f32[1024,1152]{1,0:T(8,128)} %copy-done, f32[1024,384]{1,0:T(8,128)S(1)} %copy-done.7, f32[1024,384]{1,0:T(8,128)} %copy-done.5, f32[1024,384]{1,0:T(8,128)} %copy-done.24, f32[2,2,24,3840]{3,2,1,0:T(8,128)} %get-tuple-element.67.refs_0_, ...), custom_call_target="tpu_custom_call" | custom-call | tf_op jit(solution)/shard_map/attend_back/pallas_call | solution.py:403
  347.6 8.6 %collective-permute-done.33.refs_2_ = f32[1,96,768]{2,1,0:T(8,128)S(1)} collective-permute-done((f32[1,96,768]{2,1,0:T(8,128)S(1)}, f32[1,96,768]{2,1,0:T(8,128)S(1)}, u32[]{:S(2)}, u32[]{:S(2)}) %collective-permute-start.33) | collective-permute-done | bytes 294944 | tf_op jit(solution)/shard_map/ppermute | solution.py:441
  356.2 13.0 %collective-permute-done.32.refs_1_ = f32[3,96,768]{2,1,0:T(8,128)S(1)} collective-permute-done((f32[3,96,768]{2,1,0:T(8,128)}, f32[3,96,768]{2,1,0:T(8,128)S(1)}, u32[]{:S(2)}, u32[]{:S(2)}) %collective-permute-start.32) | collective-permute-done | bytes 884768 | tf_op jit(solution)/shard_map/ppermute | solution.py:441
  377.3 3.4 plane_second.3
  382.9 10.4 %fusion.19 = f32[768,1152]{1,0:T(8,128)S(1)} fusion(f32[1024,1152]{1,0:T(8,128)S(1)} %bitcast.141, f32[512,768]{1,0:T(8,128)} %collective-permute-done.refs_1_, f32[512,768]{1,0:T(8,128)} %subtract_multiply_fusion.1.refs_1_, f32[]{:T(128)} %bitcast.43, pred[]{:T(512)S(6)} %eq.7), kind=kOutput, calls=%fused_computation.25 | convolution fusion | flops 5438963712 | bytes 11403269 | tf_op jit(solution)/shard_map/dot_general | solution.py:29
  404.2 9.6 %collective-permute-done.36.refs_1_ = f32[2,96,768]{2,1,0:T(8,128)} collective-permute-done((f32[2,96,768]{2,1,0:T(8,128)}, f32[2,96,768]{2,1,0:T(8,128)}, u32[]{:S(2)}, u32[]{:S(2)}) %collective-permute-start.36) | collective-permute-done | bytes 589856 | tf_op jit(solution)/shard_map/ppermute | solution.py:441
  422.2 9.4 %fusion.16.refs_2_ = f32[1024,768]{1,0:T(8,128)S(1)} fusion(f32[768,1152]{1,0:T(8,128)S(1)} %bitcast.135, f32[1024,1152]{1,0:T(8,128)} %get-tuple-element.71.refs_3_, f32[]{:T(128)} %bitcast.46), kind=kOutput, calls=%fused_computation.19 | convolution fusion | flops 5436997632 | bytes 11403268 | tf_op jit(solution)/shard_map/dot_general | solution.py:39
  433.3 3.3 collective-permute-done.39.refs_1_
  440.0 5.6 %collective-permute-done.38.refs_1_ = f32[2,24,3840]{2,1,0:T(8,128)S(1)} collective-permute-done((f32[2,24,3840]{2,1,0:T(8,128)S(1)}, f32[2,24,3840]{2,1,0:T(8,128)S(1)}, u32[]{:S(2)}, u32[]{:S(2)}) %collective-permute-start.38) | collective-permute-done | bytes 737312 | tf_op jit(solution)/shard_map/ppermute | solution.py:441
  448.1 8.7 %fusion.5.refs_2_ = f32[1024,768]{1,0:T(8,128)S(1)} fusion(f32[1536,768]{1,0:T(8,128)S(1)} %bitcast.139, f32[1024,1536]{1,0:T(8,128)S(1)} %bitcast.175, f32[1536]{0:T(1024)S(1)} %broadcast_add_fusion), kind=kOutput, calls=%fused_computation.6 | convolution fusion | flops 7255621632 | bytes 14161920 | tf_op jit(solution)/shard_map/dot_general | solution.py:25
  458.0 3.3 collective-permute-done.42.refs_1_
  468.2 3.1 fusion.65
  482.0 3.0 collective-permute-done.44.refs_1_
  (396 shorter events, 147.7 us)
Async XLA Ops:
  4.0 6.4 %collective-permute-start.1 = (f32[24,1280]{1,0:T(8,128)S(1)}, f32[24,1280]{1,0:T(8,128)S(1)}, u32[]{:S(2)}, u32[]{:S(2)}) collective-permute-start(f32[24,1280]{1,0:T(8,128)S(1)} %get-tuple-element.133), channel_id=1, source_target_pairs={{0,1},{1,0},{2,3},{3,2},{4,5},{5,4},{6,7},{7,6},{8,9},{9,8},{10,11... | collective-permute-start | bytes 368648 | tf_op jit(solution)/shard_map/ppermute | solution.py:441
  7.7 7.8 %collective-permute-start.7 = (f32[24,1536]{1,0:T(8,128)S(1)}, f32[24,1536]{1,0:T(8,128)S(1)}, u32[]{:S(2)}, u32[]{:S(2)}) collective-permute-start(f32[24,1536]{1,0:T(8,128)S(1)} %get-tuple-element.119), channel_id=1, source_target_pairs={{0,2},{1,3},{2,0},{3,1},{4,6},{5,7},{6,4},{7,5},{8,10},{9,11},{10,... | collective-permute-start | bytes 442376 | tf_op jit(solution)/shard_map/ppermute | solution.py:441
  9.6 65.5 %collective-permute-start = (f32[512,768]{1,0:T(8,128)}, f32[512,768]{1,0:T(8,128)}, u32[]{:S(2)}, u32[]{:S(2)}) collective-permute-start(f32[512,768]{1,0:T(8,128)} %subtract_multiply_fusion.1.refs_1_), channel_id=1, source_target_pairs={{0,1},{1,0},{2,3},{3,2},{4,5},{5,4},{6,7},{7,6},{8,9},{9,8},{10,11... | collective-permute-start | bytes 4718600 | tf_op jit(solution)/shard_map/ppermute | solution.py:441
  11.1 12.5 %collective-permute-start.2 = (f32[2,24,1280]{2,1,0:T(8,128)}, f32[2,24,1280]{2,1,0:T(8,128)S(1)}, u32[]{:S(2)}, u32[]{:S(2)}) collective-permute-start(f32[2,24,1280]{2,1,0:T(8,128)} %after.3), channel_id=1, source_target_pairs={{0,8},{1,9},{2,10},{3,11},{4,12},{5,13},{6,14},{7,15},{8,0},{9,1},... | collective-permute-start | bytes 737288 | tf_op jit(solution)/shard_map/ppermute | solution.py:441
  12.9 20.5 %collective-permute-start.3 = (f32[2,24,1280]{2,1,0:T(8,128)}, f32[2,24,1280]{2,1,0:T(8,128)S(1)}, u32[]{:S(2)}, u32[]{:S(2)}) collective-permute-start(f32[2,24,1280]{2,1,0:T(8,128)} %after.3), channel_id=1, source_target_pairs={{0,16},{1,17},{2,18},{3,19},{4,20},{5,21},{6,22},{7,23},{8,24},{9,... | collective-permute-start | bytes 737288 | tf_op jit(solution)/shard_map/ppermute | solution.py:441
  15.5 17.9 %collective-permute-start.4 = (f32[2,24,1280]{2,1,0:T(8,128)}, f32[2,24,1280]{2,1,0:T(8,128)S(1)}, u32[]{:S(2)}, u32[]{:S(2)}) collective-permute-start(f32[2,24,1280]{2,1,0:T(8,128)} %after.3), channel_id=1, source_target_pairs={{0,24},{1,25},{2,26},{3,27},{4,28},{5,29},{6,30},{7,31},{8,16},{9,... | collective-permute-start | bytes 737288 | tf_op jit(solution)/shard_map/ppermute | solution.py:441
  34.5 21.1 %collective-permute-start.8 = (f32[24,3840]{1,0:T(8,128)}, f32[24,3840]{1,0:T(8,128)S(1)}, u32[]{:S(2)}, u32[]{:S(2)}) collective-permute-start(f32[24,3840]{1,0:T(8,128)} %after.4.refs_0_), channel_id=1, source_target_pairs={{0,16},{1,17},{2,18},{3,19},{4,20},{5,21},{6,22},{7,23},{8,24},{9,... | collective-permute-start | bytes 1105928 | tf_op jit(solution)/shard_map/ppermute | solution.py:441
  39.9 22.4 %collective-permute-start.5 = (f32[4,2,24,1280]{3,2,1,0:T(8,128)}, f32[4,2,24,1280]{3,2,1,0:T(8,128)S(1)}, u32[]{:S(2)}, u32[]{:S(2)}) collective-permute-start(f32[4,2,24,1280]{3,2,1,0:T(8,128)} %pad_maximum_fusion.4.refs_1_.refs_0_), channel_id=1, source_target_pairs={{0,4},{1,5},{2,6},{3,7},{4,0},{5,1},{6,2},{7,3},{8,12},{9,13},{10,... | collective-permute-start | bytes 2949128 | tf_op jit(solution)/shard_map/ppermute | solution.py:441
  57.2 17.3 %collective-permute-start.9 = (f32[2,24,3840]{2,1,0:T(8,128)S(1)}, f32[2,24,3840]{2,1,0:T(8,128)S(1)}, u32[]{:S(2)}, u32[]{:S(2)}) collective-permute-start(f32[2,24,3840]{2,1,0:T(8,128)S(1)} %pair.2.refs_0_.refs_1_), channel_id=1, source_target_pairs={{0,8},{1,9},{2,10},{3,11},{4,12},{5,13},{6,14},{7,15},{8,0},{9,1},... | collective-permute-start | bytes 2211848 | tf_op jit(solution)/shard_map/ppermute | solution.py:441
  57.2 22.5 %collective-permute-start.6 = (f32[4,2,24,1280]{3,2,1,0:T(8,128)}, f32[4,2,24,1280]{3,2,1,0:T(8,128)}, u32[]{:S(2)}, u32[]{:S(2)}) collective-permute-start(f32[4,2,24,1280]{3,2,1,0:T(8,128)} %pad_maximum_fusion.4.refs_1_.refs_0_), channel_id=1, source_target_pairs={{0,2},{1,3},{2,0},{3,1},{4,6},{5,7},{6,4},{7,5},{8,10},{9,11},{10,... | collective-permute-start | bytes 2949128 | tf_op jit(solution)/shard_map/ppermute | solution.py:441
  76.7 3.1 collective-permute-start.10
  76.7 16.6 %collective-permute-start.11 = (f32[96,768]{1,0:T(8,128)}, f32[96,768]{1,0:T(8,128)S(1)}, u32[]{:S(2)}, u32[]{:S(2)}) collective-permute-start(f32[96,768]{1,0:T(8,128)} %after.5.refs_0_), channel_id=1, source_target_pairs={{0,16},{1,17},{2,18},{3,19},{4,20},{5,21},{6,22},{7,23},{8,24},{9,... | collective-permute-start | bytes 884744 | tf_op jit(solution)/shard_map/ppermute | solution.py:441
  76.8 59.7 %collective-permute-start.15 = (f32[4,24,3840]{2,1,0:T(8,128)S(1)}, f32[4,24,3840]{2,1,0:T(8,128)}, u32[]{:S(2)}, u32[]{:S(2)}) collective-permute-start(f32[4,24,3840]{2,1,0:T(8,128)S(1)} %pairs.2.refs_2_.refs_0_), channel_id=1, source_target_pairs={{0,1},{1,0},{2,3},{3,2},{4,5},{5,4},{6,7},{7,6},{8,9},{9,8},{10,11... | collective-permute-start | bytes 4423688 | tf_op jit(solution)/shard_map/ppermute | solution.py:441
  78.3 60.3 %collective-permute-start.14 = (f32[4,24,3840]{2,1,0:T(8,128)S(1)}, f32[4,24,3840]{2,1,0:T(8,128)S(1)}, u32[]{:S(2)}, u32[]{:S(2)}) collective-permute-start(f32[4,24,3840]{2,1,0:T(8,128)S(1)} %pairs.2.refs_2_.refs_0_), channel_id=1, source_target_pairs={{0,4},{1,5},{2,6},{3,7},{4,0},{5,1},{6,2},{7,3},{8,12},{9,13},{10,... | collective-permute-start | bytes 4423688 | tf_op jit(solution)/shard_map/ppermute | solution.py:441
  96.7 15.5 %collective-permute-start.12 = (f32[2,96,768]{2,1,0:T(8,128)}, f32[2,96,768]{2,1,0:T(8,128)S(1)}, u32[]{:S(2)}, u32[]{:S(2)}) collective-permute-start(f32[2,96,768]{2,1,0:T(8,128)} %pair.3.refs_0_), channel_id=1, source_target_pairs={{0,8},{1,9},{2,10},{3,11},{4,12},{5,13},{6,14},{7,15},{8,0},{9,1},... | collective-permute-start | bytes 1769480 | tf_op jit(solution)/shard_map/ppermute | solution.py:441
  114.8 45.7 %collective-permute-start.17 = (f32[4,96,768]{2,1,0:T(8,128)}, f32[4,96,768]{2,1,0:T(8,128)}, u32[]{:S(2)}, u32[]{:S(2)}) collective-permute-start(f32[4,96,768]{2,1,0:T(8,128)} %pairs.3.refs_0_), channel_id=1, source_target_pairs={{0,4},{1,5},{2,6},{3,7},{4,0},{5,1},{6,2},{7,3},{8,12},{9,13},{10,... | collective-permute-start | bytes 3538952 | tf_op jit(solution)/shard_map/ppermute | solution.py:441
  116.3 44.2 %collective-permute-start.18 = (f32[4,96,768]{2,1,0:T(8,128)}, f32[4,96,768]{2,1,0:T(8,128)}, u32[]{:S(2)}, u32[]{:S(2)}) collective-permute-start(f32[4,96,768]{2,1,0:T(8,128)} %pairs.3.refs_0_), channel_id=1, source_target_pairs={{0,1},{1,0},{2,3},{3,2},{4,5},{5,4},{6,7},{7,6},{8,9},{9,8},{10,11... | collective-permute-start | bytes 3538952 | tf_op jit(solution)/shard_map/ppermute | solution.py:441
  136.0 24.5 %collective-permute-start.13 = (f32[512,384]{1,0:T(8,128)S(1)}, f32[512,384]{1,0:T(8,128)S(1)}, u32[]{:S(2)}, u32[]{:S(2)}) collective-permute-start(f32[512,384]{1,0:T(8,128)S(1)} %get-tuple-element.113), channel_id=1, source_target_pairs={{0,1},{1,0},{2,3},{3,2},{4,5},{5,4},{6,7},{7,6},{8,9},{9,8},{10,11... | collective-permute-start | bytes 2359304 | tf_op jit(solution)/shard_map/ppermute | solution.py:441
  137.9 28.2 %collective-permute-start.16 = (f32[3,24,3840]{2,1,0:T(8,128)S(1)}, f32[3,24,3840]{2,1,0:T(8,128)S(1)}, u32[]{:S(2)}, u32[]{:S(2)}) collective-permute-start(f32[3,24,3840]{2,1,0:T(8,128)S(1)} %corner_first.1), channel_id=1, source_target_pairs={{0,4},{1,5},{2,6},{3,7},{4,0},{5,1},{6,2},{7,3},{8,12},{9,13},{10,... | collective-permute-start | bytes 3317768 | tf_op jit(solution)/shard_map/ppermute | solution.py:441
  164.1 8.8 %collective-permute-start.19 = (f32[1,24,3840]{2,1,0:T(8,128)S(1)}, f32[1,24,3840]{2,1,0:T(8,128)S(1)}, u32[]{:S(2)}, u32[]{:S(2)}) collective-permute-start(f32[1,24,3840]{2,1,0:T(8,128)S(1)} %get-tuple-element.58), channel_id=1, source_target_pairs={{0,1},{1,0},{2,3},{3,2},{4,5},{5,4},{6,7},{7,6},{8,9},{9,8},{10,11... | collective-permute-start | bytes 1105928 | tf_op jit(solution)/shard_map/ppermute | solution.py:441
  176.0 3.3 collective-permute-start.20
  176.1 16.3 %collective-permute-start.22 = (f32[512,768]{1,0:T(8,128)}, f32[512,768]{1,0:T(8,128)}, u32[]{:S(2)}, u32[]{:S(2)}) collective-permute-start(f32[512,768]{1,0:T(8,128)} %param.16), channel_id=1, source_target_pairs={{0,2},{1,3},{2,0},{3,1},{4,6},{5,7},{6,4},{7,5},{8,10},{9,11},{10,... | collective-permute-start | bytes 4718600 | tf_op jit(solution)/shard_map/ppermute | solution.py:441
  188.9 25.3 %collective-permute-start.21 = (f32[512,768]{1,0:T(8,128)}, f32[512,768]{1,0:T(8,128)}, u32[]{:S(2)}, u32[]{:S(2)}) collective-permute-start(f32[512,768]{1,0:T(8,128)} %multiply_add_fusion.2), channel_id=1, source_target_pairs={{0,2},{1,3},{2,0},{3,1},{4,6},{5,7},{6,4},{7,5},{8,10},{9,11},{10,... | collective-permute-start | bytes 4718600 | tf_op jit(solution)/shard_map/ppermute | solution.py:441
  189.1 22.2 %collective-permute-start.23 = (f32[3,96,768]{2,1,0:T(8,128)}, f32[3,96,768]{2,1,0:T(8,128)}, u32[]{:S(2)}, u32[]{:S(2)}) collective-permute-start(f32[3,96,768]{2,1,0:T(8,128)} %get-tuple-element.61), channel_id=1, source_target_pairs={{0,4},{1,5},{2,6},{3,7},{4,0},{5,1},{6,2},{7,3},{8,12},{9,13},{10,... | collective-permute-start | bytes 2654216 | tf_op jit(solution)/shard_map/ppermute | solution.py:441
  196.1 9.2 %collective-permute-start.24 = (f32[1,96,768]{2,1,0:T(8,128)}, f32[1,96,768]{2,1,0:T(8,128)S(1)}, u32[]{:S(2)}, u32[]{:S(2)}) collective-permute-start(f32[1,96,768]{2,1,0:T(8,128)} %copy-done.47), channel_id=1, source_target_pairs={{0,1},{1,0},{2,3},{3,2},{4,5},{5,4},{6,7},{7,6},{8,9},{9,8},{10,11... | collective-permute-start | bytes 884744 | tf_op jit(solution)/shard_map/ppermute | solution.py:441
  248.1 23.8 %collective-permute-start.25 = (f32[512,768]{1,0:T(8,128)}, f32[512,768]{1,0:T(8,128)}, u32[]{:S(2)}, u32[]{:S(2)}) collective-permute-start(f32[512,768]{1,0:T(8,128)} %slice.126), channel_id=1, source_target_pairs={{0,2},{1,3},{2,0},{3,1},{4,6},{5,7},{6,4},{7,5},{8,10},{9,11},{10,... | collective-permute-start | bytes 4718600 | tf_op jit(solution)/shard_map/ppermute | solution.py:441
  269.2 41.3 %collective-permute-start.27 = (f32[3,2,96,768]{3,2,1,0:T(8,128)}, f32[3,2,96,768]{3,2,1,0:T(8,128)}, u32[]{:S(2)}, u32[]{:S(2)}) collective-permute-start(f32[3,2,96,768]{3,2,1,0:T(8,128)} %get-tuple-element.63), channel_id=1, source_target_pairs={{0,4},{1,5},{2,6},{3,7},{4,0},{5,1},{6,2},{7,3},{8,12},{9,13},{10,... | collective-permute-start | bytes 5308424 | tf_op jit(solution)/shard_map/ppermute | solution.py:441
  269.7 40.0 %collective-permute-start.28 = (f32[1,2,96,768]{3,2,1,0:T(8,128)}, f32[1,2,96,768]{3,2,1,0:T(8,128)}, u32[]{:S(2)}, u32[]{:S(2)}) collective-permute-start(f32[1,2,96,768]{3,2,1,0:T(8,128)} %get-tuple-element.64), channel_id=1, source_target_pairs={{0,1},{1,0},{2,3},{3,2},{4,5},{5,4},{6,7},{7,6},{8,9},{9,8},{10,11... | collective-permute-start | bytes 1769480 | tf_op jit(solution)/shard_map/ppermute | solution.py:441
  280.9 32.4 %collective-permute-start.26 = (f32[4,2,2,24,768]{4,3,2,1,0:T(8,128)}, f32[4,2,2,24,768]{4,3,2,1,0:T(8,128)S(1)}, u32[]{:S(2)}, u32[]{:S(2)}) collective-permute-start(f32[4,2,2,24,768]{4,3,2,1,0:T(8,128)} %dynamic-slice_bitcast_fusion), channel_id=1, source_target_pairs={{0,2},{1,3},{2,0},{3,1},{4,6},{5,7},{6,4},{7,5},{8,10},{9,11},{10,... | collective-permute-start | bytes 3538952 | tf_op jit(solution)/shard_map/ppermute | solution.py:441
  289.6 19.5 %collective-permute-start.29 = (f32[512,384]{1,0:T(8,128)S(1)}, f32[512,384]{1,0:T(8,128)S(1)}, u32[]{:S(2)}, u32[]{:S(2)}) collective-permute-start(f32[512,384]{1,0:T(8,128)S(1)} %get-tuple-element.109.refs_0_), channel_id=1, source_target_pairs={{0,1},{1,0},{2,3},{3,2},{4,5},{5,4},{6,7},{7,6},{8,9},{9,8},{10,11... | collective-permute-start | bytes 2359304 | tf_op jit(solution)/shard_map/ppermute | solution.py:441
  315.7 61.6 %collective-permute-start.30 = (f32[2,2,24,3840]{3,2,1,0:T(8,128)}, f32[2,2,24,3840]{3,2,1,0:T(8,128)}, u32[]{:S(2)}, u32[]{:S(2)}) collective-permute-start(f32[2,2,24,3840]{3,2,1,0:T(8,128)} %get-tuple-element.67.refs_0_), channel_id=1, source_target_pairs={{0,4},{1,5},{2,6},{3,7},{4,0},{5,1},{6,2},{7,3},{8,12},{9,13},{10,... | collective-permute-start | bytes 4423688 | tf_op jit(solution)/shard_map/ppermute | solution.py:441
  317.0 60.3 %collective-permute-start.31 = (f32[2,2,24,3840]{3,2,1,0:T(8,128)}, f32[2,2,24,3840]{3,2,1,0:T(8,128)}, u32[]{:S(2)}, u32[]{:S(2)}) collective-permute-start(f32[2,2,24,3840]{3,2,1,0:T(8,128)} %get-tuple-element.68.refs_1_), channel_id=1, source_target_pairs={{0,1},{1,0},{2,3},{3,2},{4,5},{5,4},{6,7},{7,6},{8,9},{9,8},{10,11... | collective-permute-start | bytes 4423688 | tf_op jit(solution)/shard_map/ppermute | solution.py:441
  317.8 51.4 %collective-permute-start.32 = (f32[3,96,768]{2,1,0:T(8,128)}, f32[3,96,768]{2,1,0:T(8,128)S(1)}, u32[]{:S(2)}, u32[]{:S(2)}) collective-permute-start(f32[3,96,768]{2,1,0:T(8,128)} %get-tuple-element.65.refs_3_.refs_2_), channel_id=1, source_target_pairs={{0,1},{1,0},{2,3},{3,2},{4,5},{5,4},{6,7},{7,6},{8,9},{9,8},{10,11... | collective-permute-start | bytes 2654216 | tf_op jit(solution)/shard_map/ppermute | solution.py:441
  319.0 37.2 %collective-permute-start.33 = (f32[1,96,768]{2,1,0:T(8,128)S(1)}, f32[1,96,768]{2,1,0:T(8,128)S(1)}, u32[]{:S(2)}, u32[]{:S(2)}) collective-permute-start(f32[1,96,768]{2,1,0:T(8,128)S(1)} %get-tuple-element.66.refs_4_.refs_3_), channel_id=1, source_target_pairs={{0,4},{1,5},{2,6},{3,7},{4,0},{5,1},{6,2},{7,3},{8,12},{9,13},{10,... | collective-permute-start | bytes 884744 | tf_op jit(solution)/shard_map/ppermute | solution.py:441
  395.1 5.0 %collective-permute-start.37 = (f32[4,2,2,24,1280]{4,3,2,1,0:T(8,128)S(1)}, f32[4,2,2,24,1280]{4,3,2,1,0:T(8,128)S(1)}, u32[]{:S(2)}, u32[]{:S(2)}) collective-permute-start(f32[4,2,2,24,1280]{4,3,2,1,0:T(8,128)S(1)} %get-tuple-element.79), channel_id=1, source_target_pairs={{0,2},{1,3},{2,0},{3,1},{4,6},{5,7},{6,4},{7,5},{8,10},{9,11},{10,... | collective-permute-start | bytes 5898248 | tf_op jit(solution)/shard_map/ppermute | solution.py:441
  395.2 22.2 %collective-permute-start.34 = (f32[2,24,3840]{2,1,0:T(8,128)}, f32[2,24,3840]{2,1,0:T(8,128)}, u32[]{:S(2)}, u32[]{:S(2)}) collective-permute-start(f32[2,24,3840]{2,1,0:T(8,128)} %get-tuple-element.74.refs_0_), channel_id=1, source_target_pairs={{0,1},{1,0},{2,3},{3,2},{4,5},{5,4},{6,7},{7,6},{8,9},{9,8},{10,11... | collective-permute-start | bytes 2211848 | tf_op jit(solution)/shard_map/ppermute | solution.py:441
  396.7 20.8 %collective-permute-start.35 = (f32[2,24,3840]{2,1,0:T(8,128)}, f32[2,24,3840]{2,1,0:T(8,128)}, u32[]{:S(2)}, u32[]{:S(2)}) collective-permute-start(f32[2,24,3840]{2,1,0:T(8,128)} %get-tuple-element.75.refs_1_), channel_id=1, source_target_pairs={{0,4},{1,5},{2,6},{3,7},{4,0},{5,1},{6,2},{7,3},{8,12},{9,13},{10,... | collective-permute-start | bytes 2211848 | tf_op jit(solution)/shard_map/ppermute | solution.py:441
  398.1 15.7 %collective-permute-start.36 = (f32[2,96,768]{2,1,0:T(8,128)}, f32[2,96,768]{2,1,0:T(8,128)}, u32[]{:S(2)}, u32[]{:S(2)}) collective-permute-start(f32[2,96,768]{2,1,0:T(8,128)} %get-tuple-element.72.refs_5_), channel_id=1, source_target_pairs={{0,8},{1,9},{2,10},{3,11},{4,12},{5,13},{6,14},{7,15},{8,0},{9,1},... | collective-permute-start | bytes 1769480 | tf_op jit(solution)/shard_map/ppermute | solution.py:441
  402.9 33.7 %collective-permute-start.39 = (f32[4,2,24,1280]{3,2,1,0:T(8,128)}, f32[4,2,24,1280]{3,2,1,0:T(8,128)}, u32[]{:S(2)}, u32[]{:S(2)}) collective-permute-start(f32[4,2,24,1280]{3,2,1,0:T(8,128)} %get-tuple-element.80.refs_2_), channel_id=1, source_target_pairs={{0,4},{1,5},{2,6},{3,7},{4,0},{5,1},{6,2},{7,3},{8,12},{9,13},{10,... | collective-permute-start | bytes 2949128 | tf_op jit(solution)/shard_map/ppermute | solution.py:441
  419.8 25.8 %collective-permute-start.38 = (f32[2,24,3840]{2,1,0:T(8,128)S(1)}, f32[2,24,3840]{2,1,0:T(8,128)S(1)}, u32[]{:S(2)}, u32[]{:S(2)}) collective-permute-start(f32[2,24,3840]{2,1,0:T(8,128)S(1)} %get-tuple-element.83.refs_0_), channel_id=1, source_target_pairs={{0,8},{1,9},{2,10},{3,11},{4,12},{5,13},{6,14},{7,15},{8,0},{9,1},... | collective-permute-start | bytes 2211848 | tf_op jit(solution)/shard_map/ppermute | solution.py:441
  421.6 43.9 %collective-permute-start.47 = (f32[96,768]{1,0:T(8,128)}, f32[96,768]{1,0:T(8,128)}, u32[]{:S(2)}, u32[]{:S(2)}) collective-permute-start(f32[96,768]{1,0:T(8,128)} %get-tuple-element.81.refs_3_), channel_id=1, source_target_pairs={{0,16},{1,17},{2,18},{3,19},{4,20},{5,21},{6,22},{7,23},{8,24},{9,... | collective-permute-start | bytes 884744 | tf_op jit(solution)/shard_map/ppermute | solution.py:441
  432.8 35.4 %collective-permute-start.41 = (f32[512,768]{1,0:T(8,128)}, f32[512,768]{1,0:T(8,128)}, u32[]{:S(2)}, u32[]{:S(2)}) collective-permute-start(f32[512,768]{1,0:T(8,128)} %constant_dynamic-slice_fusion.1), channel_id=1, source_target_pairs={{0,1},{1,0},{2,3},{3,2},{4,5},{5,4},{6,7},{7,6},{8,9},{9,8},{10,11... | collective-permute-start | bytes 4718600 | tf_op jit(solution)/shard_map/ppermute | solution.py:441
  438.0 23.4 %collective-permute-start.42 = (f32[2,2,24,1280]{3,2,1,0:T(8,128)S(1)}, f32[2,2,24,1280]{3,2,1,0:T(8,128)S(1)}, u32[]{:S(2)}, u32[]{:S(2)}) collective-permute-start(f32[2,2,24,1280]{3,2,1,0:T(8,128)S(1)} %get-tuple-element.85.refs_2_), channel_id=1, source_target_pairs={{0,8},{1,9},{2,10},{3,11},{4,12},{5,13},{6,14},{7,15},{8,0},{9,1},... | collective-permute-start | bytes 1474568 | tf_op jit(solution)/shard_map/ppermute | solution.py:441
  446.8 16.4 %collective-permute-start.45 = (f32[24,3840]{1,0:T(8,128)S(1)}, f32[24,3840]{1,0:T(8,128)S(1)}, u32[]{:S(2)}, u32[]{:S(2)}) collective-permute-start(f32[24,3840]{1,0:T(8,128)S(1)} %get-tuple-element.86.refs_0_), channel_id=1, source_target_pairs={{0,16},{1,17},{2,18},{3,19},{4,20},{5,21},{6,22},{7,23},{8,24},{9,... | collective-permute-start | bytes 1105928 | tf_op jit(solution)/shard_map/ppermute | solution.py:441
  458.0 21.8 %collective-permute-start.40 = (f32[512,768]{1,0:T(8,128)}, f32[512,768]{1,0:T(8,128)}, u32[]{:S(2)}, u32[]{:S(2)}) collective-permute-start(f32[512,768]{1,0:T(8,128)} %slice.128), channel_id=1, source_target_pairs={{0,2},{1,3},{2,0},{3,1},{4,6},{5,7},{6,4},{7,5},{8,10},{9,11},{10,... | collective-permute-start | bytes 4718600 | tf_op jit(solution)/shard_map/ppermute | solution.py:441
  462.7 14.5 %collective-permute-start.43 = (f32[2,24,1280]{2,1,0:T(8,128)}, f32[2,24,1280]{2,1,0:T(8,128)}, u32[]{:S(2)}, u32[]{:S(2)}) collective-permute-start(f32[2,24,1280]{2,1,0:T(8,128)} %get-tuple-element.89.refs_2_), channel_id=1, source_target_pairs={{0,16},{1,17},{2,18},{3,19},{4,20},{5,21},{6,22},{7,23},{8,24},{9,... | collective-permute-start | bytes 737288 | tf_op jit(solution)/shard_map/ppermute | solution.py:441
  465.2 7.9 %collective-permute-start.46 = (f32[24,1536]{1,0:T(8,128)}, f32[24,1536]{1,0:T(8,128)}, u32[]{:S(2)}, u32[]{:S(2)}) collective-permute-start(f32[24,1536]{1,0:T(8,128)} %get-tuple-element.117), channel_id=1, source_target_pairs={{0,2},{1,3},{2,0},{3,1},{4,6},{5,7},{6,4},{7,5},{8,10},{9,11},{10,... | collective-permute-start | bytes 442376 | tf_op jit(solution)/shard_map/ppermute | solution.py:441
  479.2 5.8 %collective-permute-start.44 = (f32[24,1280]{1,0:T(8,128)S(1)}, f32[24,1280]{1,0:T(8,128)S(1)}, u32[]{:S(2)}, u32[]{:S(2)}) collective-permute-start(f32[24,1280]{1,0:T(8,128)S(1)} %get-tuple-element.91), channel_id=1, source_target_pairs={{0,1},{1,0},{2,3},{3,2},{4,5},{5,4},{6,7},{7,6},{8,9},{9,8},{10,11... | collective-permute-start | bytes 368648 | tf_op jit(solution)/shard_map/ppermute | solution.py:441
  (99 other events, 626.2 us)

commit v4 on v3

--- a/solution.py
+++ b/solution.py
@@ -800,13 +800,15 @@
         x_corner_b[...] = y_of_b[:CUT]
         y_corner_b[...] = x_of_b[CUT:]
 
+    grid = (COLUMNS, 2, 2, 2)
+    scales = jnp.stack([gain_one, shift_one], axis=1).reshape(grid + (shard, 2))
     low, high = (CUT,), (COLUMNS - CUT,)
     block_a, block_b = own_a.shape[1:], own_b.shape[1:]
     x_corner_a, = local_call(
         corner_first, "corner_first", where, [sides_a[1]], [head_out], [low + block_a]
     )
     y_corner_a, x_corner_b, y_corner_b = local_call(
-        corner_rest, "corner_rest", where, [sides_a[0], *sides_b], [there],
+        corner_rest, "corner_rest", where, [sides_a[0], *sides_b], [there, scales],
         [high + block_a, low + block_b, high + block_b],
     )
     corners_a = swap(x_corner_a, over_x), swap(y_corner_a, over_y)
@@ -869,10 +871,8 @@
         [lanes(d_out_b, d_gain_two, d_shift_two), lanes(d_up_b, d_down_b)],
         axis=1,
     )
-    grid = (COLUMNS, 2, 2, 2)
-    scales = jnp.stack([gain_one, shift_one], axis=1).reshape(grid + (shard, 2))
     small = jnp.pad(small, ((0, 0), (0, 6), (0, 0)))
-    chip_a = matmul_tn(both_normed + zero_after(where, sent, small, scales), d_pre).reshape(COLUMNS, 2, 2, 2, shard, hidden)
+    chip_a = matmul_tn(both_normed + zero_after(where, sent, small), d_pre).reshape(COLUMNS, 2, 2, 2, shard, hidden)
     def join_rows(place, own, arrived, out):
         y = place[3]
         out[pl.ds(y * rows, rows)] = own[...]
@@ -884,11 +884,11 @@
     )
     block_b = (4 * shard, D)
     block_a = (shard, 5 * D)
-    to_x, to_y = plane_first(where, [chip_b], block_b, CUT)
+    to_x, to_y = plane_first(where, [chip_b], block_b, 2)
     side_b = swap(to_x, over_x), swap(to_y, over_y)
     d_out_w = matmul_tn(attended, d_middle).reshape(COLUMNS, 2, 2, 2, shard, D)
     chip_a = [chip_a, d_out_w, swap(pick(d_out_w, 1 - core, 2), over_core)]
-    kept_b, *sent_b = plane_second(where, [chip_b], block_b, *side_b, CUT, [d_out])
+    kept_b, *sent_b = plane_second(where, [chip_b], block_b, *side_b, 2, [d_out])
     first_a = plane_first(where, chip_a, block_a, 2, sent_b)
     side_a = swap(first_a[0], over_x), swap(first_a[1], over_y)
 
@@ -896,11 +896,13 @@
         seq_lengths, projected, d_out, head_out, log_sum, *first_a, *sent_b
     )
     corner = swap(sent_b[0], over_y), swap(sent_b[1], over_x)
-    pair_b, sent_b = column_first(where, block_b, kept_b, *corner, CUT, [d_proj])
+    pair_b, sent_b = column_first(where, block_b, kept_b, *corner, 2, [d_proj])
     kept_a, *sent_a = plane_second(where, chip_a, block_a, *side_a, 2, [sent_b])
     corner_a = swap(sent_a[0], over_y), swap(sent_a[1], over_x)
 
     moved = matmul_tn(normed_one + zero_after(where, *sent_a), d_proj)
+    own_b, sent_b = column_second(where, pair_b, swap(sent_b, over_z[1]), [moved])
+    pair_a, sent_a = column_first(where, block_a, kept_a, *corner_a, 2, [sent_b])
     last_lane = wide + PAIR - 1
 
     def finish(place, moved, weight, scales, total, small, kept, sent):
@@ -952,7 +954,7 @@
             d_bias_all,
             small.reshape(grid + (8, PAIR)),
         ],
-        (),
+        [sent_a],
         [(COLUMNS, 2, 2) + block] * 2,
     )
 
@@ -970,9 +972,7 @@
         (),
         [(COLUMNS, 2) + block] * 2,
     )
-    own_b, sent_b = column_second(where, pair_b, swap(sent_b, over_z[1]), [second])
-    pair_a, sent_a = column_first(where, block_a, kept_a, *corner_a, 2, [sent_b])
-    d_norm = matmul_nt(d_proj + zero_after(where, sent_a), w_qkv)
+    d_norm = matmul_nt(d_proj + zero_after(where, second), w_qkv)
     d_norm_sent = rows_of(d_norm, 1 - y)
 
     def line_sum(place, kept, arrived, pair, sent):

time: 494 us -> 487 us (0.986); the launches traced: 489 us -> 488 us
  waiting for transfers between devices: 146 us -> 136 us
  Pallas kernels: 96.8 us -> 104 us
  matrix products: 105 us -> 111 us
    pallas_call x4, Pallas kernels: 12.4 us -> 22.8 us  [assemble(): pl.pallas_call(functools.partial(assemble_kernel, (len(pieces), copies)),...]
    ppermute x48, waiting for transfers between devices: 146 us -> 136 us  [swap(): return lax.ppermute(values, AXES, pairs)]
    dot_general x4, matrix products: 33 us -> 38.2 us  [matmul(): jnp.dot(left, right, precision=top_prec, preferred_element_type=jnp.float32)]
    unnamed x200 -> x168, local copies, waits for them, and re-layouts: 28.2 us -> 24.9 us
  transfers between devices with their start and end apart: 48 -> 48, of which waited for: 24 -> 21; matrix products, arithmetic and copies ran while one was open for 25% -> 28% of each run, Pallas kernels for 17% -> 16%
where the time goes in v4:
time: 487 us; the launch traced here: 488 us
  waiting for transfers between devices  136 us (28%)
  matrix products  111 us (23%)
  Pallas kernels  104 us (21%)
  local copies, waits for them, and re-layouts  60 us (12%)
  starting transfers between devices  44.2 us (9%)
  other arithmetic  29.6 us (6%)
    ppermute x48, waiting for transfers between devices, swap(): return lax.ppermute(values, AXES, pairs)  136 us
    ppermute x48, starting transfers between devices, swap(): return lax.ppermute(values, AXES, pairs)  44.2 us
    dot_general x4, matrix products, matmul_tn(): lax.dot_general(left, right, (((0,), (0,)), ((), ())), precision=top_prec...  40.2 us
    pallas_call x28, Pallas kernels, local_call(): pl.pallas_call(call, in_specs=[pl.BlockSpec(memory_space=pltpu.SMEM)] + [...  38.2 us
    dot_general x4, matrix products, matmul(): jnp.dot(left, right, precision=top_prec, preferred_element_type=jnp.float32)  38.2 us
    dot_general x4, matrix products, matmul_nt(): lax.dot_general(left, right, (((1,), (1,)), ((), ())), precision=top_prec...  32.9 us
    pallas_call x1, Pallas kernels, attend_back(): pl.pallas_call(attend_back_kernel, grid=(pairs,), in_specs=[pl.BlockSpec(...  27.2 us
    unnamed x168, local copies, waits for them, and re-layouts  24.9 us
  transfers between devices with their start and end apart: 48, of which 21 were waited for; matrix products, arithmetic and copies ran while one was open for 28% of the time, Pallas kernels for 16%

profile of v4, /device:TPU:0, one launch (start us, length us, event | category | flops | bytes accessed | tf_op | source)
XLA Modules:
  0.0 487.9 jit_solution(10186408437647400786)
XLA Ops:
  4.0 3.0 collective-permute-start.1
  12.9 2.6 collective-permute-start.3
  16.9 6.7 %collective-permute-done.2 = f32[2,24,1280]{2,1,0:T(8,128)S(1)} collective-permute-done((f32[2,24,1280]{2,1,0:T(8,128)}, f32[2,24,1280]{2,1,0:T(8,128)S(1)}, u32[]{:S(2)}, u32[]{:S(2)}) %collective-permute-start.2) | collective-permute-done | bytes 245792 | tf_op jit(solution)/shard_map/ppermute | solution.py:441
  23.6 9.8 %collective-permute-done.3 = f32[2,24,1280]{2,1,0:T(8,128)S(1)} collective-permute-done((f32[2,24,1280]{2,1,0:T(8,128)}, f32[2,24,1280]{2,1,0:T(8,128)S(1)}, u32[]{:S(2)}, u32[]{:S(2)}) %collective-permute-start.3) | collective-permute-done | bytes 245792 | tf_op jit(solution)/shard_map/ppermute | solution.py:441
  34.5 5.4 %collective-permute-start.8 = (f32[24,3840]{1,0:T(8,128)}, f32[24,3840]{1,0:T(8,128)S(1)}, u32[]{:S(2)}, u32[]{:S(2)}) collective-permute-start(f32[24,3840]{1,0:T(8,128)} %after.4.refs_0_), channel_id=1, source_target_pairs={{0,16},{1,17},{2,18},{3,19},{4,20},{5,21},{6,22},{7,23},{8,24},{9,... | collective-permute-start | bytes 1105928 | tf_op jit(solution)/shard_map/ppermute | solution.py:441
  41.5 14.1 %collective-permute-done.8.refs_1_ = f32[24,3840]{1,0:T(8,128)S(1)} collective-permute-done((f32[24,3840]{1,0:T(8,128)}, f32[24,3840]{1,0:T(8,128)S(1)}, u32[]{:S(2)}, u32[]{:S(2)}) %collective-permute-start.8) | collective-permute-done | bytes 368672 | tf_op jit(solution)/shard_map/ppermute | solution.py:441
  57.3 5.0 %collective-permute-done.5.refs_2_.refs_0_.refs_1_ = f32[4,2,24,1280]{3,2,1,0:T(8,128)S(1)} collective-permute-done((f32[4,2,24,1280]{3,2,1,0:T(8,128)}, f32[4,2,24,1280]{3,2,1,0:T(8,128)S(1)}, u32[]{:S(2)}, u32[]{:S(2)}) %collective-permute-start.5) | collective-permute-done | bytes 983072 | tf_op jit(solution)/shard_map/ppermute | solution.py:441
  62.3 12.2 %collective-permute-done.9.refs_1_ = f32[2,24,3840]{2,1,0:T(8,128)S(1)} collective-permute-done((f32[2,24,3840]{2,1,0:T(8,128)S(1)}, f32[2,24,3840]{2,1,0:T(8,128)S(1)}, u32[]{:S(2)}, u32[]{:S(2)}) %collective-permute-start.9) | collective-permute-done | bytes 737312 | tf_op jit(solution)/shard_map/ppermute | solution.py:441
  81.0 3.1 assemble.4
  88.6 4.7 collective-permute-done.11.refs_1_
  101.7 10.5 %convolution_add_fusion.refs_2_.qkv_ref = f32[1024,1152]{1,0:T(8,128)S(1)} fusion(f32[768,1152]{1,0:T(8,128)} %bitcast.134, f32[1152]{0:T(1024)} %add.213, f32[512,768]{1,0:T(8,128)} %collective-permute-done.refs_1_, f32[512,768]{1,0:T(8,128)} %subtract_multiply_fusion.1.refs_1_, f32[768]{0:T(1024)} %add.210, f32[768]{0:T(1024)S(1)} %mul.147, pred[]{:T(512)S(6)} %eq.7), kind=kOutput, calls=%fused_computation.21 | convolution fusion | flops 5440929792 | bytes 11414017 | tf_op jit(solution)/shard_map/dot_general | solution.py:25
  112.2 2.6 pairs.3.refs_0_
  118.5 16.1 %attend.1 = (f32[1024,384]{1,0:T(8,128)S(1)}, f32[1024,384]{1,0:T(8,128)S(1)}) custom-call(s32[1]{0:T(128)S(6)} %copy.110.len_ref, f32[1024,1152]{1,0:T(8,128)} %copy-done, f32[4,96,768]{2,1,0:T(8,128)} %pairs.3.refs_0_), custom_call_target="tpu_custom_call" | custom-call | tf_op jit(solution)/shard_map/attend/pallas_call | solution.py:387
  141.4 19.8 %collective-permute-done.13.refs_3_ = f32[512,384]{1,0:T(8,128)} collective-permute-done((f32[512,384]{1,0:T(8,128)}, f32[512,384]{1,0:T(8,128)}, u32[]{:S(2)}, u32[]{:S(2)}) %collective-permute-start.13) | collective-permute-done | bytes 786464 | tf_op jit(solution)/shard_map/ppermute | solution.py:441
  161.2 3.1 corner_rest.1
  166.8 7.6 %collective-permute-done.19.refs_4_ = f32[1,24,3840]{2,1,0:T(8,128)S(1)} collective-permute-done((f32[1,24,3840]{2,1,0:T(8,128)S(1)}, f32[1,24,3840]{2,1,0:T(8,128)S(1)}, u32[]{:S(2)}, u32[]{:S(2)}) %collective-permute-start.19) | collective-permute-done | bytes 368672 | tf_op jit(solution)/shard_map/ppermute | solution.py:441
  174.4 13.9 %assemble.5 = f32[4,2,2,24,768]{4,3,2,1,0:T(8,128)} custom-call(s32[4]{0:T(128)S(1)} %pad_add_fusion.place_ref, f32[4,24,3840]{2,1,0:T(8,128)S(1)} %pairs.2.refs_2_.refs_0_, f32[4,24,3840]{2,1,0:T(8,128)} %collective-permute-done.14.refs_0_.refs_1_, f32[4,24,3840]{2,1,0:T(8,128)S(1)} %collective-permute-done.15.refs_0_.refs_2_, ...), custom_call_target="tpu_custom_call" | custom-call | tf_op jit(solution)/shard_map/assemble/pallas_call | solution.py:492
  189.2 2.4 collective-permute-done.20
  191.6 2.9 maximum_select_fusion.1
  196.9 3.8 fusion.69
  203.2 2.8 fusion.67
  205.9 2.7 constant_dynamic-update-slice_fusion
  211.2 2.9 assemble.6
  215.0 3.9 collective-permute-done.24.refs_4_
  218.9 6.0 %collective-permute-done.23.refs_3_ = f32[3,96,768]{2,1,0:T(8,128)} collective-permute-done((f32[3,96,768]{2,1,0:T(8,128)}, f32[3,96,768]{2,1,0:T(8,128)}, u32[]{:S(2)}, u32[]{:S(2)}) %collective-permute-start.23) | collective-permute-done | bytes 884768 | tf_op jit(solution)/shard_map/ppermute | solution.py:441
  224.9 2.9 assemble.7
  227.8 11.5 %fusion.30 = f32[1024,1536]{1,0:T(8,128)S(1)} fusion(f32[768,1536]{1,0:T(8,128)S(1)} %bitcast.149, f32[512,768]{1,0:T(8,128)} %collective-permute-done.21, f32[512,768]{1,0:T(8,128)} %multiply_add_fusion.2), kind=kOutput, calls=%fused_computation.36 | convolution fusion | flops 7248543744 | bytes 14155776 | tf_op jit(solution)/shard_map/dot_general | solution.py:25
  239.3 12.8 %fusion.70 = (f32[1536]{0:T(1024)S(1)}, f32[1024,1536]{1,0:T(8,128)S(1)}) fusion(f32[1024,1536]{1,0:T(8,128)S(1)} %fusion.30, f32[1536]{0:T(1024)S(1)} %reshape.179, f32[1024,768]{1,0:T(8,128)} %constant_dynamic-update-slice_fusion, f32[1536,768]{1,0:T(8,128)S(1)} %bitcast.137), kind=kOutput, calls=%fused_computation.159 | convolution fusion | flops 7265057280 | bytes 20459520 | tf_op jit(solution)/shard_map/dot_general | solution.py:39
  252.1 7.8 %fusion.71 = f32[1024,768]{1,0:T(8,128)S(1)} fusion(f32[1024,1536]{1,0:T(8,128)S(1)} %get-tuple-element.139, f32[768,1536]{1,0:T(8,128)S(1)} %bitcast.150), kind=kOutput, calls=%fused_computation.160 | convolution fusion | flops 7247757312 | bytes 14155776 | tf_op jit(solution)/shard_map/dot_general | solution.py:39
  261.4 11.9 %fusion.12 = f32[1536,768]{1,0:T(8,128)S(1)} fusion(f32[1024,768]{1,0:T(8,128)} %constant_dynamic-update-slice_fusion, f32[1024,1536]{1,0:T(8,128)} %copy-done.78, f32[1536]{0:T(1024)S(1)} %reshape.179), kind=kOutput, calls=%fused_computation.13 | convolution fusion | flops 7255621632 | bytes 14161920 | tf_op jit(solution)/shard_map/dot_general | solution.py:29
  279.0 2.9 multiply_reduce_fusion.1
  283.9 4.2 fusion.42
  290.3 3.3 fusion.34
  300.3 13.1 %fusion.21 = f32[768,1536]{1,0:T(8,128)S(1)} fusion(f32[1024,1536]{1,0:T(8,128)} %copy-done.77, f32[512,768]{1,0:T(8,128)} %collective-permute-done.21, f32[512,768]{1,0:T(8,128)} %multiply_add_fusion.2, f32[]{:T(128)} %bitcast.37), kind=kOutput, calls=%fused_computation.27 | convolution fusion | flops 7249330176 | bytes 14155780 | tf_op jit(solution)/shard_map/dot_general | solution.py:29
  313.4 8.5 %collective-permute-done.29.refs_1_ = f32[512,384]{1,0:T(8,128)S(1)} collective-permute-done((f32[512,384]{1,0:T(8,128)S(1)}, f32[512,384]{1,0:T(8,128)S(1)}, u32[]{:S(2)}, u32[]{:S(2)}) %collective-permute-start.29) | collective-permute-done | bytes 786464 | tf_op jit(solution)/shard_map/ppermute | solution.py:441
  322.7 3.2 plane_second.2
  325.9 2.4 plane_first.3
  332.3 27.2 %attend_back.1 = (f32[1024,1152]{1,0:T(8,128)}, f32[8,1152]{1,0:T(8,128)S(1)}) custom-call(s32[1]{0:T(128)S(6)} %copy.110.len_ref, f32[1024,1152]{1,0:T(8,128)} %copy-done, f32[1024,384]{1,0:T(8,128)S(1)} %copy-done.7, f32[1024,384]{1,0:T(8,128)} %copy-done.5, f32[1024,384]{1,0:T(8,128)} %copy-done.19, f32[2,2,24,3840]{3,2,1,0:T(8,128)} %get-tuple-element.67.refs_0_, ...), custom_call_target="tpu_custom_call" | custom-call | tf_op jit(solution)/shard_map/attend_back/pallas_call | solution.py:403
  359.6 16.4 %collective-permute-done.32.refs_1_ = f32[2,96,768]{2,1,0:T(8,128)S(1)} collective-permute-done((f32[2,96,768]{2,1,0:T(8,128)S(1)}, f32[2,96,768]{2,1,0:T(8,128)S(1)}, u32[]{:S(2)}, u32[]{:S(2)}) %collective-permute-start.32) | collective-permute-done | bytes 589856 | tf_op jit(solution)/shard_map/ppermute | solution.py:441
  384.0 2.6 plane_second.3
  391.3 11.0 %fusion.19.refs_2_ = f32[768,1152]{1,0:T(8,128)S(1)} fusion(f32[1024,1152]{1,0:T(8,128)S(1)} %bitcast.140, f32[512,768]{1,0:T(8,128)} %collective-permute-done.refs_1_, f32[512,768]{1,0:T(8,128)} %subtract_multiply_fusion.1.refs_1_, f32[]{:T(128)} %bitcast.43, pred[]{:T(512)S(6)} %eq.7), kind=kOutput, calls=%fused_computation.25 | convolution fusion | flops 5438963712 | bytes 11403269 | tf_op jit(solution)/shard_map/dot_general | solution.py:29
  408.3 4.0 collective-permute-done.38.refs_1_
  418.9 9.0 %fusion.16.refs_2_ = f32[1024,768]{1,0:T(8,128)S(1)} fusion(f32[768,1152]{1,0:T(8,128)S(1)} %bitcast.135, f32[1024,1152]{1,0:T(8,128)} %get-tuple-element.71.refs_3_, f32[]{:T(128)} %bitcast.46), kind=kOutput, calls=%fused_computation.19 | convolution fusion | flops 5436997632 | bytes 11403268 | tf_op jit(solution)/shard_map/dot_general | solution.py:39
  429.7 9.4 %collective-permute-done.39.refs_1_ = f32[4,2,24,1280]{3,2,1,0:T(8,128)} collective-permute-done((f32[4,2,24,1280]{3,2,1,0:T(8,128)}, f32[4,2,24,1280]{3,2,1,0:T(8,128)}, u32[]{:S(2)}, u32[]{:S(2)}) %collective-permute-start.39) | collective-permute-done | bytes 983072 | tf_op jit(solution)/shard_map/ppermute | solution.py:441
  443.2 2.3 collective-permute-start.45
  446.7 12.4 %fusion.5.refs_2_ = f32[1024,768]{1,0:T(8,128)S(1)} fusion(f32[1536,768]{1,0:T(8,128)} %bitcast.138, f32[1024,1536]{1,0:T(8,128)} %copy-done.78, f32[1536]{0:T(1024)S(1)} %broadcast_add_fusion), kind=kOutput, calls=%fused_computation.6 | convolution fusion | flops 7255621632 | bytes 14161920 | tf_op jit(solution)/shard_map/dot_general | solution.py:25
  467.5 3.1 fusion.65
  481.3 2.9 collective-permute-done.44.refs_1_
  (362 shorter events, 133.0 us)
Async XLA Ops:
  4.0 6.4 %collective-permute-start.1 = (f32[24,1280]{1,0:T(8,128)S(1)}, f32[24,1280]{1,0:T(8,128)S(1)}, u32[]{:S(2)}, u32[]{:S(2)}) collective-permute-start(f32[24,1280]{1,0:T(8,128)S(1)} %get-tuple-element.133), channel_id=1, source_target_pairs={{0,1},{1,0},{2,3},{3,2},{4,5},{5,4},{6,7},{7,6},{8,9},{9,8},{10,11... | collective-permute-start | bytes 368648 | tf_op jit(solution)/shard_map/ppermute | solution.py:441
  7.7 7.8 %collective-permute-start.7 = (f32[24,1536]{1,0:T(8,128)S(1)}, f32[24,1536]{1,0:T(8,128)S(1)}, u32[]{:S(2)}, u32[]{:S(2)}) collective-permute-start(f32[24,1536]{1,0:T(8,128)S(1)} %get-tuple-element.119), channel_id=1, source_target_pairs={{0,2},{1,3},{2,0},{3,1},{4,6},{5,7},{6,4},{7,5},{8,10},{9,11},{10,... | collective-permute-start | bytes 442376 | tf_op jit(solution)/shard_map/ppermute | solution.py:441
  9.6 65.5 %collective-permute-start = (f32[512,768]{1,0:T(8,128)}, f32[512,768]{1,0:T(8,128)}, u32[]{:S(2)}, u32[]{:S(2)}) collective-permute-start(f32[512,768]{1,0:T(8,128)} %subtract_multiply_fusion.1.refs_1_), channel_id=1, source_target_pairs={{0,1},{1,0},{2,3},{3,2},{4,5},{5,4},{6,7},{7,6},{8,9},{9,8},{10,11... | collective-permute-start | bytes 4718600 | tf_op jit(solution)/shard_map/ppermute | solution.py:441
  11.1 12.5 %collective-permute-start.2 = (f32[2,24,1280]{2,1,0:T(8,128)}, f32[2,24,1280]{2,1,0:T(8,128)S(1)}, u32[]{:S(2)}, u32[]{:S(2)}) collective-permute-start(f32[2,24,1280]{2,1,0:T(8,128)} %after.3), channel_id=1, source_target_pairs={{0,8},{1,9},{2,10},{3,11},{4,12},{5,13},{6,14},{7,15},{8,0},{9,1},... | collective-permute-start | bytes 737288 | tf_op jit(solution)/shard_map/ppermute | solution.py:441
  12.9 20.5 %collective-permute-start.3 = (f32[2,24,1280]{2,1,0:T(8,128)}, f32[2,24,1280]{2,1,0:T(8,128)S(1)}, u32[]{:S(2)}, u32[]{:S(2)}) collective-permute-start(f32[2,24,1280]{2,1,0:T(8,128)} %after.3), channel_id=1, source_target_pairs={{0,16},{1,17},{2,18},{3,19},{4,20},{5,21},{6,22},{7,23},{8,24},{9,... | collective-permute-start | bytes 737288 | tf_op jit(solution)/shard_map/ppermute | solution.py:441
  15.5 17.9 %collective-permute-start.4 = (f32[2,24,1280]{2,1,0:T(8,128)}, f32[2,24,1280]{2,1,0:T(8,128)S(1)}, u32[]{:S(2)}, u32[]{:S(2)}) collective-permute-start(f32[2,24,1280]{2,1,0:T(8,128)} %after.3), channel_id=1, source_target_pairs={{0,24},{1,25},{2,26},{3,27},{4,28},{5,29},{6,30},{7,31},{8,16},{9,... | collective-permute-start | bytes 737288 | tf_op jit(solution)/shard_map/ppermute | solution.py:441
  34.5 21.1 %collective-permute-start.8 = (f32[24,3840]{1,0:T(8,128)}, f32[24,3840]{1,0:T(8,128)S(1)}, u32[]{:S(2)}, u32[]{:S(2)}) collective-permute-start(f32[24,3840]{1,0:T(8,128)} %after.4.refs_0_), channel_id=1, source_target_pairs={{0,16},{1,17},{2,18},{3,19},{4,20},{5,21},{6,22},{7,23},{8,24},{9,... | collective-permute-start | bytes 1105928 | tf_op jit(solution)/shard_map/ppermute | solution.py:441
  39.9 22.4 %collective-permute-start.5 = (f32[4,2,24,1280]{3,2,1,0:T(8,128)}, f32[4,2,24,1280]{3,2,1,0:T(8,128)S(1)}, u32[]{:S(2)}, u32[]{:S(2)}) collective-permute-start(f32[4,2,24,1280]{3,2,1,0:T(8,128)} %pad_maximum_fusion.4.refs_1_.refs_0_), channel_id=1, source_target_pairs={{0,4},{1,5},{2,6},{3,7},{4,0},{5,1},{6,2},{7,3},{8,12},{9,13},{10,... | collective-permute-start | bytes 2949128 | tf_op jit(solution)/shard_map/ppermute | solution.py:441
  57.1 17.3 %collective-permute-start.9 = (f32[2,24,3840]{2,1,0:T(8,128)S(1)}, f32[2,24,3840]{2,1,0:T(8,128)S(1)}, u32[]{:S(2)}, u32[]{:S(2)}) collective-permute-start(f32[2,24,3840]{2,1,0:T(8,128)S(1)} %pair.2.refs_0_.refs_1_), channel_id=1, source_target_pairs={{0,8},{1,9},{2,10},{3,11},{4,12},{5,13},{6,14},{7,15},{8,0},{9,1},... | collective-permute-start | bytes 2211848 | tf_op jit(solution)/shard_map/ppermute | solution.py:441
  57.2 22.6 %collective-permute-start.6 = (f32[4,2,24,1280]{3,2,1,0:T(8,128)}, f32[4,2,24,1280]{3,2,1,0:T(8,128)}, u32[]{:S(2)}, u32[]{:S(2)}) collective-permute-start(f32[4,2,24,1280]{3,2,1,0:T(8,128)} %pad_maximum_fusion.4.refs_1_.refs_0_), channel_id=1, source_target_pairs={{0,2},{1,3},{2,0},{3,1},{4,6},{5,7},{6,4},{7,5},{8,10},{9,11},{10,... | collective-permute-start | bytes 2949128 | tf_op jit(solution)/shard_map/ppermute | solution.py:441
  76.7 3.1 collective-permute-start.10
  76.7 16.6 %collective-permute-start.11 = (f32[96,768]{1,0:T(8,128)}, f32[96,768]{1,0:T(8,128)S(1)}, u32[]{:S(2)}, u32[]{:S(2)}) collective-permute-start(f32[96,768]{1,0:T(8,128)} %after.5.refs_0_), channel_id=1, source_target_pairs={{0,16},{1,17},{2,18},{3,19},{4,20},{5,21},{6,22},{7,23},{8,24},{9,... | collective-permute-start | bytes 884744 | tf_op jit(solution)/shard_map/ppermute | solution.py:441
  76.7 60.0 %collective-permute-start.15 = (f32[4,24,3840]{2,1,0:T(8,128)S(1)}, f32[4,24,3840]{2,1,0:T(8,128)S(1)}, u32[]{:S(2)}, u32[]{:S(2)}) collective-permute-start(f32[4,24,3840]{2,1,0:T(8,128)S(1)} %pairs.2.refs_2_.refs_0_), channel_id=1, source_target_pairs={{0,1},{1,0},{2,3},{3,2},{4,5},{5,4},{6,7},{7,6},{8,9},{9,8},{10,11... | collective-permute-start | bytes 4423688 | tf_op jit(solution)/shard_map/ppermute | solution.py:441
  78.3 63.1 %collective-permute-start.14 = (f32[4,24,3840]{2,1,0:T(8,128)S(1)}, f32[4,24,3840]{2,1,0:T(8,128)}, u32[]{:S(2)}, u32[]{:S(2)}) collective-permute-start(f32[4,24,3840]{2,1,0:T(8,128)S(1)} %pairs.2.refs_2_.refs_0_), channel_id=1, source_target_pairs={{0,4},{1,5},{2,6},{3,7},{4,0},{5,1},{6,2},{7,3},{8,12},{9,13},{10,... | collective-permute-start | bytes 4423688 | tf_op jit(solution)/shard_map/ppermute | solution.py:441
  96.6 15.6 %collective-permute-start.12 = (f32[2,96,768]{2,1,0:T(8,128)}, f32[2,96,768]{2,1,0:T(8,128)S(1)}, u32[]{:S(2)}, u32[]{:S(2)}) collective-permute-start(f32[2,96,768]{2,1,0:T(8,128)} %pair.3.refs_0_), channel_id=1, source_target_pairs={{0,8},{1,9},{2,10},{3,11},{4,12},{5,13},{6,14},{7,15},{8,0},{9,1},... | collective-permute-start | bytes 1769480 | tf_op jit(solution)/shard_map/ppermute | solution.py:441
  114.9 46.3 %collective-permute-start.17 = (f32[4,96,768]{2,1,0:T(8,128)}, f32[4,96,768]{2,1,0:T(8,128)}, u32[]{:S(2)}, u32[]{:S(2)}) collective-permute-start(f32[4,96,768]{2,1,0:T(8,128)} %pairs.3.refs_0_), channel_id=1, source_target_pairs={{0,4},{1,5},{2,6},{3,7},{4,0},{5,1},{6,2},{7,3},{8,12},{9,13},{10,... | collective-permute-start | bytes 3538952 | tf_op jit(solution)/shard_map/ppermute | solution.py:441
  116.4 44.8 %collective-permute-start.18 = (f32[4,96,768]{2,1,0:T(8,128)}, f32[4,96,768]{2,1,0:T(8,128)}, u32[]{:S(2)}, u32[]{:S(2)}) collective-permute-start(f32[4,96,768]{2,1,0:T(8,128)} %pairs.3.refs_0_), channel_id=1, source_target_pairs={{0,1},{1,0},{2,3},{3,2},{4,5},{5,4},{6,7},{7,6},{8,9},{9,8},{10,11... | collective-permute-start | bytes 3538952 | tf_op jit(solution)/shard_map/ppermute | solution.py:441
  136.2 24.9 %collective-permute-start.13 = (f32[512,384]{1,0:T(8,128)}, f32[512,384]{1,0:T(8,128)}, u32[]{:S(2)}, u32[]{:S(2)}) collective-permute-start(f32[512,384]{1,0:T(8,128)} %get-tuple-element.113), channel_id=1, source_target_pairs={{0,1},{1,0},{2,3},{3,2},{4,5},{5,4},{6,7},{7,6},{8,9},{9,8},{10,11... | collective-permute-start | bytes 2359304 | tf_op jit(solution)/shard_map/ppermute | solution.py:441
  138.4 28.5 %collective-permute-start.16 = (f32[3,24,3840]{2,1,0:T(8,128)}, f32[3,24,3840]{2,1,0:T(8,128)}, u32[]{:S(2)}, u32[]{:S(2)}) collective-permute-start(f32[3,24,3840]{2,1,0:T(8,128)} %corner_first.1), channel_id=1, source_target_pairs={{0,4},{1,5},{2,6},{3,7},{4,0},{5,1},{6,2},{7,3},{8,12},{9,13},{10,... | collective-permute-start | bytes 3317768 | tf_op jit(solution)/shard_map/ppermute | solution.py:441
  165.0 9.4 %collective-permute-start.19 = (f32[1,24,3840]{2,1,0:T(8,128)S(1)}, f32[1,24,3840]{2,1,0:T(8,128)S(1)}, u32[]{:S(2)}, u32[]{:S(2)}) collective-permute-start(f32[1,24,3840]{2,1,0:T(8,128)S(1)} %get-tuple-element.58), channel_id=1, source_target_pairs={{0,1},{1,0},{2,3},{3,2},{4,5},{5,4},{6,7},{7,6},{8,9},{9,8},{10,11... | collective-permute-start | bytes 1105928 | tf_op jit(solution)/shard_map/ppermute | solution.py:441
  188.3 3.3 collective-permute-start.20
  188.4 17.5 %collective-permute-start.22 = (f32[512,768]{1,0:T(8,128)}, f32[512,768]{1,0:T(8,128)}, u32[]{:S(2)}, u32[]{:S(2)}) collective-permute-start(f32[512,768]{1,0:T(8,128)} %param.16), channel_id=1, source_target_pairs={{0,2},{1,3},{2,0},{3,1},{4,6},{5,7},{6,4},{7,5},{8,10},{9,11},{10,... | collective-permute-start | bytes 4718600 | tf_op jit(solution)/shard_map/ppermute | solution.py:441
  202.5 25.3 %collective-permute-start.21 = (f32[512,768]{1,0:T(8,128)}, f32[512,768]{1,0:T(8,128)}, u32[]{:S(2)}, u32[]{:S(2)}) collective-permute-start(f32[512,768]{1,0:T(8,128)} %multiply_add_fusion.2), channel_id=1, source_target_pairs={{0,2},{1,3},{2,0},{3,1},{4,6},{5,7},{6,4},{7,5},{8,10},{9,11},{10,... | collective-permute-start | bytes 4718600 | tf_op jit(solution)/shard_map/ppermute | solution.py:441
  202.6 22.2 %collective-permute-start.23 = (f32[3,96,768]{2,1,0:T(8,128)}, f32[3,96,768]{2,1,0:T(8,128)}, u32[]{:S(2)}, u32[]{:S(2)}) collective-permute-start(f32[3,96,768]{2,1,0:T(8,128)} %get-tuple-element.61), channel_id=1, source_target_pairs={{0,4},{1,5},{2,6},{3,7},{4,0},{5,1},{6,2},{7,3},{8,12},{9,13},{10,... | collective-permute-start | bytes 2654216 | tf_op jit(solution)/shard_map/ppermute | solution.py:441
  209.7 9.2 %collective-permute-start.24 = (f32[1,96,768]{2,1,0:T(8,128)}, f32[1,96,768]{2,1,0:T(8,128)S(1)}, u32[]{:S(2)}, u32[]{:S(2)}) collective-permute-start(f32[1,96,768]{2,1,0:T(8,128)} %copy-done.40), channel_id=1, source_target_pairs={{0,1},{1,0},{2,3},{3,2},{4,5},{5,4},{6,7},{7,6},{8,9},{9,8},{10,11... | collective-permute-start | bytes 884744 | tf_op jit(solution)/shard_map/ppermute | solution.py:441
  261.2 17.8 %collective-permute-start.25 = (f32[512,768]{1,0:T(8,128)}, f32[512,768]{1,0:T(8,128)}, u32[]{:S(2)}, u32[]{:S(2)}) collective-permute-start(f32[512,768]{1,0:T(8,128)} %slice.126), channel_id=1, source_target_pairs={{0,2},{1,3},{2,0},{3,1},{4,6},{5,7},{6,4},{7,5},{8,10},{9,11},{10,... | collective-permute-start | bytes 4718600 | tf_op jit(solution)/shard_map/ppermute | solution.py:441
  276.2 46.4 %collective-permute-start.27 = (f32[2,2,96,768]{3,2,1,0:T(8,128)}, f32[2,2,96,768]{3,2,1,0:T(8,128)}, u32[]{:S(2)}, u32[]{:S(2)}) collective-permute-start(f32[2,2,96,768]{3,2,1,0:T(8,128)} %get-tuple-element.63), channel_id=1, source_target_pairs={{0,4},{1,5},{2,6},{3,7},{4,0},{5,1},{6,2},{7,3},{8,12},{9,13},{10,... | collective-permute-start | bytes 3538952 | tf_op jit(solution)/shard_map/ppermute | solution.py:441
  276.8 45.8 %collective-permute-start.28 = (f32[2,2,96,768]{3,2,1,0:T(8,128)}, f32[2,2,96,768]{3,2,1,0:T(8,128)}, u32[]{:S(2)}, u32[]{:S(2)}) collective-permute-start(f32[2,2,96,768]{3,2,1,0:T(8,128)} %get-tuple-element.64), channel_id=1, source_target_pairs={{0,1},{1,0},{2,3},{3,2},{4,5},{5,4},{6,7},{7,6},{8,9},{9,8},{10,11... | collective-permute-start | bytes 3538952 | tf_op jit(solution)/shard_map/ppermute | solution.py:441
  289.3 36.6 %collective-permute-start.26 = (f32[4,2,2,24,768]{4,3,2,1,0:T(8,128)}, f32[4,2,2,24,768]{4,3,2,1,0:T(8,128)S(1)}, u32[]{:S(2)}, u32[]{:S(2)}) collective-permute-start(f32[4,2,2,24,768]{4,3,2,1,0:T(8,128)} %dynamic-slice_bitcast_fusion), channel_id=1, source_target_pairs={{0,2},{1,3},{2,0},{3,1},{4,6},{5,7},{6,4},{7,5},{8,10},{9,11},{10,... | collective-permute-start | bytes 3538952 | tf_op jit(solution)/shard_map/ppermute | solution.py:441
  298.6 23.4 %collective-permute-start.29 = (f32[512,384]{1,0:T(8,128)S(1)}, f32[512,384]{1,0:T(8,128)S(1)}, u32[]{:S(2)}, u32[]{:S(2)}) collective-permute-start(f32[512,384]{1,0:T(8,128)S(1)} %get-tuple-element.109.refs_0_), channel_id=1, source_target_pairs={{0,1},{1,0},{2,3},{3,2},{4,5},{5,4},{6,7},{7,6},{8,9},{9,8},{10,11... | collective-permute-start | bytes 2359304 | tf_op jit(solution)/shard_map/ppermute | solution.py:441
  328.2 55.8 %collective-permute-start.30 = (f32[2,2,24,3840]{3,2,1,0:T(8,128)}, f32[2,2,24,3840]{3,2,1,0:T(8,128)}, u32[]{:S(2)}, u32[]{:S(2)}) collective-permute-start(f32[2,2,24,3840]{3,2,1,0:T(8,128)} %get-tuple-element.67.refs_0_), channel_id=1, source_target_pairs={{0,4},{1,5},{2,6},{3,7},{4,0},{5,1},{6,2},{7,3},{8,12},{9,13},{10,... | collective-permute-start | bytes 4423688 | tf_op jit(solution)/shard_map/ppermute | solution.py:441
  329.7 54.3 %collective-permute-start.31 = (f32[2,2,24,3840]{3,2,1,0:T(8,128)}, f32[2,2,24,3840]{3,2,1,0:T(8,128)}, u32[]{:S(2)}, u32[]{:S(2)}) collective-permute-start(f32[2,2,24,3840]{3,2,1,0:T(8,128)} %get-tuple-element.68.refs_1_), channel_id=1, source_target_pairs={{0,1},{1,0},{2,3},{3,2},{4,5},{5,4},{6,7},{7,6},{8,9},{9,8},{10,11... | collective-permute-start | bytes 4423688 | tf_op jit(solution)/shard_map/ppermute | solution.py:441
  331.3 44.7 %collective-permute-start.32 = (f32[2,96,768]{2,1,0:T(8,128)S(1)}, f32[2,96,768]{2,1,0:T(8,128)S(1)}, u32[]{:S(2)}, u32[]{:S(2)}) collective-permute-start(f32[2,96,768]{2,1,0:T(8,128)S(1)} %get-tuple-element.65.refs_3_.refs_2_), channel_id=1, source_target_pairs={{0,1},{1,0},{2,3},{3,2},{4,5},{5,4},{6,7},{7,6},{8,9},{9,8},{10,11... | collective-permute-start | bytes 1769480 | tf_op jit(solution)/shard_map/ppermute | solution.py:441
  331.8 44.9 %collective-permute-start.33 = (f32[2,96,768]{2,1,0:T(8,128)}, f32[2,96,768]{2,1,0:T(8,128)S(1)}, u32[]{:S(2)}, u32[]{:S(2)}) collective-permute-start(f32[2,96,768]{2,1,0:T(8,128)} %get-tuple-element.66.refs_4_.refs_3_), channel_id=1, source_target_pairs={{0,4},{1,5},{2,6},{3,7},{4,0},{5,1},{6,2},{7,3},{8,12},{9,13},{10,... | collective-permute-start | bytes 1769480 | tf_op jit(solution)/shard_map/ppermute | solution.py:441
  386.7 16.6 %collective-permute-start.34 = (f32[2,24,3840]{2,1,0:T(8,128)S(1)}, f32[2,24,3840]{2,1,0:T(8,128)S(1)}, u32[]{:S(2)}, u32[]{:S(2)}) collective-permute-start(f32[2,24,3840]{2,1,0:T(8,128)S(1)} %get-tuple-element.74.refs_0_), channel_id=1, source_target_pairs={{0,1},{1,0},{2,3},{3,2},{4,5},{5,4},{6,7},{7,6},{8,9},{9,8},{10,11... | collective-permute-start | bytes 2211848 | tf_op jit(solution)/shard_map/ppermute | solution.py:441
  388.3 16.3 %collective-permute-start.35 = (f32[2,24,3840]{2,1,0:T(8,128)S(1)}, f32[2,24,3840]{2,1,0:T(8,128)S(1)}, u32[]{:S(2)}, u32[]{:S(2)}) collective-permute-start(f32[2,24,3840]{2,1,0:T(8,128)S(1)} %get-tuple-element.75.refs_1_), channel_id=1, source_target_pairs={{0,4},{1,5},{2,6},{3,7},{4,0},{5,1},{6,2},{7,3},{8,12},{9,13},{10,... | collective-permute-start | bytes 2211848 | tf_op jit(solution)/shard_map/ppermute | solution.py:441
  388.8 13.4 %collective-permute-start.36 = (f32[2,96,768]{2,1,0:T(8,128)S(1)}, f32[2,96,768]{2,1,0:T(8,128)S(1)}, u32[]{:S(2)}, u32[]{:S(2)}) collective-permute-start(f32[2,96,768]{2,1,0:T(8,128)S(1)} %get-tuple-element.72.refs_5_), channel_id=1, source_target_pairs={{0,8},{1,9},{2,10},{3,11},{4,12},{5,13},{6,14},{7,15},{8,0},{9,1},... | collective-permute-start | bytes 1769480 | tf_op jit(solution)/shard_map/ppermute | solution.py:441
  408.2 4.0 collective-permute-start.38
  415.0 24.1 %collective-permute-start.39 = (f32[4,2,24,1280]{3,2,1,0:T(8,128)}, f32[4,2,24,1280]{3,2,1,0:T(8,128)}, u32[]{:S(2)}, u32[]{:S(2)}) collective-permute-start(f32[4,2,24,1280]{3,2,1,0:T(8,128)} %get-tuple-element.84.refs_0_), channel_id=1, source_target_pairs={{0,4},{1,5},{2,6},{3,7},{4,0},{5,1},{6,2},{7,3},{8,12},{9,13},{10,... | collective-permute-start | bytes 2949128 | tf_op jit(solution)/shard_map/ppermute | solution.py:441
  416.3 48.5 %collective-permute-start.47 = (f32[96,768]{1,0:T(8,128)}, f32[96,768]{1,0:T(8,128)}, u32[]{:S(2)}, u32[]{:S(2)}) collective-permute-start(f32[96,768]{1,0:T(8,128)} %copy-done.35), channel_id=1, source_target_pairs={{0,16},{1,17},{2,18},{3,19},{4,20},{5,21},{6,22},{7,23},{8,24},{9,... | collective-permute-start | bytes 884744 | tf_op jit(solution)/shard_map/ppermute | solution.py:441
  416.6 25.4 %collective-permute-start.37 = (f32[2,24,3840]{2,1,0:T(8,128)}, f32[2,24,3840]{2,1,0:T(8,128)S(1)}, u32[]{:S(2)}, u32[]{:S(2)}) collective-permute-start(f32[2,24,3840]{2,1,0:T(8,128)} %copy-done.28), channel_id=1, source_target_pairs={{0,8},{1,9},{2,10},{3,11},{4,12},{5,13},{6,14},{7,15},{8,0},{9,1},... | collective-permute-start | bytes 2211848 | tf_op jit(solution)/shard_map/ppermute | solution.py:441
  429.2 38.3 %collective-permute-start.41 = (f32[512,768]{1,0:T(8,128)}, f32[512,768]{1,0:T(8,128)}, u32[]{:S(2)}, u32[]{:S(2)}) collective-permute-start(f32[512,768]{1,0:T(8,128)} %constant_dynamic-slice_fusion.1), channel_id=1, source_target_pairs={{0,1},{1,0},{2,3},{3,2},{4,5},{5,4},{6,7},{7,6},{8,9},{9,8},{10,11... | collective-permute-start | bytes 4718600 | tf_op jit(solution)/shard_map/ppermute | solution.py:441
  440.5 20.3 %collective-permute-start.42 = (f32[2,2,24,1280]{3,2,1,0:T(8,128)S(1)}, f32[2,2,24,1280]{3,2,1,0:T(8,128)S(1)}, u32[]{:S(2)}, u32[]{:S(2)}) collective-permute-start(f32[2,2,24,1280]{3,2,1,0:T(8,128)S(1)} %get-tuple-element.85.refs_2_), channel_id=1, source_target_pairs={{0,8},{1,9},{2,10},{3,11},{4,12},{5,13},{6,14},{7,15},{8,0},{9,1},... | collective-permute-start | bytes 1474568 | tf_op jit(solution)/shard_map/ppermute | solution.py:441
  443.2 19.1 %collective-permute-start.45 = (f32[24,3840]{1,0:T(8,128)S(1)}, f32[24,3840]{1,0:T(8,128)S(1)}, u32[]{:S(2)}, u32[]{:S(2)}) collective-permute-start(f32[24,3840]{1,0:T(8,128)S(1)} %get-tuple-element.86.refs_0_), channel_id=1, source_target_pairs={{0,16},{1,17},{2,18},{3,19},{4,20},{5,21},{6,22},{7,23},{8,24},{9,... | collective-permute-start | bytes 1105928 | tf_op jit(solution)/shard_map/ppermute | solution.py:441
  460.3 18.8 %collective-permute-start.40 = (f32[512,768]{1,0:T(8,128)}, f32[512,768]{1,0:T(8,128)}, u32[]{:S(2)}, u32[]{:S(2)}) collective-permute-start(f32[512,768]{1,0:T(8,128)} %slice.128), channel_id=1, source_target_pairs={{0,2},{1,3},{2,0},{3,1},{4,6},{5,7},{6,4},{7,5},{8,10},{9,11},{10,... | collective-permute-start | bytes 4718600 | tf_op jit(solution)/shard_map/ppermute | solution.py:441
  462.1 14.4 %collective-permute-start.43 = (f32[2,24,1280]{2,1,0:T(8,128)}, f32[2,24,1280]{2,1,0:T(8,128)}, u32[]{:S(2)}, u32[]{:S(2)}) collective-permute-start(f32[2,24,1280]{2,1,0:T(8,128)} %get-tuple-element.89.refs_2_), channel_id=1, source_target_pairs={{0,16},{1,17},{2,18},{3,19},{4,20},{5,21},{6,22},{7,23},{8,24},{9,... | collective-permute-start | bytes 737288 | tf_op jit(solution)/shard_map/ppermute | solution.py:441
  464.3 8.1 %collective-permute-start.46 = (f32[24,1536]{1,0:T(8,128)}, f32[24,1536]{1,0:T(8,128)}, u32[]{:S(2)}, u32[]{:S(2)}) collective-permute-start(f32[24,1536]{1,0:T(8,128)} %get-tuple-element.117), channel_id=1, source_target_pairs={{0,2},{1,3},{2,0},{3,1},{4,6},{5,7},{6,4},{7,5},{8,10},{9,11},{10,... | collective-permute-start | bytes 442376 | tf_op jit(solution)/shard_map/ppermute | solution.py:441
  478.5 5.6 %collective-permute-start.44 = (f32[24,1280]{1,0:T(8,128)S(1)}, f32[24,1280]{1,0:T(8,128)S(1)}, u32[]{:S(2)}, u32[]{:S(2)}) collective-permute-start(f32[24,1280]{1,0:T(8,128)S(1)} %get-tuple-element.91), channel_id=1, source_target_pairs={{0,1},{1,0},{2,3},{3,2},{4,5},{5,4},{6,7},{7,6},{8,9},{9,8},{10,11... | collective-permute-start | bytes 368648 | tf_op jit(solution)/shard_map/ppermute | solution.py:441
  (83 other events, 516.2 us)

commit v5 on v4

--- a/solution.py
+++ b/solution.py
@@ -391,7 +391,7 @@
         +[pl.BlockSpec(memory_space=pl.ANY)]*len(earlier),
         out_specs=[block(PAIR),block(PAIR)],
         out_shape=[jax.ShapeDtypeStruct((rows,pairs*PAIR),f32)]*2,
-        compiler_params=pltpu.CompilerParams(vmem_limit_bytes=48*2**20),
+        compiler_params=pltpu.CompilerParams(vmem_limit_bytes=30*2**20),
         cost_estimate=pl.CostEstimate(flops=0,bytes_accessed=0,transcendentals=0),
         name="attend",
     )(seq_len,qkv,*earlier)
@@ -407,7 +407,7 @@
         +[pl.BlockSpec(memory_space=pl.ANY)]*len(earlier),
         out_specs=[block(3*PAIR),pl.BlockSpec((8,3*PAIR),lambda j:(0,j))],
         out_shape=[jax.ShapeDtypeStruct((rows,cols),f32),jax.ShapeDtypeStruct((8,cols),f32)],
-        compiler_params=pltpu.CompilerParams(vmem_limit_bytes=48*2**20),
+        compiler_params=pltpu.CompilerParams(vmem_limit_bytes=30*2**20),
         cost_estimate=pl.CostEstimate(flops=0,bytes_accessed=0,transcendentals=0),
         name="attend_back",
     )(seq_len,qkv,d_out,out,lse,*earlier)
@@ -644,12 +644,11 @@
     return local_call(kernel, "sum_after", where, [own, arrived], earlier, [own.shape])[0]
 
 
-def zero_after(where, *earlier):
+def zeros_after(where, cols, *earlier):
     def kernel(place, zero):
         zero[...] = jnp.zeros_like(zero)
 
-    zero, = local_call(kernel, "zero_after", where, [], earlier, [(8, PAIR)])
-    return zero[0, 0]
+    return local_call(kernel, "zeros_after", where, [], earlier, [(1, cols)])[0]
 
 
 def copy_after(where, values, earlier):
@@ -872,7 +871,7 @@
         axis=1,
     )
     small = jnp.pad(small, ((0, 0), (0, 6), (0, 0)))
-    chip_a = matmul_tn(both_normed + zero_after(where, sent, small), d_pre).reshape(COLUMNS, 2, 2, 2, shard, hidden)
+    chip_a = matmul_tn(both_normed + zeros_after(where, D, sent, small), d_pre).reshape(COLUMNS, 2, 2, 2, shard, hidden)
     def join_rows(place, own, arrived, out):
         y = place[3]
         out[pl.ds(y * rows, rows)] = own[...]
@@ -900,7 +899,7 @@
     kept_a, *sent_a = plane_second(where, chip_a, block_a, *side_a, 2, [sent_b])
     corner_a = swap(sent_a[0], over_y), swap(sent_a[1], over_x)
 
-    moved = matmul_tn(normed_one + zero_after(where, *sent_a), d_proj)
+    moved = matmul_tn(normed_one + zeros_after(where, D, *sent_a), d_proj)
     own_b, sent_b = column_second(where, pair_b, swap(sent_b, over_z[1]), [moved])
     pair_a, sent_a = column_first(where, block_a, kept_a, *corner_a, 2, [sent_b])
     last_lane = wide + PAIR - 1
@@ -972,7 +971,7 @@
         (),
         [(COLUMNS, 2) + block] * 2,
     )
-    d_norm = matmul_nt(d_proj + zero_after(where, second), w_qkv)
+    d_norm = matmul_nt(d_proj + zeros_after(where, wide, second), w_qkv)
     d_norm_sent = rows_of(d_norm, 1 - y)
 
     def line_sum(place, kept, arrived, pair, sent):
@@ -985,7 +984,9 @@
         [(2, 2) + block] * 2,
     )
     own_a, sent_a = column_second(where, pair_a, swap(sent_a, over_z[1]), [sent_qkv])
-    down_part = matmul(gelu_forward(raw_act + (b_up + zero_after(where, sent_a))), w_down)
+    down_part = matmul(
+        gelu_forward(raw_act + (b_up + zeros_after(where, hidden, sent_a))), w_down
+    )
     layer_output = middle + down_part[:rows] + swap(down_part[rows:], over_core) + b_down
     own_qkv, sent_qkv = column_second(
         where, pair_qkv, swap(sent_qkv, over_z[1]), [down_part]

time: 487 us -> 478 us (0.982); the launches traced: 488 us -> 473 us
  Pallas kernels: 104 us -> 89.5 us
    pallas_call x4, Pallas kernels: 22.8 us -> 11.9 us  [assemble(): pl.pallas_call(functools.partial(assemble_kernel, (len(pieces), copies)),...]
    unnamed x168 -> x184, local copies, waits for them, and re-layouts: 24.9 us -> 26.8 us
  transfers between devices with their start and end apart: 48 -> 48, of which waited for: 21 -> 22; matrix products, arithmetic and copies ran while one was open for 28% -> 29% of each run, Pallas kernels for 16% -> 16%
where the time goes in v5:
time: 478 us; the launch traced here: 473 us
  waiting for transfers between devices  137 us (29%)
  matrix products  110 us (23%)
  Pallas kernels  89.5 us (19%)
  local copies, waits for them, and re-layouts  59.2 us (12%)
  starting transfers between devices  42.8 us (9%)
  other arithmetic  30.8 us (6%)
    ppermute x48, waiting for transfers between devices, swap(): return lax.ppermute(values, AXES, pairs)  137 us
    ppermute x48, starting transfers between devices, swap(): return lax.ppermute(values, AXES, pairs)  42.8 us
    dot_general x4, matrix products, matmul_tn(): lax.dot_general(left, right, (((0,), (0,)), ((), ())), precision=top_prec...  39.9 us
    dot_general x4, matrix products, matmul(): jnp.dot(left, right, precision=top_prec, preferred_element_type=jnp.float32)  38.2 us
    pallas_call x28, Pallas kernels, local_call(): pl.pallas_call(call, in_specs=[pl.BlockSpec(memory_space=pltpu.SMEM)] + [...  37.4 us
    dot_general x4, matrix products, matmul_nt(): lax.dot_general(left, right, (((1,), (1,)), ((), ())), precision=top_prec...  32.3 us
    unnamed x184, local copies, waits for them, and re-layouts  26.8 us
    pallas_call x1, Pallas kernels, attend_back(): pl.pallas_call(attend_back_kernel, grid=(pairs,), in_specs=[pl.BlockSpec(...  25.2 us
  transfers between devices with their start and end apart: 48, of which 22 were waited for; matrix products, arithmetic and copies ran while one was open for 29% of the time, Pallas kernels for 16%

profile of v5, /device:TPU:0, one launch (start us, length us, event | category | flops | bytes accessed | tf_op | source)
XLA Modules:
  0.0 472.9 jit_solution(6132427543398716077)
XLA Ops:
  4.0 3.0 collective-permute-start.1
  12.9 2.6 collective-permute-start.3
  16.9 6.7 %collective-permute-done.2 = f32[2,24,1280]{2,1,0:T(8,128)S(1)} collective-permute-done((f32[2,24,1280]{2,1,0:T(8,128)}, f32[2,24,1280]{2,1,0:T(8,128)S(1)}, u32[]{:S(2)}, u32[]{:S(2)}) %collective-permute-start.2) | collective-permute-done | bytes 245792 | tf_op jit(solution)/shard_map/ppermute | solution.py:441
  23.6 9.8 %collective-permute-done.3 = f32[2,24,1280]{2,1,0:T(8,128)S(1)} collective-permute-done((f32[2,24,1280]{2,1,0:T(8,128)}, f32[2,24,1280]{2,1,0:T(8,128)S(1)}, u32[]{:S(2)}, u32[]{:S(2)}) %collective-permute-start.3) | collective-permute-done | bytes 245792 | tf_op jit(solution)/shard_map/ppermute | solution.py:441
  34.5 5.4 %collective-permute-start.8 = (f32[24,3840]{1,0:T(8,128)}, f32[24,3840]{1,0:T(8,128)S(1)}, u32[]{:S(2)}, u32[]{:S(2)}) collective-permute-start(f32[24,3840]{1,0:T(8,128)} %after.4.refs_0_), channel_id=1, source_target_pairs={{0,16},{1,17},{2,18},{3,19},{4,20},{5,21},{6,22},{7,23},{8,24},{9,... | collective-permute-start | bytes 1105928 | tf_op jit(solution)/shard_map/ppermute | solution.py:441
  41.5 14.1 %collective-permute-done.8.refs_1_ = f32[24,3840]{1,0:T(8,128)S(1)} collective-permute-done((f32[24,3840]{1,0:T(8,128)}, f32[24,3840]{1,0:T(8,128)S(1)}, u32[]{:S(2)}, u32[]{:S(2)}) %collective-permute-start.8) | collective-permute-done | bytes 368672 | tf_op jit(solution)/shard_map/ppermute | solution.py:441
  57.3 5.0 %collective-permute-done.5.refs_2_.refs_0_.refs_1_ = f32[4,2,24,1280]{3,2,1,0:T(8,128)S(1)} collective-permute-done((f32[4,2,24,1280]{3,2,1,0:T(8,128)}, f32[4,2,24,1280]{3,2,1,0:T(8,128)S(1)}, u32[]{:S(2)}, u32[]{:S(2)}) %collective-permute-start.5) | collective-permute-done | bytes 983072 | tf_op jit(solution)/shard_map/ppermute | solution.py:441
  62.3 12.2 %collective-permute-done.9.refs_1_ = f32[2,24,3840]{2,1,0:T(8,128)S(1)} collective-permute-done((f32[2,24,3840]{2,1,0:T(8,128)S(1)}, f32[2,24,3840]{2,1,0:T(8,128)S(1)}, u32[]{:S(2)}, u32[]{:S(2)}) %collective-permute-start.9) | collective-permute-done | bytes 737312 | tf_op jit(solution)/shard_map/ppermute | solution.py:441
  81.0 3.3 assemble.4
  88.2 5.1 %collective-permute-done.11.refs_1_ = f32[96,768]{1,0:T(8,128)S(1)} collective-permute-done((f32[96,768]{1,0:T(8,128)}, f32[96,768]{1,0:T(8,128)S(1)}, u32[]{:S(2)}, u32[]{:S(2)}) %collective-permute-start.11) | collective-permute-done | bytes 294944 | tf_op jit(solution)/shard_map/ppermute | solution.py:441
  99.8 10.5 %convolution_add_fusion.refs_2_.qkv_ref = f32[1024,1152]{1,0:T(8,128)S(1)} fusion(f32[768,1152]{1,0:T(8,128)} %bitcast.132, f32[1152]{0:T(1024)} %add.222, f32[512,768]{1,0:T(8,128)} %collective-permute-done.refs_1_, f32[512,768]{1,0:T(8,128)} %subtract_multiply_fusion.1.refs_1_, f32[768]{0:T(1024)S(1)} %add.219, f32[768]{0:T(1024)S(1)} %mul.147, pred[]{:T(512)S(6)} %eq.7), kind=kOutput, calls=%fused_computation.21 | convolution fusion | flops 5440929792 | bytes 11414017 | tf_op jit(solution)/shard_map/dot_general | solution.py:25
  118.0 2.3 copy-done.1
  120.4 15.0 %attend.1 = (f32[1024,384]{1,0:T(8,128)S(1)}, f32[1024,384]{1,0:T(8,128)S(1)}) custom-call(s32[1]{0:T(128)S(6)} %copy.114.len_ref, f32[1024,1152]{1,0:T(8,128)S(1)} %copy-done.1, f32[4,96,768]{2,1,0:T(8,128)} %pairs.3.refs_0_), custom_call_target="tpu_custom_call" | custom-call | tf_op jit(solution)/shard_map/attend/pallas_call | solution.py:387
  142.2 18.2 %collective-permute-done.13.refs_3_ = f32[512,384]{1,0:T(8,128)} collective-permute-done((f32[512,384]{1,0:T(8,128)}, f32[512,384]{1,0:T(8,128)}, u32[]{:S(2)}, u32[]{:S(2)}) %collective-permute-start.13) | collective-permute-done | bytes 786464 | tf_op jit(solution)/shard_map/ppermute | solution.py:441
  160.4 3.1 corner_rest.1
  166.0 7.2 %collective-permute-done.19.refs_4_ = f32[1,24,3840]{2,1,0:T(8,128)S(1)} collective-permute-done((f32[1,24,3840]{2,1,0:T(8,128)S(1)}, f32[1,24,3840]{2,1,0:T(8,128)S(1)}, u32[]{:S(2)}, u32[]{:S(2)}) %collective-permute-start.19) | collective-permute-done | bytes 368672 | tf_op jit(solution)/shard_map/ppermute | solution.py:441
  173.3 2.9 assemble.5
  177.0 2.4 collective-permute-done.20
  179.4 2.8 maximum_select_fusion.1
  184.7 3.8 fusion.69
  191.0 2.8 fusion.67
  193.8 2.7 constant_dynamic-update-slice_fusion
  199.0 2.9 assemble.6
  202.8 3.9 collective-permute-done.24.refs_4_
  206.7 6.0 %collective-permute-done.23.refs_3_ = f32[3,96,768]{2,1,0:T(8,128)} collective-permute-done((f32[3,96,768]{2,1,0:T(8,128)}, f32[3,96,768]{2,1,0:T(8,128)}, u32[]{:S(2)}, u32[]{:S(2)}) %collective-permute-start.23) | collective-permute-done | bytes 884768 | tf_op jit(solution)/shard_map/ppermute | solution.py:441
  212.7 2.9 assemble.7
  215.6 11.5 %fusion.30 = f32[1024,1536]{1,0:T(8,128)S(1)} fusion(f32[768,1536]{1,0:T(8,128)S(1)} %bitcast.145, f32[512,768]{1,0:T(8,128)} %collective-permute-done.21, f32[512,768]{1,0:T(8,128)} %multiply_add_fusion.2), kind=kOutput, calls=%fused_computation.36 | convolution fusion | flops 7248543744 | bytes 14155776 | tf_op jit(solution)/shard_map/dot_general | solution.py:25
  227.1 12.8 %fusion.70 = (f32[1536]{0:T(1024)S(1)}, f32[1024,1536]{1,0:T(8,128)S(1)}) fusion(f32[1024,1536]{1,0:T(8,128)S(1)} %fusion.30, f32[1536]{0:T(1024)S(1)} %add.235, f32[1024,768]{1,0:T(8,128)} %constant_dynamic-update-slice_fusion, f32[1536,768]{1,0:T(8,128)S(1)} %bitcast.135), kind=kOutput, calls=%fused_computation.159 | convolution fusion | flops 7265057280 | bytes 20459520 | tf_op jit(solution)/shard_map/dot_general | solution.py:39
  239.9 7.8 %fusion.71 = f32[1024,768]{1,0:T(8,128)S(1)} fusion(f32[1024,1536]{1,0:T(8,128)S(1)} %get-tuple-element.139, f32[768,1536]{1,0:T(8,128)S(1)} %bitcast.146), kind=kOutput, calls=%fused_computation.160 | convolution fusion | flops 7247757312 | bytes 14155776 | tf_op jit(solution)/shard_map/dot_general | solution.py:39
  249.3 11.9 %fusion.12 = f32[1536,768]{1,0:T(8,128)S(1)} fusion(f32[1024,768]{1,0:T(8,128)} %constant_dynamic-update-slice_fusion, f32[1024,1536]{1,0:T(8,128)} %copy-done.88, f32[1536]{0:T(1024)S(1)} %add.235), kind=kOutput, calls=%fused_computation.13 | convolution fusion | flops 7255621632 | bytes 14161920 | tf_op jit(solution)/shard_map/dot_general | solution.py:29
  266.8 2.8 multiply_reduce_fusion.1
  269.7 2.6 fusion.66
  272.3 4.2 fusion.42
  278.7 3.3 fusion.34
  285.4 2.7 dynamic-slice_bitcast_fusion.1
  290.6 12.8 %fusion.21 = f32[768,1536]{1,0:T(8,128)S(1)} fusion(f32[1024,1536]{1,0:T(8,128)} %copy-done.87, f32[512,768]{1,0:T(8,128)} %collective-permute-done.21, f32[512,768]{1,0:T(8,128)} %multiply_add_fusion.2, f32[768]{0:T(1024)} %reduce), kind=kOutput, calls=%fused_computation.27 | convolution fusion | flops 7249330176 | bytes 14158848 | tf_op jit(solution)/shard_map/dot_general | solution.py:29
  303.4 6.5 %collective-permute-done.29.refs_1_ = f32[512,384]{1,0:T(8,128)} collective-permute-done((f32[512,384]{1,0:T(8,128)}, f32[512,384]{1,0:T(8,128)}, u32[]{:S(2)}, u32[]{:S(2)}) %collective-permute-start.29) | collective-permute-done | bytes 786464 | tf_op jit(solution)/shard_map/ppermute | solution.py:441
  311.2 2.3 copy-done.3
  320.4 25.2 %attend_back.1 = (f32[1024,1152]{1,0:T(8,128)S(1)}, f32[8,1152]{1,0:T(8,128)S(1)}) custom-call(s32[1]{0:T(128)S(6)} %copy.114.len_ref, f32[1024,1152]{1,0:T(8,128)S(1)} %bitcast.126, f32[1024,384]{1,0:T(8,128)S(1)} %join_rows.1.refs_3_.do_ref, f32[1024,384]{1,0:T(8,128)S(1)} %copy-done.8, f32[1024,384]{1,0:T(8,128)S(1)} %copy-done.22, ...), custom_call_target="tpu_custom_call" | custom-call | tf_op jit(solution)/shard_map/attend_back/pallas_call | solution.py:403
  345.7 18.1 %collective-permute-done.32.refs_1_ = f32[2,96,768]{2,1,0:T(8,128)S(1)} collective-permute-done((f32[2,96,768]{2,1,0:T(8,128)S(1)}, f32[2,96,768]{2,1,0:T(8,128)S(1)}, u32[]{:S(2)}, u32[]{:S(2)}) %collective-permute-start.32) | collective-permute-done | bytes 589856 | tf_op jit(solution)/shard_map/ppermute | solution.py:441
  372.7 11.0 %fusion.19.refs_2_ = f32[768,1152]{1,0:T(8,128)S(1)} fusion(f32[1024,1152]{1,0:T(8,128)} %copy-done.15, f32[512,768]{1,0:T(8,128)} %collective-permute-done.refs_1_, f32[512,768]{1,0:T(8,128)} %subtract_multiply_fusion.1.refs_1_, f32[768]{0:T(1024)S(1)} %reduce.1, pred[]{:T(512)S(6)} %eq.7), kind=kOutput, calls=%fused_computation.25 | convolution fusion | flops 5438963712 | bytes 11406337 | tf_op jit(solution)/shard_map/dot_general | solution.py:29
  392.3 4.0 collective-permute-done.38.refs_1_
  403.8 8.3 %fusion.16.refs_2_ = f32[1024,768]{1,0:T(8,128)S(1)} fusion(f32[768,1152]{1,0:T(8,128)S(1)} %bitcast.133, f32[1024,1152]{1,0:T(8,128)} %copy-done.15, f32[1152]{0:T(1024)} %reduce.2), kind=kOutput, calls=%fused_computation.19 | convolution fusion | flops 5436997632 | bytes 11407872 | tf_op jit(solution)/shard_map/dot_general | solution.py:39
  414.0 9.2 %collective-permute-done.39.refs_1_ = f32[4,2,24,1280]{3,2,1,0:T(8,128)} collective-permute-done((f32[4,2,24,1280]{3,2,1,0:T(8,128)}, f32[4,2,24,1280]{3,2,1,0:T(8,128)}, u32[]{:S(2)}, u32[]{:S(2)}) %collective-permute-start.39) | collective-permute-done | bytes 983072 | tf_op jit(solution)/shard_map/ppermute | solution.py:441
  429.0 2.3 collective-permute-start.45
  431.3 12.4 %fusion.5.refs_2_ = f32[1024,768]{1,0:T(8,128)S(1)} fusion(f32[1536,768]{1,0:T(8,128)} %bitcast.136, f32[1024,1536]{1,0:T(8,128)} %copy-done.88, f32[1536]{0:T(1024)S(1)} %add_reduce_fusion), kind=kOutput, calls=%fused_computation.6 | convolution fusion | flops 7255621632 | bytes 14161920 | tf_op jit(solution)/shard_map/dot_general | solution.py:25
  452.3 3.1 fusion.65
  466.1 3.0 collective-permute-done.44.refs_1_
  (377 shorter events, 135.5 us)
Async XLA Ops:
  4.0 6.4 %collective-permute-start.1 = (f32[24,1280]{1,0:T(8,128)S(1)}, f32[24,1280]{1,0:T(8,128)S(1)}, u32[]{:S(2)}, u32[]{:S(2)}) collective-permute-start(f32[24,1280]{1,0:T(8,128)S(1)} %get-tuple-element.133), channel_id=1, source_target_pairs={{0,1},{1,0},{2,3},{3,2},{4,5},{5,4},{6,7},{7,6},{8,9},{9,8},{10,11... | collective-permute-start | bytes 368648 | tf_op jit(solution)/shard_map/ppermute | solution.py:441
  7.7 7.8 %collective-permute-start.7 = (f32[24,1536]{1,0:T(8,128)S(1)}, f32[24,1536]{1,0:T(8,128)S(1)}, u32[]{:S(2)}, u32[]{:S(2)}) collective-permute-start(f32[24,1536]{1,0:T(8,128)S(1)} %get-tuple-element.119), channel_id=1, source_target_pairs={{0,2},{1,3},{2,0},{3,1},{4,6},{5,7},{6,4},{7,5},{8,10},{9,11},{10,... | collective-permute-start | bytes 442376 | tf_op jit(solution)/shard_map/ppermute | solution.py:441
  9.6 65.5 %collective-permute-start = (f32[512,768]{1,0:T(8,128)}, f32[512,768]{1,0:T(8,128)}, u32[]{:S(2)}, u32[]{:S(2)}) collective-permute-start(f32[512,768]{1,0:T(8,128)} %subtract_multiply_fusion.1.refs_1_), channel_id=1, source_target_pairs={{0,1},{1,0},{2,3},{3,2},{4,5},{5,4},{6,7},{7,6},{8,9},{9,8},{10,11... | collective-permute-start | bytes 4718600 | tf_op jit(solution)/shard_map/ppermute | solution.py:441
  11.1 12.5 %collective-permute-start.2 = (f32[2,24,1280]{2,1,0:T(8,128)}, f32[2,24,1280]{2,1,0:T(8,128)S(1)}, u32[]{:S(2)}, u32[]{:S(2)}) collective-permute-start(f32[2,24,1280]{2,1,0:T(8,128)} %after.3), channel_id=1, source_target_pairs={{0,8},{1,9},{2,10},{3,11},{4,12},{5,13},{6,14},{7,15},{8,0},{9,1},... | collective-permute-start | bytes 737288 | tf_op jit(solution)/shard_map/ppermute | solution.py:441
  12.9 20.5 %collective-permute-start.3 = (f32[2,24,1280]{2,1,0:T(8,128)}, f32[2,24,1280]{2,1,0:T(8,128)S(1)}, u32[]{:S(2)}, u32[]{:S(2)}) collective-permute-start(f32[2,24,1280]{2,1,0:T(8,128)} %after.3), channel_id=1, source_target_pairs={{0,16},{1,17},{2,18},{3,19},{4,20},{5,21},{6,22},{7,23},{8,24},{9,... | collective-permute-start | bytes 737288 | tf_op jit(solution)/shard_map/ppermute | solution.py:441
  15.5 17.9 %collective-permute-start.4 = (f32[2,24,1280]{2,1,0:T(8,128)}, f32[2,24,1280]{2,1,0:T(8,128)S(1)}, u32[]{:S(2)}, u32[]{:S(2)}) collective-permute-start(f32[2,24,1280]{2,1,0:T(8,128)} %after.3), channel_id=1, source_target_pairs={{0,24},{1,25},{2,26},{3,27},{4,28},{5,29},{6,30},{7,31},{8,16},{9,... | collective-permute-start | bytes 737288 | tf_op jit(solution)/shard_map/ppermute | solution.py:441
  34.5 21.1 %collective-permute-start.8 = (f32[24,3840]{1,0:T(8,128)}, f32[24,3840]{1,0:T(8,128)S(1)}, u32[]{:S(2)}, u32[]{:S(2)}) collective-permute-start(f32[24,3840]{1,0:T(8,128)} %after.4.refs_0_), channel_id=1, source_target_pairs={{0,16},{1,17},{2,18},{3,19},{4,20},{5,21},{6,22},{7,23},{8,24},{9,... | collective-permute-start | bytes 1105928 | tf_op jit(solution)/shard_map/ppermute | solution.py:441
  39.9 22.4 %collective-permute-start.5 = (f32[4,2,24,1280]{3,2,1,0:T(8,128)}, f32[4,2,24,1280]{3,2,1,0:T(8,128)S(1)}, u32[]{:S(2)}, u32[]{:S(2)}) collective-permute-start(f32[4,2,24,1280]{3,2,1,0:T(8,128)} %pad_maximum_fusion.4.refs_1_.refs_0_), channel_id=1, source_target_pairs={{0,4},{1,5},{2,6},{3,7},{4,0},{5,1},{6,2},{7,3},{8,12},{9,13},{10,... | collective-permute-start | bytes 2949128 | tf_op jit(solution)/shard_map/ppermute | solution.py:441
  57.2 17.3 %collective-permute-start.9 = (f32[2,24,3840]{2,1,0:T(8,128)S(1)}, f32[2,24,3840]{2,1,0:T(8,128)S(1)}, u32[]{:S(2)}, u32[]{:S(2)}) collective-permute-start(f32[2,24,3840]{2,1,0:T(8,128)S(1)} %pair.2.refs_0_.refs_1_), channel_id=1, source_target_pairs={{0,8},{1,9},{2,10},{3,11},{4,12},{5,13},{6,14},{7,15},{8,0},{9,1},... | collective-permute-start | bytes 2211848 | tf_op jit(solution)/shard_map/ppermute | solution.py:441
  57.2 22.6 %collective-permute-start.6 = (f32[4,2,24,1280]{3,2,1,0:T(8,128)}, f32[4,2,24,1280]{3,2,1,0:T(8,128)}, u32[]{:S(2)}, u32[]{:S(2)}) collective-permute-start(f32[4,2,24,1280]{3,2,1,0:T(8,128)} %pad_maximum_fusion.4.refs_1_.refs_0_), channel_id=1, source_target_pairs={{0,2},{1,3},{2,0},{3,1},{4,6},{5,7},{6,4},{7,5},{8,10},{9,11},{10,... | collective-permute-start | bytes 2949128 | tf_op jit(solution)/shard_map/ppermute | solution.py:441
  76.7 3.1 collective-permute-start.10
  76.7 16.6 %collective-permute-start.11 = (f32[96,768]{1,0:T(8,128)}, f32[96,768]{1,0:T(8,128)S(1)}, u32[]{:S(2)}, u32[]{:S(2)}) collective-permute-start(f32[96,768]{1,0:T(8,128)} %after.5.refs_0_), channel_id=1, source_target_pairs={{0,16},{1,17},{2,18},{3,19},{4,20},{5,21},{6,22},{7,23},{8,24},{9,... | collective-permute-start | bytes 884744 | tf_op jit(solution)/shard_map/ppermute | solution.py:441
  76.8 60.8 %collective-permute-start.15 = (f32[4,24,3840]{2,1,0:T(8,128)S(1)}, f32[4,24,3840]{2,1,0:T(8,128)S(1)}, u32[]{:S(2)}, u32[]{:S(2)}) collective-permute-start(f32[4,24,3840]{2,1,0:T(8,128)S(1)} %pairs.2.refs_2_.refs_0_), channel_id=1, source_target_pairs={{0,1},{1,0},{2,3},{3,2},{4,5},{5,4},{6,7},{7,6},{8,9},{9,8},{10,11... | collective-permute-start | bytes 4423688 | tf_op jit(solution)/shard_map/ppermute | solution.py:441
  78.3 63.9 %collective-permute-start.14 = (f32[4,24,3840]{2,1,0:T(8,128)S(1)}, f32[4,24,3840]{2,1,0:T(8,128)}, u32[]{:S(2)}, u32[]{:S(2)}) collective-permute-start(f32[4,24,3840]{2,1,0:T(8,128)S(1)} %pairs.2.refs_2_.refs_0_), channel_id=1, source_target_pairs={{0,4},{1,5},{2,6},{3,7},{4,0},{5,1},{6,2},{7,3},{8,12},{9,13},{10,... | collective-permute-start | bytes 4423688 | tf_op jit(solution)/shard_map/ppermute | solution.py:441
  96.7 15.5 %collective-permute-start.12 = (f32[2,96,768]{2,1,0:T(8,128)}, f32[2,96,768]{2,1,0:T(8,128)S(1)}, u32[]{:S(2)}, u32[]{:S(2)}) collective-permute-start(f32[2,96,768]{2,1,0:T(8,128)} %pair.3.refs_0_), channel_id=1, source_target_pairs={{0,8},{1,9},{2,10},{3,11},{4,12},{5,13},{6,14},{7,15},{8,0},{9,1},... | collective-permute-start | bytes 1769480 | tf_op jit(solution)/shard_map/ppermute | solution.py:441
  114.4 46.0 %collective-permute-start.17 = (f32[4,96,768]{2,1,0:T(8,128)}, f32[4,96,768]{2,1,0:T(8,128)}, u32[]{:S(2)}, u32[]{:S(2)}) collective-permute-start(f32[4,96,768]{2,1,0:T(8,128)} %pairs.3.refs_0_), channel_id=1, source_target_pairs={{0,4},{1,5},{2,6},{3,7},{4,0},{5,1},{6,2},{7,3},{8,12},{9,13},{10,... | collective-permute-start | bytes 3538952 | tf_op jit(solution)/shard_map/ppermute | solution.py:441
  115.9 44.5 %collective-permute-start.18 = (f32[4,96,768]{2,1,0:T(8,128)}, f32[4,96,768]{2,1,0:T(8,128)}, u32[]{:S(2)}, u32[]{:S(2)}) collective-permute-start(f32[4,96,768]{2,1,0:T(8,128)} %pairs.3.refs_0_), channel_id=1, source_target_pairs={{0,1},{1,0},{2,3},{3,2},{4,5},{5,4},{6,7},{7,6},{8,9},{9,8},{10,11... | collective-permute-start | bytes 3538952 | tf_op jit(solution)/shard_map/ppermute | solution.py:441
  137.0 23.4 %collective-permute-start.13 = (f32[512,384]{1,0:T(8,128)}, f32[512,384]{1,0:T(8,128)}, u32[]{:S(2)}, u32[]{:S(2)}) collective-permute-start(f32[512,384]{1,0:T(8,128)} %get-tuple-element.113), channel_id=1, source_target_pairs={{0,1},{1,0},{2,3},{3,2},{4,5},{5,4},{6,7},{7,6},{8,9},{9,8},{10,11... | collective-permute-start | bytes 2359304 | tf_op jit(solution)/shard_map/ppermute | solution.py:441
  139.2 26.9 %collective-permute-start.16 = (f32[3,24,3840]{2,1,0:T(8,128)}, f32[3,24,3840]{2,1,0:T(8,128)}, u32[]{:S(2)}, u32[]{:S(2)}) collective-permute-start(f32[3,24,3840]{2,1,0:T(8,128)} %corner_first.1), channel_id=1, source_target_pairs={{0,4},{1,5},{2,6},{3,7},{4,0},{5,1},{6,2},{7,3},{8,12},{9,13},{10,... | collective-permute-start | bytes 3317768 | tf_op jit(solution)/shard_map/ppermute | solution.py:441
  164.2 9.1 %collective-permute-start.19 = (f32[1,24,3840]{2,1,0:T(8,128)S(1)}, f32[1,24,3840]{2,1,0:T(8,128)S(1)}, u32[]{:S(2)}, u32[]{:S(2)}) collective-permute-start(f32[1,24,3840]{2,1,0:T(8,128)S(1)} %get-tuple-element.58), channel_id=1, source_target_pairs={{0,1},{1,0},{2,3},{3,2},{4,5},{5,4},{6,7},{7,6},{8,9},{9,8},{10,11... | collective-permute-start | bytes 1105928 | tf_op jit(solution)/shard_map/ppermute | solution.py:441
  176.2 3.3 collective-permute-start.20
  176.2 17.5 %collective-permute-start.22 = (f32[512,768]{1,0:T(8,128)}, f32[512,768]{1,0:T(8,128)}, u32[]{:S(2)}, u32[]{:S(2)}) collective-permute-start(f32[512,768]{1,0:T(8,128)} %param.16), channel_id=1, source_target_pairs={{0,2},{1,3},{2,0},{3,1},{4,6},{5,7},{6,4},{7,5},{8,10},{9,11},{10,... | collective-permute-start | bytes 4718600 | tf_op jit(solution)/shard_map/ppermute | solution.py:441
  190.3 25.3 %collective-permute-start.21 = (f32[512,768]{1,0:T(8,128)}, f32[512,768]{1,0:T(8,128)}, u32[]{:S(2)}, u32[]{:S(2)}) collective-permute-start(f32[512,768]{1,0:T(8,128)} %multiply_add_fusion.2), channel_id=1, source_target_pairs={{0,2},{1,3},{2,0},{3,1},{4,6},{5,7},{6,4},{7,5},{8,10},{9,11},{10,... | collective-permute-start | bytes 4718600 | tf_op jit(solution)/shard_map/ppermute | solution.py:441
  190.4 22.2 %collective-permute-start.23 = (f32[3,96,768]{2,1,0:T(8,128)}, f32[3,96,768]{2,1,0:T(8,128)}, u32[]{:S(2)}, u32[]{:S(2)}) collective-permute-start(f32[3,96,768]{2,1,0:T(8,128)} %get-tuple-element.61), channel_id=1, source_target_pairs={{0,4},{1,5},{2,6},{3,7},{4,0},{5,1},{6,2},{7,3},{8,12},{9,13},{10,... | collective-permute-start | bytes 2654216 | tf_op jit(solution)/shard_map/ppermute | solution.py:441
  197.5 9.2 %collective-permute-start.24 = (f32[1,96,768]{2,1,0:T(8,128)}, f32[1,96,768]{2,1,0:T(8,128)S(1)}, u32[]{:S(2)}, u32[]{:S(2)}) collective-permute-start(f32[1,96,768]{2,1,0:T(8,128)} %copy-done.47), channel_id=1, source_target_pairs={{0,1},{1,0},{2,3},{3,2},{4,5},{5,4},{6,7},{7,6},{8,9},{9,8},{10,11... | collective-permute-start | bytes 884744 | tf_op jit(solution)/shard_map/ppermute | solution.py:441
  249.0 17.8 %collective-permute-start.25 = (f32[512,768]{1,0:T(8,128)}, f32[512,768]{1,0:T(8,128)}, u32[]{:S(2)}, u32[]{:S(2)}) collective-permute-start(f32[512,768]{1,0:T(8,128)} %slice.110), channel_id=1, source_target_pairs={{0,2},{1,3},{2,0},{3,1},{4,6},{5,7},{6,4},{7,5},{8,10},{9,11},{10,... | collective-permute-start | bytes 4718600 | tf_op jit(solution)/shard_map/ppermute | solution.py:441
  264.1 47.1 %collective-permute-start.27 = (f32[2,2,96,768]{3,2,1,0:T(8,128)}, f32[2,2,96,768]{3,2,1,0:T(8,128)}, u32[]{:S(2)}, u32[]{:S(2)}) collective-permute-start(f32[2,2,96,768]{3,2,1,0:T(8,128)} %get-tuple-element.63), channel_id=1, source_target_pairs={{0,4},{1,5},{2,6},{3,7},{4,0},{5,1},{6,2},{7,3},{8,12},{9,13},{10,... | collective-permute-start | bytes 3538952 | tf_op jit(solution)/shard_map/ppermute | solution.py:441
  264.6 46.5 %collective-permute-start.28 = (f32[2,2,96,768]{3,2,1,0:T(8,128)}, f32[2,2,96,768]{3,2,1,0:T(8,128)}, u32[]{:S(2)}, u32[]{:S(2)}) collective-permute-start(f32[2,2,96,768]{3,2,1,0:T(8,128)} %get-tuple-element.64), channel_id=1, source_target_pairs={{0,1},{1,0},{2,3},{3,2},{4,5},{5,4},{6,7},{7,6},{8,9},{9,8},{10,11... | collective-permute-start | bytes 3538952 | tf_op jit(solution)/shard_map/ppermute | solution.py:441
  277.7 37.8 %collective-permute-start.26 = (f32[4,2,2,24,768]{4,3,2,1,0:T(8,128)}, f32[4,2,2,24,768]{4,3,2,1,0:T(8,128)S(1)}, u32[]{:S(2)}, u32[]{:S(2)}) collective-permute-start(f32[4,2,2,24,768]{4,3,2,1,0:T(8,128)} %dynamic-slice_bitcast_fusion), channel_id=1, source_target_pairs={{0,2},{1,3},{2,0},{3,1},{4,6},{5,7},{6,4},{7,5},{8,10},{9,11},{10,... | collective-permute-start | bytes 3538952 | tf_op jit(solution)/shard_map/ppermute | solution.py:441
  288.1 21.8 %collective-permute-start.29 = (f32[512,384]{1,0:T(8,128)}, f32[512,384]{1,0:T(8,128)}, u32[]{:S(2)}, u32[]{:S(2)}) collective-permute-start(f32[512,384]{1,0:T(8,128)} %get-tuple-element.109.refs_0_), channel_id=1, source_target_pairs={{0,1},{1,0},{2,3},{3,2},{4,5},{5,4},{6,7},{7,6},{8,9},{9,8},{10,11... | collective-permute-start | bytes 2359304 | tf_op jit(solution)/shard_map/ppermute | solution.py:441
  316.3 49.9 %collective-permute-start.30 = (f32[2,2,24,3840]{3,2,1,0:T(8,128)S(1)}, f32[2,2,24,3840]{3,2,1,0:T(8,128)S(1)}, u32[]{:S(2)}, u32[]{:S(2)}) collective-permute-start(f32[2,2,24,3840]{3,2,1,0:T(8,128)S(1)} %get-tuple-element.67.refs_0_), channel_id=1, source_target_pairs={{0,4},{1,5},{2,6},{3,7},{4,0},{5,1},{6,2},{7,3},{8,12},{9,13},{10,... | collective-permute-start | bytes 4423688 | tf_op jit(solution)/shard_map/ppermute | solution.py:441
  317.9 48.4 %collective-permute-start.31 = (f32[2,2,24,3840]{3,2,1,0:T(8,128)S(1)}, f32[2,2,24,3840]{3,2,1,0:T(8,128)S(1)}, u32[]{:S(2)}, u32[]{:S(2)}) collective-permute-start(f32[2,2,24,3840]{3,2,1,0:T(8,128)S(1)} %get-tuple-element.68.refs_1_), channel_id=1, source_target_pairs={{0,1},{1,0},{2,3},{3,2},{4,5},{5,4},{6,7},{7,6},{8,9},{9,8},{10,11... | collective-permute-start | bytes 4423688 | tf_op jit(solution)/shard_map/ppermute | solution.py:441
  319.4 44.4 %collective-permute-start.32 = (f32[2,96,768]{2,1,0:T(8,128)S(1)}, f32[2,96,768]{2,1,0:T(8,128)S(1)}, u32[]{:S(2)}, u32[]{:S(2)}) collective-permute-start(f32[2,96,768]{2,1,0:T(8,128)S(1)} %get-tuple-element.65.refs_3_.refs_2_), channel_id=1, source_target_pairs={{0,1},{1,0},{2,3},{3,2},{4,5},{5,4},{6,7},{7,6},{8,9},{9,8},{10,11... | collective-permute-start | bytes 1769480 | tf_op jit(solution)/shard_map/ppermute | solution.py:441
  319.9 43.9 %collective-permute-start.33 = (f32[2,96,768]{2,1,0:T(8,128)S(1)}, f32[2,96,768]{2,1,0:T(8,128)S(1)}, u32[]{:S(2)}, u32[]{:S(2)}) collective-permute-start(f32[2,96,768]{2,1,0:T(8,128)S(1)} %get-tuple-element.66.refs_4_.refs_3_), channel_id=1, source_target_pairs={{0,4},{1,5},{2,6},{3,7},{4,0},{5,1},{6,2},{7,3},{8,12},{9,13},{10,... | collective-permute-start | bytes 1769480 | tf_op jit(solution)/shard_map/ppermute | solution.py:441
  369.4 17.7 %collective-permute-start.34 = (f32[2,24,3840]{2,1,0:T(8,128)}, f32[2,24,3840]{2,1,0:T(8,128)}, u32[]{:S(2)}, u32[]{:S(2)}) collective-permute-start(f32[2,24,3840]{2,1,0:T(8,128)} %get-tuple-element.74.refs_0_), channel_id=1, source_target_pairs={{0,1},{1,0},{2,3},{3,2},{4,5},{5,4},{6,7},{7,6},{8,9},{9,8},{10,11... | collective-permute-start | bytes 2211848 | tf_op jit(solution)/shard_map/ppermute | solution.py:441
  370.9 16.6 %collective-permute-start.35 = (f32[2,24,3840]{2,1,0:T(8,128)}, f32[2,24,3840]{2,1,0:T(8,128)}, u32[]{:S(2)}, u32[]{:S(2)}) collective-permute-start(f32[2,24,3840]{2,1,0:T(8,128)} %get-tuple-element.75.refs_1_), channel_id=1, source_target_pairs={{0,4},{1,5},{2,6},{3,7},{4,0},{5,1},{6,2},{7,3},{8,12},{9,13},{10,... | collective-permute-start | bytes 2211848 | tf_op jit(solution)/shard_map/ppermute | solution.py:441
  371.5 13.1 %collective-permute-start.36 = (f32[2,96,768]{2,1,0:T(8,128)}, f32[2,96,768]{2,1,0:T(8,128)S(1)}, u32[]{:S(2)}, u32[]{:S(2)}) collective-permute-start(f32[2,96,768]{2,1,0:T(8,128)} %get-tuple-element.72.refs_5_), channel_id=1, source_target_pairs={{0,8},{1,9},{2,10},{3,11},{4,12},{5,13},{6,14},{7,15},{8,0},{9,1},... | collective-permute-start | bytes 1769480 | tf_op jit(solution)/shard_map/ppermute | solution.py:441
  392.3 4.0 collective-permute-start.38
  399.0 24.1 %collective-permute-start.39 = (f32[4,2,24,1280]{3,2,1,0:T(8,128)}, f32[4,2,24,1280]{3,2,1,0:T(8,128)}, u32[]{:S(2)}, u32[]{:S(2)}) collective-permute-start(f32[4,2,24,1280]{3,2,1,0:T(8,128)} %get-tuple-element.84.refs_0_), channel_id=1, source_target_pairs={{0,4},{1,5},{2,6},{3,7},{4,0},{5,1},{6,2},{7,3},{8,12},{9,13},{10,... | collective-permute-start | bytes 2949128 | tf_op jit(solution)/shard_map/ppermute | solution.py:441
  401.9 47.7 %collective-permute-start.47 = (f32[96,768]{1,0:T(8,128)}, f32[96,768]{1,0:T(8,128)}, u32[]{:S(2)}, u32[]{:S(2)}) collective-permute-start(f32[96,768]{1,0:T(8,128)} %copy-done.40), channel_id=1, source_target_pairs={{0,16},{1,17},{2,18},{3,19},{4,20},{5,21},{6,22},{7,23},{8,24},{9,... | collective-permute-start | bytes 884744 | tf_op jit(solution)/shard_map/ppermute | solution.py:441
  402.0 25.2 %collective-permute-start.37 = (f32[2,24,3840]{2,1,0:T(8,128)}, f32[2,24,3840]{2,1,0:T(8,128)}, u32[]{:S(2)}, u32[]{:S(2)}) collective-permute-start(f32[2,24,3840]{2,1,0:T(8,128)} %copy-done.33), channel_id=1, source_target_pairs={{0,8},{1,9},{2,10},{3,11},{4,12},{5,13},{6,14},{7,15},{8,0},{9,1},... | collective-permute-start | bytes 2211848 | tf_op jit(solution)/shard_map/ppermute | solution.py:441
  413.5 38.8 %collective-permute-start.41 = (f32[512,768]{1,0:T(8,128)}, f32[512,768]{1,0:T(8,128)}, u32[]{:S(2)}, u32[]{:S(2)}) collective-permute-start(f32[512,768]{1,0:T(8,128)} %constant_dynamic-slice_fusion.1), channel_id=1, source_target_pairs={{0,1},{1,0},{2,3},{3,2},{4,5},{5,4},{6,7},{7,6},{8,9},{9,8},{10,11... | collective-permute-start | bytes 4718600 | tf_op jit(solution)/shard_map/ppermute | solution.py:441
  424.5 20.5 %collective-permute-start.42 = (f32[2,2,24,1280]{3,2,1,0:T(8,128)S(1)}, f32[2,2,24,1280]{3,2,1,0:T(8,128)S(1)}, u32[]{:S(2)}, u32[]{:S(2)}) collective-permute-start(f32[2,2,24,1280]{3,2,1,0:T(8,128)S(1)} %get-tuple-element.85.refs_2_), channel_id=1, source_target_pairs={{0,8},{1,9},{2,10},{3,11},{4,12},{5,13},{6,14},{7,15},{8,0},{9,1},... | collective-permute-start | bytes 1474568 | tf_op jit(solution)/shard_map/ppermute | solution.py:441
  429.0 18.2 %collective-permute-start.45 = (f32[24,3840]{1,0:T(8,128)S(1)}, f32[24,3840]{1,0:T(8,128)S(1)}, u32[]{:S(2)}, u32[]{:S(2)}) collective-permute-start(f32[24,3840]{1,0:T(8,128)S(1)} %get-tuple-element.86.refs_0_), channel_id=1, source_target_pairs={{0,16},{1,17},{2,18},{3,19},{4,20},{5,21},{6,22},{7,23},{8,24},{9,... | collective-permute-start | bytes 1105928 | tf_op jit(solution)/shard_map/ppermute | solution.py:441
  445.0 18.9 %collective-permute-start.40 = (f32[512,768]{1,0:T(8,128)}, f32[512,768]{1,0:T(8,128)}, u32[]{:S(2)}, u32[]{:S(2)}) collective-permute-start(f32[512,768]{1,0:T(8,128)} %slice.112), channel_id=1, source_target_pairs={{0,2},{1,3},{2,0},{3,1},{4,6},{5,7},{6,4},{7,5},{8,10},{9,11},{10,... | collective-permute-start | bytes 4718600 | tf_op jit(solution)/shard_map/ppermute | solution.py:441
  446.3 15.0 %collective-permute-start.43 = (f32[2,24,1280]{2,1,0:T(8,128)}, f32[2,24,1280]{2,1,0:T(8,128)}, u32[]{:S(2)}, u32[]{:S(2)}) collective-permute-start(f32[2,24,1280]{2,1,0:T(8,128)} %get-tuple-element.89.refs_2_), channel_id=1, source_target_pairs={{0,16},{1,17},{2,18},{3,19},{4,20},{5,21},{6,22},{7,23},{8,24},{9,... | collective-permute-start | bytes 737288 | tf_op jit(solution)/shard_map/ppermute | solution.py:441
  449.2 7.9 %collective-permute-start.46 = (f32[24,1536]{1,0:T(8,128)}, f32[24,1536]{1,0:T(8,128)}, u32[]{:S(2)}, u32[]{:S(2)}) collective-permute-start(f32[24,1536]{1,0:T(8,128)} %get-tuple-element.117), channel_id=1, source_target_pairs={{0,2},{1,3},{2,0},{3,1},{4,6},{5,7},{6,4},{7,5},{8,10},{9,11},{10,... | collective-permute-start | bytes 442376 | tf_op jit(solution)/shard_map/ppermute | solution.py:441
  463.4 5.8 %collective-permute-start.44 = (f32[24,1280]{1,0:T(8,128)S(1)}, f32[24,1280]{1,0:T(8,128)S(1)}, u32[]{:S(2)}, u32[]{:S(2)}) collective-permute-start(f32[24,1280]{1,0:T(8,128)S(1)} %get-tuple-element.91), channel_id=1, source_target_pairs={{0,1},{1,0},{2,3},{3,2},{4,5},{5,4},{6,7},{7,6},{8,9},{9,8},{10,11... | collective-permute-start | bytes 368648 | tf_op jit(solution)/shard_map/ppermute | solution.py:441
  (91 other events, 493.2 us)
